TPU v7x, 128 devices: a whole 4x4x4 slice. The times are simulated.
128 devices in a mesh: row: 8 (over y, core), col: 16 (over z, x).
Axes of the slice: x: 4, y: 4, z: 4, core: 2. Of those that a mesh axis runs over, the one named last changes fastest.
Arguments:
- src_emb: bfloat16 [32768, 128], P('row'), may hold values from -160 to 160
- tgt_emb: bfloat16 [16384, 128], P('col'), may hold values from -20 to 20
- cost_factor: bfloat16 [128, 128], replicated, may hold values from -1 to 1
- col_start: float32 [16384], P('col'), may hold values from -8 to 8
Outputs:
- bary_src: bfloat16 [32768, 128], P(('row', 'col'))
- bary_tgt: bfloat16 [16384, 128], P('col')
- cross_moment: float32 [128, 128], replicated
- row_potential: float32 [32768], P('row')
- col_potential: float32 [16384], P('col')
All inputs are finite; a program needn't handle non-finite values.
Results may differ from a plain program's by a relative error of at most 0.011.
Values sent between devices are 32-bit elements; how exact they have to be, the bound alone decides.
No kernel may reach another device: no remote copies, remote signals or barrier semaphores. Data moves between devices by JAX's collectives and lax.ppermute only.
A program may use at most 64 MiB of HBM per device.

v0:
```python
import math

import jax
import jax.numpy as jnp
from jax import lax
from jax.sharding import PartitionSpec as P

SWEEPS = 2


def row_reduce(largest, totals):
    global_max = lax.pmax(largest, "col")
    global_sum = lax.psum(totals * jnp.exp(largest - global_max), "col")
    return global_max + jnp.log(global_sum)


def col_reduce(largest, totals):
    global_max = lax.pmax(largest, "row")
    global_sum = lax.psum(totals * jnp.exp(largest - global_max), "row")
    return global_max + jnp.log(global_sum)


def local(src_emb, tgt_emb, cost_factor, col_start):
    src_rows = src_emb.shape[0]
    tgt_rows = tgt_emb.shape[0]
    width = src_emb.shape[1]
    src_count = src_rows * lax.axis_size("row")
    tgt_count = tgt_rows * lax.axis_size("col")
    log_src = -math.log(src_count)
    log_tgt = -math.log(tgt_count)
    projected = jnp.dot(src_emb, cost_factor, preferred_element_type=jnp.float32).astype(
        jnp.bfloat16
    )
    block_rows = math.gcd(src_rows, 512)
    block_count = src_rows // block_rows
    proj_blocks = projected.reshape(block_count, block_rows, width)
    src_blocks = src_emb.reshape(block_count, block_rows, width)

    def score_tile(proj_block):
        return lax.dot_general(
            proj_block, tgt_emb, (((1,), (1,)), ((), ())), preferred_element_type=jnp.float32
        )

    def row_parts(potential):

        def row_block_step(proj_block):
            logits = score_tile(proj_block) + potential[None, :]
            largest = jnp.max(logits, axis=1)
            return (largest, jnp.sum(jnp.exp(logits - largest[:, None]), axis=1))

        largest, totals = lax.map(row_block_step, proj_blocks)
        return (largest.reshape(src_rows), totals.reshape(src_rows))

    def col_parts(potential):

        def col_block_step(running, inputs):
            largest, totals = running
            proj_block, row_part = inputs
            logits = score_tile(proj_block) + row_part[:, None]
            new_largest = jnp.maximum(largest, jnp.max(logits, axis=0))
            totals = totals * jnp.exp(largest - new_largest) + jnp.sum(
                jnp.exp(logits - new_largest[None, :]), axis=0
            )
            return ((new_largest, totals), None)

        initial = (jnp.full((tgt_rows,), -1e30, jnp.float32), jnp.zeros((tgt_rows,), jnp.float32))
        (largest, totals), unused = lax.scan(
            col_block_step, initial, (proj_blocks, potential.reshape(block_count, block_rows))
        )
        return (largest, totals)

    col_potential = col_start
    for sweep_index in range(SWEEPS):
        largest, totals = row_parts(col_potential)
        row_potential = log_src - row_reduce(largest, totals)
        largest, totals = col_parts(row_potential)
        col_potential = log_tgt - col_reduce(largest, totals)

    def final_step(running, inputs):
        proj_block, src_block, row_part = inputs
        logits = score_tile(proj_block) + row_part[:, None] + col_potential[None, :]
        coupling = jnp.exp(logits).astype(jnp.bfloat16)
        target_part = jnp.dot(coupling, tgt_emb, preferred_element_type=jnp.float32)
        running = running + lax.dot_general(
            coupling, src_block, (((0,), (0,)), ((), ())), preferred_element_type=jnp.float32
        )
        return (running, target_part)

    source_mix, mix_blocks = lax.scan(
        final_step,
        jnp.zeros((tgt_rows, width), jnp.float32),
        (proj_blocks, src_blocks, row_potential.reshape(block_count, block_rows)),
    )
    target_mix = mix_blocks.reshape(src_rows, width)
    share = src_rows // lax.axis_size("col")
    target_full = lax.psum(target_mix, "col")
    moment_part = jnp.dot(
        src_emb.astype(jnp.float32).T,
        target_full,
        precision=lax.Precision.HIGHEST,
        preferred_element_type=jnp.float32,
    )
    source_sum, cross_moment = lax.psum((source_mix, moment_part), "row")
    owned = lax.dynamic_slice_in_dim(target_full, lax.axis_index("col") * share, share, 0)
    bary_src = (src_count * owned).astype(jnp.bfloat16)
    bary_tgt = (tgt_count * source_sum).astype(jnp.bfloat16)
    return (bary_src, bary_tgt, cross_moment, row_potential, col_potential)


def solution(mesh):
    placed = (P("row", None), P("col", None), P(), P("col"))
    return jax.shard_map(
        local,
        mesh=mesh,
        in_specs=placed,
        out_specs=(P(("row", "col"), None), P("col", None), P(), P("row"), P("col")),
        check_vma=False,
    )
```

profile of v0, /device:TPU:0, one launch (start us, length us, event | category | flops | bytes accessed | tf_op | source)
XLA Modules:
  0.0 600.7 jit_solution(6877661758735622198)
XLA Ops:
  7.9 2.6 convolution_convert_fusion
  10.6 16.9 %while.63 = (s32[]{:T(128)}, f32[8,512]{1,0:T(8,128)S(1)}, f32[8,512]{1,0:T(8,128)S(1)}, bf16[8,512,128]{2,1,0:T(8,128)(2,1)}, bf16[1024,128]{1,0:T(8,128)(2,1)S...) while((s32[]{:T(128)}, f32[8,512]{1,0:T(8,128)S(1)}, f32[8,512]{1,0:T(8,128)S(1)}, ...), condition=%wide.region_3.4_spmd, body=%wide.region_0.3_spmd.sunk | while | flops 136838144 | bytes 4610653 | solution.py:51
  10.6 1.4 add_reduce_fusion.8
  12.7 1.4 add_reduce_fusion.8
  14.8 1.4 add_reduce_fusion.8
  23.3 1.4 add_reduce_fusion.8
  27.5 75.7 %pmax.28 = f32[4096]{0:T(1024)S(1)} all-reduce(f32[4096]{0:T(1024)S(1)} %bitcast.117), channel_id=1, replica_groups=mesh['row'=8,'col'=16] {'col'}, use_global_device_ids=true, to_apply=%region_4.5 | all-reduce | flops 4096 | bytes 32768 | tf_op jit(solution)/shard_map/pmax | solution.py:12
  103.2 69.5 %psum.49 = f32[4096]{0:T(1024)S(1)} all-reduce(f32[4096]{0:T(1024)S(1)} %exponential_multiply_fusion.1), channel_id=1, replica_groups=mesh['row'=8,'col'=16] {'col'}, use_global_device_ids=true, to_apply=%region_5.6 | all-reduce | flops 4096 | bytes 32768 | tf_op jit(solution)/shard_map/psum | solution.py:13
  172.8 15.0 %while.65 = (s32[]{:T(128)}, f32[1024]{0:T(1024)S(1)}, f32[1024]{0:T(1024)S(1)}, bf16[8,512,128]{2,1,0:T(8,128)(2,1)}, bf16[1024,128]{1,0:T(8,128)(2,1)S(1)}, /*index=5*/f32[8,512]{1,0:T(8,128)S(1)}, s32[]{:T(128)}, s32[]{:T(128)}) while((s32[]{:T(128)}, f32[1024]{0:T(1024)S(1)}, f32[1024]{0:T(1024)S(1)}, ...), condition=%wide.region_9.10_spmd.clone, body=%wide.region_6.9_spmd.clone.sunk | while | flops 136844288 | bytes 4649572 | solution.py:67
  187.8 12.4 %pmax.29 = f32[1024]{0:T(1024)S(1)} all-reduce(f32[1024]{0:T(1024)S(1)} %get-tuple-element.182), channel_id=1, replica_groups=mesh['row'=8,'col'=16] {'row'}, use_global_device_ids=true, to_apply=%region_10.11 | all-reduce | flops 1024 | bytes 8192 | tf_op jit(solution)/shard_map/pmax | solution.py:18
  200.2 12.5 %psum.50 = f32[1024]{0:T(1024)S(1)} all-reduce(f32[1024]{0:T(1024)S(1)} %exponential_multiply_fusion.3), channel_id=1, replica_groups=mesh['row'=8,'col'=16] {'row'}, use_global_device_ids=true, to_apply=%region_11.12 | all-reduce | flops 1024 | bytes 8192 | tf_op jit(solution)/shard_map/psum | solution.py:19
  212.7 16.9 %while.64 = (s32[]{:T(128)}, f32[8,512]{1,0:T(8,128)S(1)}, f32[8,512]{1,0:T(8,128)S(1)}, bf16[8,512,128]{2,1,0:T(8,128)(2,1)}, bf16[1024,128]{1,0:T(8,128)(2,1)S...) while((s32[]{:T(128)}, f32[8,512]{1,0:T(8,128)S(1)}, f32[8,512]{1,0:T(8,128)S(1)}, ...), condition=%wide.region_15.16_spmd, body=%wide.region_12.15_spmd.sunk | while | flops 136838144 | bytes 4610653 | solution.py:51
  229.6 69.5 %pmax.30 = f32[4096]{0:T(1024)S(1)} all-reduce(f32[4096]{0:T(1024)S(1)} %bitcast.119), channel_id=1, replica_groups=mesh['row'=8,'col'=16] {'col'}, use_global_device_ids=true, to_apply=%region_16.17 | all-reduce | flops 4096 | bytes 32768 | tf_op jit(solution)/shard_map/pmax | solution.py:12
  299.2 69.5 %psum.51 = f32[4096]{0:T(1024)S(1)} all-reduce(f32[4096]{0:T(1024)S(1)} %exponential_multiply_fusion), channel_id=1, replica_groups=mesh['row'=8,'col'=16] {'col'}, use_global_device_ids=true, to_apply=%region_17.18 | all-reduce | flops 4096 | bytes 32768 | tf_op jit(solution)/shard_map/psum | solution.py:13
  369.3 15.0 %while.66 = (s32[]{:T(128)}, f32[1024]{0:T(1024)S(1)}, f32[1024]{0:T(1024)S(1)}, bf16[8,512,128]{2,1,0:T(8,128)(2,1)}, bf16[1024,128]{1,0:T(8,128)(2,1)S(1)}, /*index=5*/f32[8,512]{1,0:T(8,128)S(1)}, s32[]{:T(128)}, s32[]{:T(128)}) while((s32[]{:T(128)}, f32[1024]{0:T(1024)S(1)}, f32[1024]{0:T(1024)S(1)}, ...), condition=%wide.region_21.22_spmd.clone, body=%wide.region_18.21_spmd.clone.sunk | while | flops 136844288 | bytes 4649572 | solution.py:67
  384.3 12.4 %pmax.31 = f32[1024]{0:T(1024)S(1)} all-reduce(f32[1024]{0:T(1024)S(1)} %get-tuple-element.186), channel_id=1, replica_groups=mesh['row'=8,'col'=16] {'row'}, use_global_device_ids=true, to_apply=%region_22.23 | all-reduce | flops 1024 | bytes 8192 | tf_op jit(solution)/shard_map/pmax | solution.py:18
  396.7 12.4 %psum.52 = f32[1024]{0:T(1024)S(1)} all-reduce(f32[1024]{0:T(1024)S(1)} %exponential_multiply_fusion.2), channel_id=1, replica_groups=mesh['row'=8,'col'=16] {'row'}, use_global_device_ids=true, to_apply=%region_23.24 | all-reduce | flops 1024 | bytes 8192 | tf_op jit(solution)/shard_map/psum | solution.py:19
  409.2 32.8 %while.67 = (s32[]{:T(128)}, f32[1024,128]{1,0:T(8,128)S(1)}, f32[8,512,128]{2,1,0:T(8,128)}, bf16[8,512,128]{2,1,0:T(8,128)(2,1)}, bf16[1024,128]{1,0:T(8,128)(...) while((s32[]{:T(128)}, f32[1024,128]{1,0:T(8,128)S(1)}, ...), condition=%wide.region_25.26_spmd.clone, body=%wide.region_24.25_spmd.clone.sunk | while | flops 404488192 | bytes 5254771 | solution.py:89
  411.7 1.5 convolution_add_fusion.2
  415.8 1.5 convolution_add_fusion.2
  419.9 1.5 convolution_add_fusion.2
  424.0 1.5 convolution_add_fusion.2
  428.1 1.5 convolution_add_fusion.2
  432.2 1.5 convolution_add_fusion.2
  436.3 1.5 convolution_add_fusion.2
  440.4 1.5 convolution_add_fusion.2
  442.1 83.7 %all-reduce.4.cloned.1.call-done = f32[4096,128]{1,0:T(8,128)} async-done(((f32[4096,128]{1,0:T(8,128)}), f32[4096,128]{1,0:T(8,128)}) %all-reduce.4.cloned.1.call-update) | async-done | bytes 2097168 | tf_op jit(solution)/shard_map/psum | solution.py:96
  525.8 4.0 convolution_bitcast_fusion.1
  529.9 1.5 multiply_convert_fusion.1
  531.4 59.1 %all-reduce.6.cloned.1.call-done = (f32[1024,128]{1,0:T(8,128)}, f32[128,128]{0,1:T(8,128)}) async-done(((f32[1024,128]{1,0:T(8,128)}, f32[128,128]{0,1:T(8,128)}), (f32[1024,128]{1,0:T(8,128)}, f32[128,128]{0,1:T(8,128)})) %all-reduce.6.cloned.1.call-update) | async-done | bytes 589840 | tf_op jit(solution)/shard_map/psum | solution.py:103
  590.6 1.8 multiply_convert_fusion
  592.3 1.6 copy.9
  (222 shorter events, 78.5 us)
Async XLA Ops:
  7.2 0.8 copy-start
  7.2 3.4 copy-start.1
  7.2 3.4 copy-start.4
  7.2 518.6 %all-reduce.4.cloned.1.call-start = ((), (), s32[]{:S(2)}) async-start(), calls=%async_computation | async-start | bytes 4194304 | tf_op jit(solution)/shard_map/psum | solution.py:96
  368.7 0.6 copy-start.5
  442.0 87.9 %copy-start.2 = (f32[1024,128]{1,0:T(8,128)}, f32[1024,128]{1,0:T(8,128)S(1)}, u32[]{:S(2)}) copy-start(f32[1024,128]{1,0:T(8,128)S(1)} %get-tuple-element.189) | copy-start | bytes 1572868
  442.0 87.9 %copy-start.6 = (f32[1024]{0:T(1024)}, f32[1024]{0:T(1024)S(1)}, u32[]{:S(2)}) copy-start(f32[1024]{0:T(1024)S(1)} %get-tuple-element.697) | copy-start | bytes 12292
  442.0 83.8 %copy-start.3 = (bf16[8,512,128]{2,1,0:T(8,128)(2,1)S(1)}, bf16[8,512,128]{2,1,0:T(8,128)(2,1)}, u32[]{:S(2)}) copy-start(bf16[8,512,128]{2,1,0:T(8,128)(2,1)} %get-tuple-element.688) | copy-start | bytes 3145732
  442.0 148.5 %all-reduce.6.cloned.1.call-start = ((), (), s32[]{:S(2)}) async-start(), calls=%async_computation.1 | async-start | bytes 1179648 | tf_op jit(solution)/shard_map/psum | solution.py:103
Sparse Core Ops, SparseCore 0:
  442.1 83.6 all-reduce.3
  530.0 60.5 all-reduce.5
where the time goes:
time: 602 us; the launch traced here: 601 us
  blocking collectives  334 us (55%)
  waiting for transfers between devices  143 us (24%)
  matrix products  83.6 us (14%)
  other arithmetic  19 us (3%)
  between operations  14.3 us (2%)
    pmax x2, blocking collectives, row_reduce(): global_max = lax.pmax(largest, 'col')  145 us
    psum x2, blocking collectives, row_reduce(): global_sum = lax.psum(totals * jnp.exp(largest - global_max), 'col')  139 us
    psum x1, waiting for transfers between devices, local(): target_full = lax.psum(target_mix, 'col')  83.7 us
    psum x1, waiting for transfers between devices, local(): source_sum, cross_moment = lax.psum((source_mix, moment_part), 'row')  59.1 us
    dot_general x40, matrix products, score_tile(): lax.dot_general(proj_block, tgt_emb, (((1,), (1,)), ((), ())), preferred_...  55.7 us
    psum x2, blocking collectives, col_reduce(): global_sum = lax.psum(totals * jnp.exp(largest - global_max), 'row')  24.9 us
    pmax x2, blocking collectives, col_reduce(): global_max = lax.pmax(largest, 'row')  24.9 us
  transfers between devices with their start and end apart: 2, of which 2 were waited for; matrix products, arithmetic and copies ran while one was open for 0% of the time, Pallas kernels for 0%

commit v1 on v0

v1 whole, which is shorter than its diff:
```python
import functools
import math

import jax
import jax.numpy as jnp
from jax import lax
from jax.experimental import pallas as pl
from jax.experimental.pallas import tpu as pltpu
from jax.sharding import PartitionSpec as P

F32 = jnp.float32
BF16 = jnp.bfloat16
NT = (((1,), (1,)), ((), ()))
TINY = 2.0**-80
BLK = 256
CHUNK = 128
VMEM_LIMIT = 24 * 1024 * 1024


def split3(x):
    hi = x.astype(BF16).astype(F32)
    mid = (x - hi).astype(BF16).astype(F32)
    lo = (x - hi - mid).astype(BF16).astype(F32)
    return hi, mid, lo


def iota(shape, dim):
    return lax.broadcasted_iota(jnp.int32, shape, dim)


def lanes(b, size):
    return pl.ds(pl.multiple_of(b * size, size), size)


def aug_columns(shift):
    hi, mid, lo = split3(shift)
    lane = iota((shift.shape[0], 128), 1)
    out = jnp.where(lane < 3, 1.0, 0.0)
    out = jnp.where(lane == 3, hi, out)
    out = jnp.where(lane == 4, mid, out)
    out = jnp.where(lane == 5, lo, out)
    return out.astype(BF16)


def aug_rows(term):
    hi, mid, lo = split3(term)
    sub = iota((16, term.shape[1]), 0)
    out = jnp.where((sub >= 3) & (sub < 6), 1.0, 0.0)
    out = jnp.where(sub == 0, hi, out)
    out = jnp.where(sub == 1, mid, out)
    out = jnp.where(sub == 2, lo, out)
    zeros = jnp.zeros((112, term.shape[1]), BF16)
    return jnp.concatenate([out.astype(BF16), zeros], axis=0)


def log_sum(x):
    largest = jnp.max(x, axis=0, keepdims=True)
    return largest + jnp.log(jnp.sum(jnp.exp(x - largest), axis=0, keepdims=True))


def first_rows(src, tgt, factor, start, lse, proj_t, src_t, tgt_t, aug, *, copies):
    eye = jnp.where(iota((128, 128), 0) == iota((128, 128), 1), 1.0, 0.0).astype(BF16)
    factor_t = factor[...].astype(F32).T.astype(BF16)
    left = jnp.concatenate([factor_t, eye], axis=0)
    tgt_t[...] = lax.dot_general(eye, tgt[...], NT, preferred_element_type=F32).astype(BF16)
    column = jnp.broadcast_to(start[...], (8, start.shape[1])).T[:, :1]
    aug[:, :128] = tgt[...]
    aug[:, 128:] = aug_columns(column)
    under = aug_rows(jnp.zeros((1, BLK), F32))

    def block(b, carry):
        at = lanes(b, BLK)
        both = lax.dot_general(left, src[at, :], NT, preferred_element_type=F32).astype(BF16)
        proj_t[:, at] = both[:128]
        src_t[:, at] = both[128:]
        right = jnp.concatenate([both[:128], under], axis=0)
        largest = jnp.full((8, BLK), -jnp.inf, F32)
        total = jnp.zeros((8, BLK), F32)
        for c in range(tgt.shape[0] // CHUNK):
            x = jnp.dot(aug[c * CHUNK : (c + 1) * CHUNK, :], right, preferred_element_type=F32)
            x = x.reshape(CHUNK // 8, 8, BLK)
            new = jnp.maximum(largest, jnp.max(x, axis=0))
            total = total * jnp.exp(largest - new) + jnp.sum(jnp.exp(x - new[None]), axis=0)
            largest = new
        top = jnp.max(largest, axis=0, keepdims=True)
        value = top + jnp.log(jnp.sum(total * jnp.exp(largest - top), axis=0, keepdims=True))
        lse[:, at] = jnp.broadcast_to(value, (copies, BLK))
        return carry

    lax.fori_loop(0, src.shape[0] // BLK, block, 0)


def first_columns(parts, proj_t, aug_in, start, kernel_t, lse, shift, rho, aug, sums, *, copies):
    blocks = proj_t.shape[1] // BLK
    chunks = aug.shape[0] // CHUNK
    rho[...] = -log_sum(parts[...])
    aug[...] = aug_in[...]
    shift[...] = start[...]

    def scores(c, right):
        return jnp.dot(aug[c * CHUNK : (c + 1) * CHUNK, :], right, preferred_element_type=F32)

    def right_of(at):
        return jnp.concatenate([proj_t[:, at], aug_rows(rho[:, at])], axis=0)

    def fill():
        sums[...] = jnp.zeros_like(sums)

        def block(b, carry):
            at = lanes(b, BLK)
            right = right_of(at)
            for c in range(chunks):
                rows = slice(c * CHUNK, (c + 1) * CHUNK)
                e = jnp.exp(scores(c, right))
                kernel_t[rows, at] = e.astype(BF16)
                sums[rows, :] += e[:, :128] + e[:, 128:]
            return carry

        lax.fori_loop(0, blocks, block, 0)
        return jnp.sum(sums[...].T, axis=0, keepdims=True)

    total = fill()
    lse[...] = jnp.broadcast_to(jnp.log(total) - shift[...], lse.shape)

    @pl.when(jnp.min(total) < TINY)
    def _():
        sums[...] = jnp.full(sums.shape, -jnp.inf, F32)

        def block(b, carry):
            right = right_of(lanes(b, BLK))
            for c in range(chunks):
                rows = slice(c * CHUNK, (c + 1) * CHUNK)
                x = scores(c, right)
                sums[rows, :] = jnp.maximum(sums[rows, :], jnp.maximum(x[:, :128], x[:, 128:]))
            return carry

        lax.fori_loop(0, blocks, block, 0)
        top = jnp.max(sums[...], axis=1, keepdims=True)
        old = jnp.broadcast_to(start[...], (8, start.shape[1])).T[:, :1]
        aug[:, 128:] = aug_columns(old - top)
        wide = jnp.broadcast_to(top, sums.shape).T
        shift[...] = start[...] - wide[:1]
        again = fill()
        lse[...] = jnp.broadcast_to(jnp.log(again) - shift[...], lse.shape)


def second_rows(parts, shift, kernel_t, sums, weight, potential, *, src_count, tgt_count):
    total = log_sum(parts[...])
    potential[...] = math.log(src_count) - math.log(tgt_count) - total
    w = jnp.exp(-math.log(tgt_count) - total - shift[...])
    weight[...] = w
    hi = w.astype(BF16).astype(F32)
    sub = iota((16, w.shape[1]), 0)
    left = jnp.where(sub == 0, hi, jnp.where(sub == 1, w - hi, 0.0)).astype(BF16)
    size = 512

    def block(b, carry):
        at = lanes(b, size)
        x = jnp.dot(left, kernel_t[:, at], preferred_element_type=F32)
        sums[:, at] = jnp.broadcast_to(x[:1] + x[1:2], (sums.shape[0], size))
        return carry

    lax.fori_loop(0, kernel_t.shape[1] // size, block, 0)


def second_columns(
    core, parts, rho, kernel_t, src_t, weight, sums, keep, send, scale, potential, total, *, src_count
):
    q = jnp.sum(parts[...], axis=0, keepdims=True)
    u = 1.0 / (src_count * q)
    scale[...] = u
    potential[...] = rho[...] - 2.0 * math.log(src_count) - jnp.log(q)
    size = 512
    for b in range(kernel_t.shape[1] // size):
        at = slice(b * size, (b + 1) * size)
        ub = u[:, at]
        hi = ub.astype(BF16).astype(F32)
        sub = iota((16, size), 0)
        low = jnp.where(sub == 0, hi, jnp.where(sub == 1, ub - hi, 0.0)).astype(BF16)
        left = jnp.concatenate([(src_t[:, at].astype(F32) * ub).astype(BF16), low], axis=0)
        x = lax.dot_general(left, kernel_t[:, at], NT, preferred_element_type=F32)
        if b == 0:
            total[...] = x
        else:
            total[...] += x
    w = weight[...]
    sums[...] = jnp.broadcast_to(w * (total[128:129, :] + total[129:130, :]), sums.shape)
    half = keep.shape[0]
    own = core[0] * half
    keep[...] = total[pl.ds(pl.multiple_of(own, half), half), :] * w
    send[...] = total[pl.ds(pl.multiple_of(half - own, half), half), :] * w


def target_sums(parts, weight, before, tgt_t, kernel_t, scale, out, potential, gain, *, src_count, tgt_count):
    total = jnp.sum(parts[...], axis=0, keepdims=True)
    g = 1.0 / (tgt_count * total)
    gain[...] = g
    potential[...] = before[...] - math.log(tgt_count) - jnp.log(total)
    left = (tgt_t[...].astype(F32) * (weight[...] * g)).astype(BF16)
    share = out.shape[2]

    def block(b, carry):
        at = lanes(b, share)
        x = jnp.dot(left, kernel_t[:, at], preferred_element_type=F32)
        out[b] = x * (scale[:, at] * src_count)
        return carry

    lax.fori_loop(0, out.shape[0], block, 0)


def finish_sources(low, high, gain, tgt, moment, out, *, tgt_count):
    full = jnp.concatenate([low[...], high[...]], axis=0) * gain[...]
    moment[...] = jnp.dot(
        full, tgt[...].astype(F32), precision=lax.Precision.HIGHEST, preferred_element_type=F32
    )
    out[...] = (full * tgt_count).T.astype(BF16)


def finish_targets(parts, out):
    out[...] = jnp.sum(parts[...], axis=0).T.astype(BF16)


def call(body, outs, *args, scratch=(), smem=0):
    specs = [pl.BlockSpec(memory_space=pltpu.SMEM)] * smem
    specs += [pl.BlockSpec(memory_space=pltpu.VMEM)] * (len(args) - smem)
    return pl.pallas_call(
        body,
        out_shape=outs,
        in_specs=specs,
        out_specs=jax.tree.map(lambda _: pl.BlockSpec(memory_space=pltpu.VMEM), outs),
        scratch_shapes=list(scratch),
        compiler_params=pltpu.CompilerParams(vmem_limit_bytes=VMEM_LIMIT),
    )(*args)


def f32(*shape):
    return jax.ShapeDtypeStruct(shape, F32)


def bf16(*shape):
    return jax.ShapeDtypeStruct(shape, BF16)


def local(src_emb, tgt_emb, cost_factor, col_start):
    rows, cols = src_emb.shape[0], tgt_emb.shape[0]
    width = src_emb.shape[1]
    row_size, col_size = lax.axis_size("row"), lax.axis_size("col")
    src_count, tgt_count = rows * row_size, cols * col_size
    share = rows // col_size
    start = col_start.reshape(1, cols)
    core = lax.rem(lax.axis_index("row"), 2).reshape(1).astype(jnp.int32)

    def swap(x):
        return lax.ppermute(x, "row", [(i, i ^ 1) for i in range(row_size)])

    ring = ({0: 1, 1: 0, 2: 3, 3: 2}, {1: 2, 2: 1, 3: 0, 0: 3})

    def along_y(x, step):
        return lax.ppermute(x, "row", [(i, ring[step][i // 2] * 2 + i % 2) for i in range(row_size)])

    def along_z(x, step):
        return lax.ppermute(x, "col", [(i, ring[step][i // 4] * 4 + i % 4) for i in range(col_size)])

    def along_x(x, step):
        return lax.ppermute(x, "col", [(i, i // 4 * 4 + ring[step][i % 4]) for i in range(col_size)])

    def exchange(x, axis):
        return lax.all_to_all(x, axis, 0, 0)

    lse, proj_t, src_t, tgt_t, aug = call(
        functools.partial(first_rows, copies=col_size),
        [f32(col_size, rows), bf16(width, rows), bf16(width, rows), bf16(width, cols), bf16(cols, 2 * width)],
        src_emb, tgt_emb, cost_factor, start,
    )
    parts = exchange(lse, "col")
    kernel_t, lse, shift, rho = call(
        functools.partial(first_columns, copies=row_size),
        [pltpu.VMEM((cols, rows), BF16), f32(row_size, cols), f32(1, cols), f32(1, rows)],
        parts, proj_t, aug, start,
        scratch=[pltpu.VMEM((cols, 2 * width), BF16), pltpu.VMEM((cols, 128), F32)],
    )
    parts = exchange(lse, "row")
    sums, weight, before = call(
        functools.partial(second_rows, src_count=src_count, tgt_count=tgt_count),
        [f32(col_size, rows), f32(1, cols), f32(1, cols)],
        parts, shift, kernel_t,
    )
    parts = exchange(sums, "col")
    sums, keep, send, scale, row_potential = call(
        functools.partial(second_columns, src_count=src_count),
        [f32(row_size, cols), f32(width // 2, cols), f32(width // 2, cols), f32(1, rows), f32(1, rows)],
        core, parts, rho, kernel_t, src_t, weight,
        scratch=[pltpu.VMEM((width + 16, cols), F32)], smem=1,
    )
    parts = exchange(sums, "row")
    out, col_potential, gain = call(
        functools.partial(target_sums, src_count=src_count, tgt_count=tgt_count),
        [f32(col_size, width, share), f32(1, cols), f32(1, cols)],
        parts, weight, before, tgt_t, kernel_t, scale,
    )
    bary_src, = call(finish_targets, [bf16(share, width)], exchange(out, "col"))

    half = keep + swap(send)
    half = half + along_y(half, 0)
    half = half + along_y(half, 1)
    other = swap(half)
    first = core[0] == 0
    low = jnp.where(first, half, other)
    high = jnp.where(first, other, half)
    moment, bary_tgt = call(
        functools.partial(finish_sources, tgt_count=tgt_count),
        [f32(width, width), bf16(cols, width)],
        low, high, gain, tgt_emb,
    )
    for step in range(2):
        moment = moment + along_z(moment, step)
    for step in range(2):
        moment = moment + along_x(moment, step)
    return (bary_src, bary_tgt, moment, row_potential.reshape(rows), col_potential.reshape(cols))


def solution(mesh):
    placed = (P("row", None), P("col", None), P(), P("col"))
    return jax.shard_map(
        local,
        mesh=mesh,
        in_specs=placed,
        out_specs=(P(("row", "col"), None), P("col", None), P(), P("row"), P("col")),
        check_vma=False,
    )
```

time: 602 us -> 133 us (0.22)
  blocking collectives: 334 us -> 34 us
  waiting for transfers between devices: 143 us -> 41 us
  matrix products: 83.6 us -> 0 us
  Pallas kernels: 0 us -> 27.1 us
  other arithmetic: 19 us -> 0.82 us
  starting transfers between devices: 0.08 us -> 17.4 us
  between operations: 14.3 us -> 0.82 us
  local copies, waits for them, and re-layouts: 4.95 us -> 11.4 us
    pmax x4 -> x0, blocking collectives: 170 us -> none  [the longest x2 145 us: row_reduce(): global_max = lax.pmax(largest, 'col')]
    psum x4 -> x0, blocking collectives: 164 us -> none  [the longest x2 139 us: row_reduce(): global_sum = lax.psum(totals * jnp.exp(largest - global_max), 'col')]
    psum x2 -> x0, waiting for transfers between devices: 143 us -> none  [the longest x1 83.7 us: local(): target_full = lax.psum(target_mix, 'col')]
    dot_general x58 -> x0, matrix products: 83.6 us -> none  [the longest x40 55.7 us: score_tile(): lax.dot_general(proj_block, tgt_emb, (((1,), (1,)), ((), ())), preferred_...]
    all_to_all x0 -> x3, blocking collectives: none -> 34 us  [exchange(): return lax.all_to_all(x, axis, 0, 0)]
    ppermute x0 -> x8, waiting for transfers between devices: none -> 32.2 us  [the longest x2 15.3 us: along_y(): lax.ppermute(x, 'row', [(i, ring[step][i // 2] * 2 + i % 2) for i in rang...]
    pallas_call x0 -> x7, Pallas kernels: none -> 27.1 us  [call(): pl.pallas_call(body, out_shape=outs, in_specs=specs, out_specs=jax.tree.m...]
    reduce_sum x32 -> x0, other arithmetic: 15.4 us -> none  [the longest x16 8.6 us: row_block_step(): return (largest, jnp.sum(jnp.exp(logits - largest[:, None]), axis=1))]
  transfers between devices with their start and end apart: 2 -> 10, of which waited for: 2 -> 9; matrix products, arithmetic and copies ran while one was open for 0% -> 1% of each run, Pallas kernels for 0% -> 1%
where the time goes in v1:
time: 133 us
  waiting for transfers between devices  41 us (31%)
  blocking collectives  34 us (26%)
  Pallas kernels  27.1 us (20%)
  starting transfers between devices  17.4 us (13%)
  local copies, waits for them, and re-layouts  11.4 us (9%)
    all_to_all x3, blocking collectives, exchange(): return lax.all_to_all(x, axis, 0, 0)  34 us
    pallas_call x7, Pallas kernels, call(): pl.pallas_call(body, out_shape=outs, in_specs=specs, out_specs=jax.tree.m...  27.1 us
    ppermute x2, waiting for transfers between devices, along_y(): lax.ppermute(x, 'row', [(i, ring[step][i // 2] * 2 + i % 2) for i in rang...  15.3 us
    unnamed x32, local copies, waits for them, and re-layouts  10.1 us
    all_to_all x2, waiting for transfers between devices, exchange(): return lax.all_to_all(x, axis, 0, 0)  8.86 us
    ppermute x2, waiting for transfers between devices, along_z(): lax.ppermute(x, 'col', [(i, ring[step][i // 4] * 4 + i % 4) for i in rang...  7.77 us
    all_to_all x2, starting transfers between devices, exchange(): return lax.all_to_all(x, axis, 0, 0)  7.38 us
    ppermute x2, waiting for transfers between devices, along_x(): lax.ppermute(x, 'col', [(i, i // 4 * 4 + ring[step][i % 4]) for i in rang...  6.01 us
  transfers between devices with their start and end apart: 10, of which 9 were waited for; matrix products, arithmetic and copies ran while one was open for 1% of the time, Pallas kernels for 1%

profile of v1, /device:TPU:0, one launch (start us, length us, event | category | flops | bytes accessed | tf_op | source)
XLA Modules:
  0.0 132.7 jit_solution(1078853495181461259)
XLA Ops:
  0.6 1.2 copy-done.4
  1.9 0.9 copy-done.5
  2.8 0.8 copy-done.9
  4.3 9.9 %shard_map.83 = (f32[16,4096]{1,0:T(8,128)S(1)}, bf16[128,4096]{1,0:T(8,128)(2,1)S(1)}, bf16[128,4096]{1,0:T(8,128)(2,1)S(1)}, bf16[128,1024]{1,0:T(8,128)(2,1)S(1)}, bf16[1024,256]{1,0:T(8,128)(2,1)S(1)}) custom-call(bf16[4096,128]{1,0:T(8,128)(2,1)S(1)} %copy-done.4, bf16[1024,128]{1,0:T(8,128)(2,1)S(1)} %copy-done.5, bf16[128,128]{1,0:T(8,128)(2,1)S(1)} %copy-done.9, ...), custom_call_target="tpu_custom_call" | custom-call | tf_op jit(solution)/shard_map/pallas_call | solution.py:226
  14.4 16.5 %all_to_all.49 = f32[16,1,4096]{2,1,0:T(1,128)S(1)} all-to-all(f32[16,1,4096]{2,1,0:T(1,128)S(1)} %copy.9), channel_id=1, replica_groups=mesh['row'=8,'col'=16] {'col'}, dimensions={0} | all-to-all | bytes 524288 | tf_op jit(solution)/shard_map/all_to_all | solution.py:268
  31.0 5.3 %shard_map.84 = (bf16[1024,4096]{1,0:T(8,128)(2,1)S(1)}, f32[8,1024]{1,0:T(8,128)S(1)}, f32[1,1024]{1,0:T(1,128)S(1)}, f32[1,4096]{1,0:T(1,128)S(1)}) custom-call(f32[16,4096]{1,0:T(8,128)S(1)} %bitcast.21, bf16[128,4096]{1,0:T(8,128)(2,1)S(1)} %get-tuple-element.28.proj_t, bf16[1024,256]{1,0:T(8,128)(2,1)S(1)} %get-tuple-element.29.aug_in, ...), custom_call_target="tpu_custom_call" | custom-call | tf_op jit(solution)/shard_map/pallas_call | solution.py:226
  36.4 9.7 %all_to_all.50 = f32[8,1,1024]{2,1,0:T(1,128)S(1)} all-to-all(f32[8,1,1024]{2,1,0:T(1,128)S(1)} %copy.10), channel_id=1, replica_groups=mesh['row'=8,'col'=16] {'row'}, dimensions={0} | all-to-all | bytes 65536 | tf_op jit(solution)/shard_map/all_to_all | solution.py:268
  46.2 2.1 %shard_map.85 = (f32[16,4096]{1,0:T(8,128)S(1)}, f32[1,1024]{1,0:T(1,128)S(1)}, f32[1,1024]{1,0:T(1,128)S(1)}) custom-call(f32[8,1024]{1,0:T(8,128)S(1)} %bitcast.25, f32[1,1024]{1,0:T(1,128)S(1)} %get-tuple-element.31.shift, bf16[1024,4096]{1,0:T(8,128)(2,1)S(1)} %get-tuple-element.32.kernel_t), custom_call_target="tpu_custom_call" | custom-call | tf_op jit(solution)/shard_map/pallas_call | solution.py:226
  48.2 1.0 copy.11
  49.2 3.5 %all-to-all-start.2 = ((f32[16,1,4096]{2,1,0:T(1,128)}), f32[16,1,4096]{2,1,0:T(1,128)S(1)}, u32[]{:S(2)}, u32[]{:S(2)}) async-start(f32[16,1,4096]{2,1,0:T(1,128)} %copy.11), calls=%async_computation.2 | async-start | bytes 524288 | tf_op jit(solution)/shard_map/all_to_all | solution.py:268
  52.8 8.9 %all-to-all-done.2 = f32[16,1,4096]{2,1,0:T(1,128)S(1)} async-done(((f32[16,1,4096]{2,1,0:T(1,128)}), f32[16,1,4096]{2,1,0:T(1,128)S(1)}, u32[]{:S(2)}, u32[]{:S(2)}) %all-to-all-start.2) | async-done | bytes 262176 | tf_op jit(solution)/shard_map/all_to_all | solution.py:268
  61.8 3.4 %copy-done.1 = bf16[1024,4096]{1,0:T(8,128)(2,1)S(1)} copy-done((bf16[1024,4096]{1,0:T(8,128)(2,1)S(1)}, bf16[1024,4096]{1,0:T(8,128)(2,1)}, u32[]{:S(2)}) %copy-start.1) | copy-done | bytes 8388632
  65.2 3.5 %shard_map.86 = (f32[8,1024]{1,0:T(8,128)S(1)}, f32[64,1024]{1,0:T(8,128)S(1)}, f32[64,1024]{1,0:T(8,128)S(1)}, f32[1,4096]{1,0:T(1,128)S(1)}, f32[1,4096]{1,0:T(1,128)}) custom-call(s32[1]{0:T(128)} %bitcast.core, f32[16,4096]{1,0:T(8,128)S(1)} %bitcast.20, f32[1,4096]{1,0:T(1,128)S(1)} %get-tuple-element.34.rho, bf16[1024,4096]{1,0:T(8,128)(2,1)S(1)} %copy-done.1, ...), custom_call_target="tpu_custom_call" | custom-call | tf_op jit(solution)/shard_map/pallas_call | solution.py:226
  70.1 7.8 %all_to_all.51 = f32[8,1,1024]{2,1,0:T(1,128)S(1)} all-to-all(f32[8,1,1024]{2,1,0:T(1,128)S(1)} %copy.12), channel_id=1, replica_groups=mesh['row'=8,'col'=16] {'row'}, dimensions={0} | all-to-all | bytes 65536 | tf_op jit(solution)/shard_map/all_to_all | solution.py:268
  78.0 4.3 %shard_map.87 = (f32[16,128,256]{2,1,0:T(8,128)S(1)}, f32[1,1024]{1,0:T(1,128)}, f32[1,1024]{1,0:T(1,128)S(1)}) custom-call(f32[8,1024]{1,0:T(8,128)S(1)} %bitcast.24, f32[1,1024]{1,0:T(1,128)S(1)} %get-tuple-element.36.weight, f32[1,1024]{1,0:T(1,128)S(1)} %get-tuple-element.38.before, bf16[128,1024]{1,0:T(8,128)(2,1)S(1)} %get-tuple-element.39.tgt_t, ...), custom_call_target="tpu_custom_call" | custom-call | tf_op jit(solution)/shard_map/pallas_call | solution.py:226
  82.3 1.4 %copy-done.3 = f32[16,128,256]{2,1,0:T(8,128)} copy-done((f32[16,128,256]{2,1,0:T(8,128)}, f32[16,128,256]{2,1,0:T(8,128)S(1)}, u32[]{:S(2)}) %copy-start.3) | copy-done | bytes 2097176
  83.7 3.8 %all-to-all-start.4 = ((f32[16,128,256]{2,1,0:T(8,128)}), f32[16,128,256]{2,1,0:T(8,128)S(1)}, u32[]{:S(2)}, u32[]{:S(2)}) async-start(f32[16,128,256]{2,1,0:T(8,128)} %copy-done.3), calls=%async_computation.4 | async-start | bytes 4194304 | tf_op jit(solution)/shard_map/all_to_all | solution.py:268
  87.6 1.5 %collective-permute-done = f32[64,1024]{1,0:T(8,128)S(1)} collective-permute-done((f32[64,1024]{1,0:T(8,128)S(1)}, f32[64,1024]{1,0:T(8,128)S(1)}, u32[]{:S(2)}, u32[]{:S(2)}) %collective-permute-start) | collective-permute-done | bytes 262176 | tf_op jit(solution)/shard_map/ppermute | solution.py:254
  89.9 7.8 %collective-permute-done.1 = f32[64,1024]{1,0:T(8,128)S(1)} collective-permute-done((f32[64,1024]{1,0:T(8,128)S(1)}, f32[64,1024]{1,0:T(8,128)S(1)}, u32[]{:S(2)}, u32[]{:S(2)}) %collective-permute-start.1) | collective-permute-done | bytes 262176 | tf_op jit(solution)/shard_map/ppermute | solution.py:259
  97.7 1.2 collective-permute-start.2
  98.9 7.6 %collective-permute-done.2 = f32[64,1024]{1,0:T(8,128)S(1)} collective-permute-done((f32[64,1024]{1,0:T(8,128)S(1)}, f32[64,1024]{1,0:T(8,128)S(1)}, u32[]{:S(2)}, u32[]{:S(2)}) %collective-permute-start.2) | collective-permute-done | bytes 262176 | tf_op jit(solution)/shard_map/ppermute | solution.py:259
  106.6 1.5 %collective-permute-done.3 = f32[64,1024]{1,0:T(8,128)S(1)} collective-permute-done((f32[64,1024]{1,0:T(8,128)S(1)}, f32[64,1024]{1,0:T(8,128)S(1)}, u32[]{:S(2)}, u32[]{:S(2)}) %collective-permute-start.3) | collective-permute-done | bytes 262176 | tf_op jit(solution)/shard_map/ppermute | solution.py:254
  108.2 1.2 shard_map.89
  109.4 1.8 %collective-permute-start.4 = (f32[128,128]{1,0:T(8,128)S(1)}, f32[128,128]{1,0:T(8,128)S(1)}, u32[]{:S(2)}, u32[]{:S(2)}) collective-permute-start(f32[128,128]{1,0:T(8,128)S(1)} %get-tuple-element.46), channel_id=1, source_target_pairs={{0,4},{1,5},{2,6},{3,7},{4,0},{5,1},{6,2},{7,3},{8,12},{9,13},{10,... | collective-permute-start | bytes 196616 | tf_op jit(solution)/shard_map/ppermute | solution.py:262
  111.3 3.3 %collective-permute-done.4 = f32[128,128]{1,0:T(8,128)S(1)} collective-permute-done((f32[128,128]{1,0:T(8,128)S(1)}, f32[128,128]{1,0:T(8,128)S(1)}, u32[]{:S(2)}, u32[]{:S(2)}) %collective-permute-start.4) | collective-permute-done | bytes 65568 | tf_op jit(solution)/shard_map/ppermute | solution.py:262
  114.6 2.3 %collective-permute-start.5 = (f32[128,128]{1,0:T(8,128)S(1)}, f32[128,128]{1,0:T(8,128)S(1)}, u32[]{:S(2)}, u32[]{:S(2)}) collective-permute-start(f32[128,128]{1,0:T(8,128)S(1)} %add.24), channel_id=1, source_target_pairs={{0,12},{1,13},{2,14},{3,15},{4,8},{5,9},{6,10},{7,11},{8,4},{9,5},... | collective-permute-start | bytes 196616 | tf_op jit(solution)/shard_map/ppermute | solution.py:262
  116.9 4.5 %collective-permute-done.5 = f32[128,128]{1,0:T(8,128)S(1)} collective-permute-done((f32[128,128]{1,0:T(8,128)S(1)}, f32[128,128]{1,0:T(8,128)S(1)}, u32[]{:S(2)}, u32[]{:S(2)}) %collective-permute-start.5) | collective-permute-done | bytes 65568 | tf_op jit(solution)/shard_map/ppermute | solution.py:262
  121.3 1.2 collective-permute-start.6
  122.6 3.1 %collective-permute-done.6 = f32[128,128]{1,0:T(8,128)S(1)} collective-permute-done((f32[128,128]{1,0:T(8,128)S(1)}, f32[128,128]{1,0:T(8,128)S(1)}, u32[]{:S(2)}, u32[]{:S(2)}) %collective-permute-start.6) | collective-permute-done | bytes 65568 | tf_op jit(solution)/shard_map/ppermute | solution.py:265
  125.7 2.7 %collective-permute-start.7 = (f32[128,128]{1,0:T(8,128)S(1)}, f32[128,128]{1,0:T(8,128)S(1)}, u32[]{:S(2)}, u32[]{:S(2)}) collective-permute-start(f32[128,128]{1,0:T(8,128)S(1)} %add.26), channel_id=1, source_target_pairs={{0,3},{1,2},{2,1},{3,0},{4,7},{5,6},{6,5},{7,4},{8,11},{9,10},{10,... | collective-permute-start | bytes 196616 | tf_op jit(solution)/shard_map/ppermute | solution.py:265
  128.4 2.9 %collective-permute-done.7 = f32[128,128]{1,0:T(8,128)S(1)} collective-permute-done((f32[128,128]{1,0:T(8,128)S(1)}, f32[128,128]{1,0:T(8,128)S(1)}, u32[]{:S(2)}, u32[]{:S(2)}) %collective-permute-start.7) | collective-permute-done | bytes 65568 | tf_op jit(solution)/shard_map/ppermute | solution.py:265
  131.9 0.8 shard_map.88
  (42 shorter events, 4.5 us)
Async XLA Ops:
  0.6 1.2 copy-start.4
  1.9 0.9 copy-start.5
  2.8 0.8 copy-start.9
  3.6 0.7 copy-start.10
  4.3 26.8 %copy-start.11 = (f32[1024]{0:T(1024)S(1)}, f32[1024]{0:T(1024)}, u32[]{:S(2)}) copy-start(f32[1024]{0:T(1024)} %param.7) | copy-start | bytes 12292
  36.4 11.9 %copy-start = (bf16[1024,4096]{1,0:T(8,128)(2,1)}, bf16[1024,4096]{1,0:T(8,128)(2,1)S(1)}, u32[]{:S(2)}) copy-start(bf16[1024,4096]{1,0:T(8,128)(2,1)S(1)} %get-tuple-element.32.kernel_t) | copy-start | bytes 25165828
  49.2 12.4 %all-to-all-start.2 = ((f32[16,1,4096]{2,1,0:T(1,128)}), f32[16,1,4096]{2,1,0:T(1,128)S(1)}, u32[]{:S(2)}, u32[]{:S(2)}) async-start(f32[16,1,4096]{2,1,0:T(1,128)} %copy.11), calls=%async_computation.2 | async-start | bytes 524288 | tf_op jit(solution)/shard_map/all_to_all | solution.py:268
  61.8 3.4 %copy-start.1 = (bf16[1024,4096]{1,0:T(8,128)(2,1)S(1)}, bf16[1024,4096]{1,0:T(8,128)(2,1)}, u32[]{:S(2)}) copy-start(bf16[1024,4096]{1,0:T(8,128)(2,1)} %copy-done) | copy-start | bytes 25165828
  65.2 12.8 %copy-start.2 = (bf16[1024,4096]{1,0:T(8,128)(2,1)S(1)}, bf16[1024,4096]{1,0:T(8,128)(2,1)}, u32[]{:S(2)}) copy-start(bf16[1024,4096]{1,0:T(8,128)(2,1)} %copy-done) | copy-start | bytes 25165828
  68.7 0.7 copy-start.7
  69.4 0.7 copy-start.12
  82.3 1.4 %copy-start.3 = (f32[16,128,256]{2,1,0:T(8,128)}, f32[16,128,256]{2,1,0:T(8,128)S(1)}, u32[]{:S(2)}) copy-start(f32[16,128,256]{2,1,0:T(8,128)S(1)} %get-tuple-element.41) | copy-start | bytes 6291460
  83.7 3.9 %copy-start.13 = (f32[64,1024]{1,0:T(8,128)S(1)}, f32[64,1024]{1,0:T(8,128)}, u32[]{:S(2)}) copy-start(f32[64,1024]{1,0:T(8,128)} %copy-done.12) | copy-start | bytes 786436
  83.7 5.5 %copy-start.8 = (f32[64,1024]{1,0:T(8,128)S(1)}, f32[64,1024]{1,0:T(8,128)}, u32[]{:S(2)}) copy-start(f32[64,1024]{1,0:T(8,128)} %copy-done.7) | copy-start | bytes 786436
  83.7 48.2 %all-to-all-start.4 = ((f32[16,128,256]{2,1,0:T(8,128)}), f32[16,128,256]{2,1,0:T(8,128)S(1)}, u32[]{:S(2)}, u32[]{:S(2)}) async-start(f32[16,128,256]{2,1,0:T(8,128)} %copy-done.3), calls=%async_computation.4 | async-start | bytes 4194304 | tf_op jit(solution)/shard_map/all_to_all | solution.py:268
  87.5 20.7 %copy-start.6 = (bf16[1024,128]{1,0:T(8,128)(2,1)S(1)}, bf16[1024,128]{1,0:T(8,128)(2,1)}, u32[]{:S(2)}) copy-start(bf16[1024,128]{1,0:T(8,128)(2,1)} %tgt.3) | copy-start | bytes 786436
  87.6 1.6 %collective-permute-start = (f32[64,1024]{1,0:T(8,128)S(1)}, f32[64,1024]{1,0:T(8,128)S(1)}, u32[]{:S(2)}, u32[]{:S(2)}) collective-permute-start(f32[64,1024]{1,0:T(8,128)S(1)} %copy-done.13), channel_id=1, source_target_pairs={{0,16},{16,0},{32,48},{48,32},{64,80},{80,64},{96,112},{112,96},{1... | collective-permute-start | bytes 786440 | tf_op jit(solution)/shard_map/ppermute | solution.py:254
  89.2 8.4 %collective-permute-start.1 = (f32[64,1024]{1,0:T(8,128)S(1)}, f32[64,1024]{1,0:T(8,128)S(1)}, u32[]{:S(2)}, u32[]{:S(2)}) collective-permute-start(f32[64,1024]{1,0:T(8,128)S(1)} %add.21), channel_id=1, source_target_pairs={{0,32},{16,48},{32,0},{48,16},{64,96},{80,112},{96,64},{112,80},{1... | collective-permute-start | bytes 786440 | tf_op jit(solution)/shard_map/ppermute | solution.py:259
  97.7 8.8 %collective-permute-start.2 = (f32[64,1024]{1,0:T(8,128)S(1)}, f32[64,1024]{1,0:T(8,128)S(1)}, u32[]{:S(2)}, u32[]{:S(2)}) collective-permute-start(f32[64,1024]{1,0:T(8,128)S(1)} %add.22), channel_id=1, source_target_pairs={{0,96},{16,112},{32,64},{48,80},{64,32},{80,48},{96,0},{112,16},{1... | collective-permute-start | bytes 786440 | tf_op jit(solution)/shard_map/ppermute | solution.py:259
  106.5 1.6 %collective-permute-start.3 = (f32[64,1024]{1,0:T(8,128)S(1)}, f32[64,1024]{1,0:T(8,128)S(1)}, u32[]{:S(2)}, u32[]{:S(2)}) collective-permute-start(f32[64,1024]{1,0:T(8,128)S(1)} %add.23), channel_id=1, source_target_pairs={{0,16},{16,0},{32,48},{48,32},{64,80},{80,64},{96,112},{112,96},{1... | collective-permute-start | bytes 786440 | tf_op jit(solution)/shard_map/ppermute | solution.py:254
  109.4 5.1 %collective-permute-start.4 = (f32[128,128]{1,0:T(8,128)S(1)}, f32[128,128]{1,0:T(8,128)S(1)}, u32[]{:S(2)}, u32[]{:S(2)}) collective-permute-start(f32[128,128]{1,0:T(8,128)S(1)} %get-tuple-element.46), channel_id=1, source_target_pairs={{0,4},{1,5},{2,6},{3,7},{4,0},{5,1},{6,2},{7,3},{8,12},{9,13},{10,... | collective-permute-start | bytes 196616 | tf_op jit(solution)/shard_map/ppermute | solution.py:262
  114.6 6.7 %collective-permute-start.5 = (f32[128,128]{1,0:T(8,128)S(1)}, f32[128,128]{1,0:T(8,128)S(1)}, u32[]{:S(2)}, u32[]{:S(2)}) collective-permute-start(f32[128,128]{1,0:T(8,128)S(1)} %add.24), channel_id=1, source_target_pairs={{0,12},{1,13},{2,14},{3,15},{4,8},{5,9},{6,10},{7,11},{8,4},{9,5},... | collective-permute-start | bytes 196616 | tf_op jit(solution)/shard_map/ppermute | solution.py:262
  121.3 4.3 %collective-permute-start.6 = (f32[128,128]{1,0:T(8,128)S(1)}, f32[128,128]{1,0:T(8,128)S(1)}, u32[]{:S(2)}, u32[]{:S(2)}) collective-permute-start(f32[128,128]{1,0:T(8,128)S(1)} %add.25), channel_id=1, source_target_pairs={{0,1},{1,0},{2,3},{3,2},{4,5},{5,4},{6,7},{7,6},{8,9},{9,8},{10,11... | collective-permute-start | bytes 196616 | tf_op jit(solution)/shard_map/ppermute | solution.py:265
  125.7 5.6 %collective-permute-start.7 = (f32[128,128]{1,0:T(8,128)S(1)}, f32[128,128]{1,0:T(8,128)S(1)}, u32[]{:S(2)}, u32[]{:S(2)}) collective-permute-start(f32[128,128]{1,0:T(8,128)S(1)} %add.26), channel_id=1, source_target_pairs={{0,3},{1,2},{2,1},{3,0},{4,7},{5,6},{6,5},{7,4},{8,11},{9,10},{10,... | collective-permute-start | bytes 196616 | tf_op jit(solution)/shard_map/ppermute | solution.py:265

commit v2 on v1

v2 whole, which is shorter than its diff:
```python
import functools
import math

import jax
import jax.numpy as jnp
from jax import lax
from jax.experimental import pallas as pl
from jax.experimental.pallas import tpu as pltpu
from jax.sharding import PartitionSpec as P

F32 = jnp.float32
BF16 = jnp.bfloat16
NT = (((1,), (1,)), ((), ()))
TINY = 2.0**-80
BLK = 512
CHUNK = 256
SLABS = BLK // 128
VMEM_LIMIT = 24 * 1024 * 1024


def split3(x):
    hi = x.astype(BF16).astype(F32)
    mid = (x - hi).astype(BF16).astype(F32)
    lo = (x - hi - mid).astype(BF16).astype(F32)
    return hi, mid, lo


def iota(shape, dim):
    return lax.broadcasted_iota(jnp.int32, shape, dim)


def lanes(b, size):
    if isinstance(b, int):
        return slice(b * size, (b + 1) * size)
    return pl.ds(pl.multiple_of(b * size, size), size)


def aug_columns(shift):
    hi, mid, lo = split3(shift)
    lane = iota((shift.shape[0], 128), 1)
    out = jnp.where(lane < 3, 1.0, 0.0)
    out = jnp.where(lane == 3, hi, out)
    out = jnp.where(lane == 4, mid, out)
    out = jnp.where(lane == 5, lo, out)
    return out.astype(BF16)


def aug_rows(term):
    hi, mid, lo = split3(term)
    sub = iota((16, term.shape[1]), 0)
    out = jnp.where((sub >= 3) & (sub < 6), 1.0, 0.0)
    out = jnp.where(sub == 0, hi, out)
    out = jnp.where(sub == 1, mid, out)
    out = jnp.where(sub == 2, lo, out)
    zeros = jnp.zeros((112, term.shape[1]), BF16)
    return jnp.concatenate([out.astype(BF16), zeros], axis=0)


def log_sum(x):
    largest = jnp.max(x, axis=0, keepdims=True)
    return largest + jnp.log(jnp.sum(jnp.exp(x - largest), axis=0, keepdims=True))


def flat(x):
    return jnp.concatenate([x[i : i + 1, :] for i in range(x.shape[0])], axis=1)


def stack(x, width):
    return jnp.concatenate([x[:, i * width : (i + 1) * width] for i in range(x.shape[1] // width)], axis=0)


def column(x):
    return jnp.broadcast_to(x, (8, x.shape[1])).T[:, :1]


def identity(n):
    return jnp.where(iota((n, n), 0) == iota((n, n), 1), 1.0, 0.0).astype(BF16)


def first_rows(src_in, tgt_in, factor_in, start_in, lse, proj_t, aug, src, factor, start, sems):
    copies = [
        pltpu.make_async_copy(factor_in, factor, sems.at[0]),
        pltpu.make_async_copy(src_in, src, sems.at[1]),
        pltpu.make_async_copy(start_in, start, sems.at[2]),
        pltpu.make_async_copy(tgt_in, aug.at[:, pl.ds(0, 128)], sems.at[3]),
    ]
    for copy in copies:
        copy.start()
    under = aug_rows(jnp.zeros((1, BLK), F32))
    for copy in copies:
        copy.wait()
    factor_t = factor[...].astype(F32).T.astype(BF16)
    proj_t[...] = lax.dot_general(factor_t, src[...], NT, preferred_element_type=F32).astype(BF16)
    aug[:, 128:] = aug_columns(column(flat(start[...])))
    values = []
    for b in range(src.shape[0] // BLK):
        right = jnp.concatenate([proj_t[:, b * BLK : (b + 1) * BLK], under], axis=0)
        largest = jnp.full((8, BLK), -jnp.inf, F32)
        total = jnp.zeros((8, BLK), F32)
        for c in range(aug.shape[0] // CHUNK):
            x = jnp.dot(aug[c * CHUNK : (c + 1) * CHUNK, :], right, preferred_element_type=F32)
            x = x.reshape(CHUNK // 8, 8, BLK)
            new = jnp.maximum(largest, jnp.max(x, axis=0))
            total = total * jnp.exp(largest - new) + jnp.sum(jnp.exp(x - new[None]), axis=0)
            largest = new
        top = jnp.max(largest, axis=0, keepdims=True)
        values.append(top + jnp.log(jnp.sum(total * jnp.exp(largest - top), axis=0, keepdims=True)))
    lse[...] = jnp.broadcast_to(jnp.concatenate([stack(v, 128) for v in values], axis=0)[None], lse.shape)


def transposes(src, tgt, src_t, tgt_t):
    eye = identity(128)
    tgt_t[...] = lax.dot_general(eye, tgt[...], NT, preferred_element_type=F32).astype(BF16)
    src_t[...] = lax.dot_general(eye, src[...], NT, preferred_element_type=F32).astype(BF16)


def first_columns(parts, proj_t, aug, start, kernel_t, lse, shift, rho, sums, spare):
    blocks = proj_t.shape[1] // BLK
    chunks = aug.shape[0] // CHUNK
    rho[...] = -log_sum(parts[...])[0]
    shift[...] = start[...]

    def right_of(b):
        term = jnp.concatenate([rho[pl.ds(b * SLABS + i, 1), :] for i in range(SLABS)], axis=1)
        return jnp.concatenate([proj_t[:, lanes(b, BLK)], aug_rows(term)], axis=0)

    def fold(x, op):
        out = x[:, :128]
        for i in range(1, BLK // 128):
            out = op(out, x[:, i * 128 : (i + 1) * 128])
        return out

    def fill(left, b):
        right = right_of(b)
        for c in range(chunks):
            rows = slice(c * CHUNK, (c + 1) * CHUNK)
            e = jnp.exp(jnp.dot(left[rows, :], right, preferred_element_type=F32))
            for i in range(SLABS):
                kernel_t[b * SLABS + i, rows, :] = e[:, i * 128 : (i + 1) * 128].astype(BF16)
            sums[rows, :] += fold(e, jnp.add)

    def column_sums():
        return stack(jnp.sum(sums[...].T, axis=0, keepdims=True), 128)

    sums[...] = jnp.zeros_like(sums)
    for b in range(blocks):
        fill(aug, b)
    total = column_sums()
    lse[...] = jnp.broadcast_to((jnp.log(total) - shift[...])[None], lse.shape)

    @pl.when(jnp.min(total) < TINY)
    def _():
        sums[...] = jnp.full(sums.shape, -jnp.inf, F32)

        def largest(b, carry):
            right = right_of(b)
            for c in range(chunks):
                rows = slice(c * CHUNK, (c + 1) * CHUNK)
                x = jnp.dot(aug[rows, :], right, preferred_element_type=F32)
                sums[rows, :] = jnp.maximum(sums[rows, :], fold(x, jnp.maximum))
            return carry

        lax.fori_loop(0, blocks, largest, 0)
        top = jnp.max(sums[...], axis=1, keepdims=True)
        spare[:, :128] = aug[:, :128]
        spare[:, 128:] = aug_columns(column(flat(start[...])) - top)
        shift[...] = start[...] - stack(jnp.broadcast_to(top, sums.shape).T[:1], 128)
        sums[...] = jnp.zeros_like(sums)

        def again(b, carry):
            fill(spare, b)
            return carry

        lax.fori_loop(0, blocks, again, 0)
        lse[...] = jnp.broadcast_to((jnp.log(column_sums()) - shift[...])[None], lse.shape)


def slabs(ref, first, count):
    return jnp.concatenate([ref[first + i] for i in range(count)], axis=1)


def second_rows(parts, shift, kernel_t, sums, weight, potential, *, src_count, tgt_count):
    total = log_sum(parts[...])[0]
    potential[...] = math.log(src_count) - math.log(tgt_count) - total
    w = jnp.exp(-math.log(tgt_count) - total - shift[...])
    weight[...] = w
    w = flat(w)
    hi = w.astype(BF16).astype(F32)
    sub = iota((16, w.shape[1]), 0)
    left = jnp.where(sub == 0, hi, jnp.where(sub == 1, w - hi, 0.0)).astype(BF16)
    values = []
    for b in range(kernel_t.shape[0] // SLABS):
        x = jnp.dot(left, slabs(kernel_t, b * SLABS, SLABS), preferred_element_type=F32)
        values.append(stack(x[:1] + x[1:2], 128))
    sums[...] = jnp.broadcast_to(jnp.concatenate(values, axis=0)[None], sums.shape)


def second_columns(parts, rho, kernel_t, src_t, weight, sums, keep, send, scale, potential, total, *, src_count):
    q = jnp.sum(parts[...], axis=0)
    u = 1.0 / (src_count * q)
    scale[...] = u
    potential[...] = rho[...] - 2.0 * math.log(src_count) - jnp.log(q)
    for b in range(kernel_t.shape[0] // SLABS):
        ub = flat(u[b * SLABS : (b + 1) * SLABS, :])
        hi = ub.astype(BF16).astype(F32)
        sub = iota((16, BLK), 0)
        low = jnp.where(sub == 0, hi, jnp.where(sub == 1, ub - hi, 0.0)).astype(BF16)
        scaled = (src_t[:, b * BLK : (b + 1) * BLK].astype(F32) * ub).astype(BF16)
        left = jnp.concatenate([scaled, low], axis=0)
        x = lax.dot_general(left, slabs(kernel_t, b * SLABS, SLABS), NT, preferred_element_type=F32)
        if b == 0:
            total[...] = x
        else:
            total[...] += x
    w = weight[...]
    sums[...] = jnp.broadcast_to((w * stack(total[128:129, :] + total[129:130, :], 128))[None], sums.shape)
    w = flat(w)
    half = keep.shape[0]
    own = lax.rem(lax.axis_index("row"), 2) * half
    keep[...] = total[pl.ds(pl.multiple_of(own, half), half), :] * w
    send[...] = total[pl.ds(pl.multiple_of(half - own, half), half), :] * w


def share_of(major, minor):
    col = lax.axis_index("col")
    return ((col // 4) ^ major) * 4 + ((col % 4) ^ minor)


def halves(offsets):
    first = [2 * share_of(a, b) for a in offsets for b in range(4)]
    second = [2 * share_of(b, a) + 1 for a in offsets for b in range(4)]
    return first + second


def mix(left, kernel_t, scale, held, sems, outs, offsets, src_count):
    places = halves(offsets)
    copies = [pltpu.make_async_copy(kernel_t.at[at], held.at[k], sems.at[k]) for k, at in enumerate(places)]
    for copy in copies:
        copy.start()
    factor = left()
    for copy in copies:
        copy.wait()
    for k in range(0, len(places), 2):
        x = jnp.dot(factor, slabs(held, k, 2), preferred_element_type=F32)
        for i in range(2):
            out = outs[(k + i) // 8]
            out[(k + i) % 8] = x[:, i * 128 : (i + 1) * 128] * (scale[pl.ds(places[k + i], 1), :] * src_count)


def target_send(
    parts, weight, before, tgt_t, kernel_t, scale, out_a, out_b, left, potential, gain, held, sems, *, src_count, tgt_count
):
    def factor():
        total = jnp.sum(parts[...], axis=0)
        g = 1.0 / (tgt_count * total)
        gain[...] = g
        potential[...] = before[...] - math.log(tgt_count) - jnp.log(total)
        value = (tgt_t[...].astype(F32) * flat(weight[...] * g)).astype(BF16)
        left[...] = value
        return value

    mix(factor, kernel_t, scale, held, sems, (out_a, out_b), (1, 2), src_count)


def target_keep(left, kernel_t, scale, out_a, out_b, held, sems, *, src_count):
    mix(lambda: left[...], kernel_t, scale, held, sems, (out_a, out_b), (0, 3), src_count)


def finish_sources(mine, other, gain, tgt, moment, out, *, tgt_count):
    even = lax.rem(lax.axis_index("row"), 2) == 0
    low = jnp.where(even, mine[...], other[...])
    high = jnp.where(even, other[...], mine[...])
    full = jnp.concatenate([low, high], axis=0) * flat(gain[...])
    moment[...] = jnp.dot(
        full, tgt[...].astype(F32), precision=lax.Precision.HIGHEST, preferred_element_type=F32
    )
    out[...] = (full * tgt_count).T.astype(BF16)


def merge_first(keep_a, got_a, keep_b, got_b, moment, send_a, hold_a, send_b, hold_b):
    for i, (keep, got, send, hold) in enumerate(((keep_a, got_a, send_a, hold_a), (keep_b, got_b, send_b, hold_b))):
        for k in range(4):
            hold[k] = keep[k] + got[k]
            send[k * 128 : (k + 1) * 128, :] = keep[4 + k] + got[4 + k]
        send[512:576, :] = moment[i * 64 : (i + 1) * 64, :]


def merge_second(hold_a, sent_a, got_a, hold_b, sent_b, got_b, send_a, next_a, send_b, next_b):
    for hold, sent, got, send, after in (
        (hold_a, sent_a, got_a, send_a, next_a),
        (hold_b, sent_b, got_b, send_b, next_b),
    ):
        for k in range(4):
            value = hold[k] + got[k * 128 : (k + 1) * 128, :]
            if k in (1, 2):
                send[(k - 1) * 128 : k * 128, :] = value
            else:
                after[k // 3] = value
        send[256:320, :] = sent[512:576, :] + got[512:576, :]


def merge_third(hold_a, sent_a, got_a, hold_b, sent_b, got_b, send_a, next_a, send_b, next_b):
    for hold, sent, got, send, after in (
        (hold_a, sent_a, got_a, send_a, next_a),
        (hold_b, sent_b, got_b, send_b, next_b),
    ):
        after[...] = hold[0] + got[:128, :]
        send[:128, :] = hold[1] + got[128:256, :]
        send[128:192, :] = sent[256:320, :] + got[256:320, :]


def merge_last(hold_a, sent_a, got_a, hold_b, sent_b, got_b, bary, moment_a, moment_b):
    bary[:128, :] = (hold_a[...] + got_a[:128, :]).T.astype(BF16)
    bary[128:, :] = (hold_b[...] + got_b[:128, :]).T.astype(BF16)
    moment_a[...] = sent_a[128:192, :] + got_a[128:192, :]
    moment_b[...] = sent_b[128:192, :] + got_b[128:192, :]


def call(body, outs, *args, scratch=(), spaces=None):
    spaces = spaces or {}
    return pl.pallas_call(
        body,
        out_shape=outs,
        in_specs=[pl.BlockSpec(memory_space=spaces.get(i, pltpu.VMEM)) for i in range(len(args))],
        out_specs=jax.tree.map(lambda _: pl.BlockSpec(memory_space=pltpu.VMEM), outs),
        scratch_shapes=list(scratch),
        compiler_params=pltpu.CompilerParams(vmem_limit_bytes=VMEM_LIMIT),
    )(*args)


def f32(*shape):
    return jax.ShapeDtypeStruct(shape, F32)


def bf16(*shape):
    return jax.ShapeDtypeStruct(shape, BF16)


def near(x):
    return pltpu.with_memory_space_constraint(x, pltpu.VMEM)


def far(x):
    return pltpu.with_memory_space_constraint(x, pltpu.HBM)


def local(src_emb, tgt_emb, cost_factor, col_start):
    rows, cols = src_emb.shape[0], tgt_emb.shape[0]
    width = src_emb.shape[1]
    row_size, col_size = lax.axis_size("row"), lax.axis_size("col")
    src_count, tgt_count = rows * row_size, cols * col_size
    counts = dict(src_count=src_count, tgt_count=tgt_count)
    share = rows // col_size
    row_shape, col_shape = (rows // 128, 128), (cols // 128, 128)
    start = col_start.reshape(col_shape)

    def swap(x):
        return lax.ppermute(x, "row", [(i, i ^ 1) for i in range(row_size)])

    def along_y(x, k):
        return lax.ppermute(x, "row", [(i, i ^ (2 * k)) for i in range(row_size)])

    def along_z(x, k):
        return lax.ppermute(x, "col", [(i, i ^ (4 * k)) for i in range(col_size)])

    def along_x(x, k):
        return lax.ppermute(x, "col", [(i, i ^ k) for i in range(col_size)])

    def exchange(x, axis):
        return lax.all_to_all(x, axis, 0, 0)

    lse, proj_t, aug = call(
        first_rows,
        [f32(col_size, *row_shape), bf16(width, rows), bf16(cols, 2 * width)],
        far(src_emb), far(tgt_emb), far(cost_factor), far(start),
        scratch=[
            pltpu.VMEM((rows, width), BF16),
            pltpu.VMEM((width, width), BF16),
            pltpu.VMEM(col_shape, F32),
            pltpu.SemaphoreType.DMA((4,)),
        ],
        spaces={i: pltpu.HBM for i in range(4)},
    )
    parts = exchange(lse, "col")
    src_late, tgt_late, _ = lax.optimization_barrier((src_emb, tgt_emb, proj_t))
    src_t, tgt_t = call(transposes, [bf16(width, rows), bf16(width, cols)], src_late, tgt_late)
    parts, src_t, tgt_t = lax.optimization_barrier((parts, src_t, tgt_t))
    kernel_t, lse, shift, rho = call(
        first_columns,
        [pltpu.VMEM((rows // 128, cols, 128), BF16), f32(row_size, *col_shape), f32(*col_shape), f32(*row_shape)],
        parts, proj_t, aug, start,
        scratch=[pltpu.VMEM((cols, 128), F32), pltpu.VMEM((cols, 2 * width), BF16)],
    )
    parts = exchange(lse, "row")
    sums, weight, before = call(
        functools.partial(second_rows, **counts),
        [f32(col_size, *row_shape), f32(*col_shape), f32(*col_shape)],
        parts, shift, near(kernel_t),
    )
    parts = exchange(sums, "col")
    sums, keep, send, scale, row_potential = call(
        functools.partial(second_columns, src_count=src_count),
        [f32(row_size, *col_shape), f32(width // 2, cols), f32(width // 2, cols), f32(*row_shape), f32(*row_shape)],
        parts, rho, near(kernel_t), src_t, weight,
        scratch=[pltpu.VMEM((width + 16, cols), F32)],
    )
    mine = keep + swap(send)
    sums, mine = lax.optimization_barrier((sums, mine))
    parts = exchange(sums, "row")
    mine = mine + along_y(mine, 1)
    parts, mine = lax.optimization_barrier((parts, mine))
    arrived = along_y(mine, 3)
    held = [pltpu.VMEM((16, cols, 128), BF16), pltpu.SemaphoreType.DMA((16,))]
    message = f32(8, width, 128)
    send_a, send_b, left, col_potential, gain = call(
        functools.partial(target_send, **counts),
        [message, message, bf16(width, cols), f32(*col_shape), f32(*col_shape)],
        parts, weight, before, tgt_t, far(kernel_t), scale,
        scratch=held, spaces={4: pltpu.HBM},
    )
    got_a, got_b = along_z(send_a, 1), along_x(send_b, 1)
    keep_a, keep_b = call(
        functools.partial(target_keep, src_count=src_count),
        [message, message],
        left, far(kernel_t), scale,
        scratch=held, spaces={1: pltpu.HBM},
    )
    mine, gain = lax.optimization_barrier((mine, gain))
    mine = mine + arrived
    moment, bary_tgt = call(
        functools.partial(finish_sources, tgt_count=tgt_count),
        [f32(width, width), bf16(cols, width)],
        mine, swap(mine), gain, tgt_emb,
    )
    send_a, hold_a, send_b, hold_b = call(
        merge_first, [f32(576, 128), f32(4, 128, 128)] * 2, keep_a, got_a, keep_b, got_b, moment
    )
    got_a, got_b = along_z(send_a, 3), along_x(send_b, 3)
    send_a, hold_a, send_b, hold_b = call(
        merge_second, [f32(320, 128), f32(2, 128, 128)] * 2, hold_a, send_a, got_a, hold_b, send_b, got_b
    )
    got_a, got_b = along_x(send_a, 1), along_z(send_b, 1)
    send_a, hold_a, send_b, hold_b = call(
        merge_third, [f32(192, 128), f32(128, 128)] * 2, hold_a, send_a, got_a, hold_b, send_b, got_b
    )
    got_a, got_b = along_x(send_a, 3), along_z(send_b, 3)
    bary_src, moment_a, moment_b = call(
        merge_last,
        [bf16(share, width), f32(64, 128), f32(64, 128)],
        hold_a, send_a, got_a, hold_b, send_b, got_b,
    )
    moment = jnp.concatenate([moment_a + along_z(moment_a, 1), moment_b + along_x(moment_b, 1)], axis=0)
    return (bary_src, bary_tgt, moment, row_potential.reshape(rows), col_potential.reshape(cols))


def solution(mesh):
    placed = (P("row", None), P("col", None), P(), P("col"))
    return jax.shard_map(
        local,
        mesh=mesh,
        in_specs=placed,
        out_specs=(P(("row", "col"), None), P("col", None), P(), P("row"), P("col")),
        check_vma=False,
    )
```

time: 133 us -> 111 us (0.83)
  blocking collectives: 34 us -> 21.3 us
  local copies, waits for them, and re-layouts: 11.4 us -> 2.86 us
  starting transfers between devices: 17.4 us -> 22.6 us
  Pallas kernels: 27.1 us -> 23.3 us
  waiting for transfers between devices: 41 us -> 39.3 us
    all_to_all x3 -> x2, blocking collectives: 34 us -> 21.3 us  [exchange(): return lax.all_to_all(x, axis, 0, 0)]
    unnamed x32 -> x10, local copies, waits for them, and re-layouts: 10.1 us -> 2.86 us
    all_to_all x2, starting transfers between devices: 7.38 us -> 11.3 us  [exchange(): return lax.all_to_all(x, axis, 0, 0)]
    pallas_call x7 -> x12, Pallas kernels: 27.1 us -> 23.3 us  [call(): pl.pallas_call(body, out_shape=outs, in_specs=[pl.BlockSpec(memory_space=...]
    all_to_all x2, waiting for transfers between devices: 8.86 us -> 6.81 us  [exchange(): return lax.all_to_all(x, axis, 0, 0)]
    ppermute x6 -> x12, waiting for transfers between devices: 29.1 us -> 30.9 us  [the longest x5 15.2 us: along_z(): return lax.ppermute(x, 'col', [(i, i ^ 4 * k) for i in range(col_size)])]
    ppermute x2, waiting for transfers between devices: 3.04 us -> 1.54 us  [swap(): return lax.ppermute(x, 'row', [(i, i ^ 1) for i in range(row_size)])]
    ppermute x6 -> x12, starting transfers between devices: 9.9 us -> 11.2 us  [the longest x5 4.39 us: along_z(): return lax.ppermute(x, 'col', [(i, i ^ 4 * k) for i in range(col_size)])]
  transfers between devices with their start and end apart: 10 -> 16, of which waited for: 9 -> 14; matrix products, arithmetic and copies ran while one was open for 1% -> 0% of each run, Pallas kernels for 1% -> 7%
where the time goes in v2:
time: 111 us
  waiting for transfers between devices  39.3 us (35%)
  Pallas kernels  23.3 us (21%)
  starting transfers between devices  22.6 us (20%)
  blocking collectives  21.3 us (19%)
  local copies, waits for them, and re-layouts  2.86 us (3%)
    pallas_call x12, Pallas kernels, call(): pl.pallas_call(body, out_shape=outs, in_specs=[pl.BlockSpec(memory_space=...  23.3 us
    all_to_all x2, blocking collectives, exchange(): return lax.all_to_all(x, axis, 0, 0)  21.3 us
    ppermute x5, waiting for transfers between devices, along_z(): return lax.ppermute(x, 'col', [(i, i ^ 4 * k) for i in range(col_size)])  15.2 us
    all_to_all x2, starting transfers between devices, exchange(): return lax.all_to_all(x, axis, 0, 0)  11.3 us
    ppermute x5, waiting for transfers between devices, along_x(): return lax.ppermute(x, 'col', [(i, i ^ k) for i in range(col_size)])  8.04 us
    ppermute x2, waiting for transfers between devices, along_y(): return lax.ppermute(x, 'row', [(i, i ^ 2 * k) for i in range(row_size)])  7.7 us
    all_to_all x2, waiting for transfers between devices, exchange(): return lax.all_to_all(x, axis, 0, 0)  6.81 us
    ppermute x5, starting transfers between devices, along_z(): return lax.ppermute(x, 'col', [(i, i ^ 4 * k) for i in range(col_size)])  4.39 us
  transfers between devices with their start and end apart: 16, of which 14 were waited for; matrix products, arithmetic and copies ran while one was open for 0% of the time, Pallas kernels for 7%

profile of v2, /device:TPU:0, one launch (start us, length us, event | category | flops | bytes accessed | tf_op | source)
XLA Modules:
  0.0 110.9 jit_solution(5662306445354567905)
XLA Ops:
  0.6 6.7 %shard_map.83 = (f32[16,32,128]{2,1,0:T(8,128)}, bf16[128,4096]{1,0:T(8,128)(2,1)S(1)}, bf16[1024,256]{1,0:T(8,128)(2,1)S(1)}) custom-call(bf16[4096,128]{1,0:T(8,128)(2,1)} %src, bf16[1024,128]{1,0:T(8,128)(2,1)} %tgt.2, bf16[128,128]{1,0:T(8,128)(2,1)} %factor_in.1, f32[8,128]{1,0:T(8,128)} %bitcast.3), custom_call_target="tpu_custom_call" | custom-call | tf_op jit(solution)/shard_map/pallas_call | solution.py:321
  7.3 8.0 %all-to-all-start = ((f32[16,32,128]{2,1,0:T(8,128)}), f32[16,32,128]{2,1,0:T(8,128)S(1)}, u32[]{:S(2)}, u32[]{:S(2)}) async-start(f32[16,32,128]{2,1,0:T(8,128)} %get-tuple-element.57), calls=%async_computation | async-start | bytes 524288 | tf_op jit(solution)/shard_map/all_to_all | solution.py:370
  15.3 1.2 %copy-done.1 = bf16[4096,128]{1,0:T(8,128)(2,1)S(1)} copy-done((bf16[4096,128]{1,0:T(8,128)(2,1)S(1)}, bf16[4096,128]{1,0:T(8,128)(2,1)}, u32[]{:S(2)}) %copy-start.1) | copy-done | bytes 1048600
  16.5 0.9 copy-done.2
  18.0 6.0 %all-to-all-done.parts = f32[16,32,128]{2,1,0:T(8,128)S(1)} async-done(((f32[16,32,128]{2,1,0:T(8,128)}), f32[16,32,128]{2,1,0:T(8,128)S(1)}, u32[]{:S(2)}, u32[]{:S(2)}) %all-to-all-start) | async-done | bytes 262176 | tf_op jit(solution)/shard_map/all_to_all | solution.py:370
  24.6 2.9 %shard_map.85 = (bf16[32,1024,128]{2,1,0:T(8,128)(2,1)S(1)}, f32[8,8,128]{2,1,0:T(8,128)S(1)}, f32[8,128]{1,0:T(8,128)S(1)}, f32[32,128]{1,0:T(8,128)S(1)}) custom-call(f32[16,32,128]{2,1,0:T(8,128)S(1)} %all-to-all-done.parts, bf16[128,4096]{1,0:T(8,128)(2,1)S(1)} %get-tuple-element.58.proj_t, bf16[1024,256]{1,0:T(8,128)(2,1)S(1)} %get-tuple-element.64.aug, ...), custom_call_target="tpu_custom_call" | custom-call | tf_op jit(solution)/shard_map/pallas_call | solution.py:321
  27.5 9.7 %all_to_all.20.parts = f32[8,8,128]{2,1,0:T(8,128)S(1)} all-to-all(f32[8,8,128]{2,1,0:T(8,128)S(1)} %get-tuple-element.65), channel_id=1, replica_groups=mesh['row'=8,'col'=16] {'row'}, dimensions={0} | all-to-all | bytes 65536 | tf_op jit(solution)/shard_map/all_to_all | solution.py:370
  37.2 1.2 %shard_map.86 = (f32[16,32,128]{2,1,0:T(8,128)S(1)}, f32[8,128]{1,0:T(8,128)S(1)}, f32[8,128]{1,0:T(8,128)S(1)}) custom-call(f32[8,8,128]{2,1,0:T(8,128)S(1)} %all_to_all.20.parts, f32[8,128]{1,0:T(8,128)S(1)} %get-tuple-element.66.shift, bf16[32,1024,128]{2,1,0:T(8,128)(2,1)S(1)} %get-tuple-element.67.kernel_t), custom_call_target="tpu_custom_call" | custom-call | tf_op jit(solution)/shard_map/pallas_call | solution.py:321
  38.5 11.6 %all_to_all.21.parts = f32[16,32,128]{2,1,0:T(8,128)S(1)} all-to-all(f32[16,32,128]{2,1,0:T(8,128)S(1)} %get-tuple-element.68), channel_id=1, replica_groups=mesh['row'=8,'col'=16] {'col'}, dimensions={0} | all-to-all | bytes 524288 | tf_op jit(solution)/shard_map/all_to_all | solution.py:370
  50.1 3.5 %shard_map.87 = (f32[8,8,128]{2,1,0:T(8,128)}, f32[64,1024]{1,0:T(8,128)S(1)}, f32[64,1024]{1,0:T(8,128)S(1)}, f32[32,128]{1,0:T(8,128)S(1)}, f32[32,128]{1,0:T(8,128)}) custom-call(f32[16,32,128]{2,1,0:T(8,128)S(1)} %all_to_all.21.parts, f32[32,128]{1,0:T(8,128)S(1)} %get-tuple-element.69.rho, bf16[32,1024,128]{2,1,0:T(8,128)(2,1)S(1)} %get-tuple-element.67.kernel_t, ...), custom_call_target="tpu_custom_call" | custom-call | tf_op jit(solution)/shard_map/pallas_call | solution.py:321
  53.6 1.5 %collective-permute-done = f32[64,1024]{1,0:T(8,128)S(1)} collective-permute-done((f32[64,1024]{1,0:T(8,128)S(1)}, f32[64,1024]{1,0:T(8,128)S(1)}, u32[]{:S(2)}, u32[]{:S(2)}) %collective-permute-start) | collective-permute-done | bytes 262176 | tf_op jit(solution)/shard_map/ppermute | solution.py:358
  55.8 3.3 %all-to-all-start.3 = ((f32[8,8,128]{2,1,0:T(8,128)}), f32[8,8,128]{2,1,0:T(8,128)S(1)}, u32[]{:S(2)}, u32[]{:S(2)}) async-start(f32[8,8,128]{2,1,0:T(8,128)} %get-tuple-element.75), calls=%async_computation.3 | async-start | bytes 65536 | tf_op jit(solution)/shard_map/all_to_all | solution.py:370
  59.2 4.6 %collective-permute-done.1 = f32[64,1024]{1,0:T(8,128)S(1)} collective-permute-done((f32[64,1024]{1,0:T(8,128)S(1)}, f32[64,1024]{1,0:T(8,128)S(1)}, u32[]{:S(2)}, u32[]{:S(2)}) %collective-permute-start.1) | collective-permute-done | bytes 262176 | tf_op jit(solution)/shard_map/ppermute | solution.py:361
  63.8 0.8 all-to-all-done.3.parts
  64.6 2.0 %collective-permute-start.4 = (f32[64,1024]{1,0:T(8,128)S(1)}, f32[64,1024]{1,0:T(8,128)S(1)}, u32[]{:S(2)}, u32[]{:S(2)}) collective-permute-start(f32[64,1024]{1,0:T(8,128)S(1)} %add.16), channel_id=1, source_target_pairs={{0,96},{16,112},{32,64},{48,80},{64,32},{80,48},{96,0},{112,16},{1... | collective-permute-start | bytes 786440 | tf_op jit(solution)/shard_map/ppermute | solution.py:361
  66.6 3.3 %shard_map.88 = (f32[8,128,128]{2,1,0:T(8,128)S(1)}, f32[8,128,128]{2,1,0:T(8,128)S(1)}, bf16[128,1024]{1,0:T(8,128)(2,1)S(1)}, f32[8,128]{1,0:T(8,128)}, f32[8,128]{1,0:T(8,128)S(1)}) custom-call(f32[8,8,128]{2,1,0:T(8,128)S(1)} %all-to-all-done.3.parts, f32[8,128]{1,0:T(8,128)S(1)} %get-tuple-element.71.weight, f32[8,128]{1,0:T(8,128)S(1)} %get-tuple-element.78.before, ...), custom_call_target="tpu_custom_call" | custom-call | tf_op jit(solution)/shard_map/pallas_call | solution.py:321
  70.7 3.1 %collective-permute-done.4 = f32[64,1024]{1,0:T(8,128)S(1)} collective-permute-done((f32[64,1024]{1,0:T(8,128)S(1)}, f32[64,1024]{1,0:T(8,128)S(1)}, u32[]{:S(2)}, u32[]{:S(2)}) %collective-permute-start.4) | collective-permute-done | bytes 262176 | tf_op jit(solution)/shard_map/ppermute | solution.py:361
  73.9 3.0 %shard_map.89 = (f32[8,128,128]{2,1,0:T(8,128)S(1)}, f32[8,128,128]{2,1,0:T(8,128)S(1)}) custom-call(bf16[128,1024]{1,0:T(8,128)(2,1)S(1)} %get-tuple-element.81.left, bf16[32,1024,128]{2,1,0:T(8,128)(2,1)} %copy-done, f32[32,128]{1,0:T(8,128)S(1)} %get-tuple-element.80.scale), custom_call_target="tpu_custom_call" | custom-call | tf_op jit(solution)/shard_map/pallas_call | solution.py:321
  77.0 1.3 %shard_map.90 = (f32[128,128]{1,0:T(8,128)S(1)}, bf16[1024,128]{1,0:T(8,128)(2,1)}) custom-call(f32[64,1024]{1,0:T(8,128)S(1)} %add.17.mine, f32[64,1024]{1,0:T(8,128)S(1)} %collective-permute-done.5.other, f32[8,128]{1,0:T(8,128)S(1)} %get-tuple-element.89.gain, bf16[1024,128]{1,0:T(8,128)(2,1)S(1)} %copy-done.3), custom_call_target="tpu_custom_call" | custom-call | tf_op jit(solution)/shard_map/pallas_call | solution.py:321
  78.3 5.1 %collective-permute-done.2.got_a = f32[8,128,128]{2,1,0:T(8,128)S(1)} collective-permute-done((f32[8,128,128]{2,1,0:T(8,128)S(1)}, f32[8,128,128]{2,1,0:T(8,128)S(1)}, u32[]{:S(2)}, u32[]{:S(2)}) %collective-permute-start.2) | collective-permute-done | bytes 524320 | tf_op jit(solution)/shard_map/ppermute | solution.py:364
  83.6 1.3 %collective-permute-start.6 = (f32[576,128]{1,0:T(8,128)S(1)}, f32[576,128]{1,0:T(8,128)S(1)}, u32[]{:S(2)}, u32[]{:S(2)}) collective-permute-start(f32[576,128]{1,0:T(8,128)S(1)} %get-tuple-element.92.sent_a), channel_id=1, source_target_pairs={{0,12},{1,13},{2,14},{3,15},{4,8},{5,9},{6,10},{7,11},{8,4},{9,5},... | collective-permute-start | bytes 884744 | tf_op jit(solution)/shard_map/ppermute | solution.py:364
  84.9 1.1 collective-permute-start.7
  86.0 6.3 %collective-permute-done.6.got_a = f32[576,128]{1,0:T(8,128)S(1)} collective-permute-done((f32[576,128]{1,0:T(8,128)S(1)}, f32[576,128]{1,0:T(8,128)S(1)}, u32[]{:S(2)}, u32[]{:S(2)}) %collective-permute-start.6) | collective-permute-done | bytes 294944 | tf_op jit(solution)/shard_map/ppermute | solution.py:364
  93.2 0.9 collective-permute-start.9
  94.1 4.4 %collective-permute-done.8.got_a = f32[320,128]{1,0:T(8,128)S(1)} collective-permute-done((f32[320,128]{1,0:T(8,128)S(1)}, f32[320,128]{1,0:T(8,128)S(1)}, u32[]{:S(2)}, u32[]{:S(2)}) %collective-permute-start.8) | collective-permute-done | bytes 163872 | tf_op jit(solution)/shard_map/ppermute | solution.py:367
  98.6 1.2 %collective-permute-start.10 = (f32[192,128]{1,0:T(8,128)S(1)}, f32[192,128]{1,0:T(8,128)S(1)}, u32[]{:S(2)}, u32[]{:S(2)}) collective-permute-start(f32[192,128]{1,0:T(8,128)S(1)} %get-tuple-element.100.sent_a), channel_id=1, source_target_pairs={{0,3},{1,2},{2,1},{3,0},{4,7},{5,6},{6,5},{7,4},{8,11},{9,10},{10,... | collective-permute-start | bytes 294920 | tf_op jit(solution)/shard_map/ppermute | solution.py:367
  99.8 1.9 %collective-permute-start.11 = (f32[192,128]{1,0:T(8,128)S(1)}, f32[192,128]{1,0:T(8,128)S(1)}, u32[]{:S(2)}, u32[]{:S(2)}) collective-permute-start(f32[192,128]{1,0:T(8,128)S(1)} %get-tuple-element.102.sent_b), channel_id=1, source_target_pairs={{0,12},{1,13},{2,14},{3,15},{4,8},{5,9},{6,10},{7,11},{8,4},{9,5},... | collective-permute-start | bytes 294920 | tf_op jit(solution)/shard_map/ppermute | solution.py:364
  101.7 2.8 %collective-permute-done.10.got_a = f32[192,128]{1,0:T(8,128)S(1)} collective-permute-done((f32[192,128]{1,0:T(8,128)S(1)}, f32[192,128]{1,0:T(8,128)S(1)}, u32[]{:S(2)}, u32[]{:S(2)}) %collective-permute-start.10) | collective-permute-done | bytes 98336 | tf_op jit(solution)/shard_map/ppermute | solution.py:367
  104.5 1.1 collective-permute-done.11.got_b
  105.6 0.7 shard_map.94
  106.3 1.3 %collective-permute-start.13 = (f32[64,128]{1,0:T(8,128)S(1)}, f32[64,128]{1,0:T(8,128)S(1)}, u32[]{:S(2)}, u32[]{:S(2)}) collective-permute-start(f32[64,128]{1,0:T(8,128)S(1)} %get-tuple-element.106), channel_id=1, source_target_pairs={{0,1},{1,0},{2,3},{3,2},{4,5},{5,4},{6,7},{7,6},{8,9},{9,8},{10,11... | collective-permute-start | bytes 98312 | tf_op jit(solution)/shard_map/ppermute | solution.py:367
  107.7 2.6 %collective-permute-done.12 = f32[64,128]{1,0:T(8,128)S(1)} collective-permute-done((f32[64,128]{1,0:T(8,128)S(1)}, f32[64,128]{1,0:T(8,128)S(1)}, u32[]{:S(2)}, u32[]{:S(2)}) %collective-permute-start.12) | collective-permute-done | bytes 32800 | tf_op jit(solution)/shard_map/ppermute | solution.py:364
  (30 shorter events, 4.7 us)
Async XLA Ops:
  7.3 16.7 %all-to-all-start = ((f32[16,32,128]{2,1,0:T(8,128)}), f32[16,32,128]{2,1,0:T(8,128)S(1)}, u32[]{:S(2)}, u32[]{:S(2)}) async-start(f32[16,32,128]{2,1,0:T(8,128)} %get-tuple-element.57), calls=%async_computation | async-start | bytes 524288 | tf_op jit(solution)/shard_map/all_to_all | solution.py:370
  15.3 1.2 %copy-start.1 = (bf16[4096,128]{1,0:T(8,128)(2,1)S(1)}, bf16[4096,128]{1,0:T(8,128)(2,1)}, u32[]{:S(2)}) copy-start(bf16[4096,128]{1,0:T(8,128)(2,1)} %src) | copy-start | bytes 3145732
  16.5 0.9 copy-start.2
  24.0 0.7 copy-start.4
  27.5 26.1 %copy-start = (bf16[32,1024,128]{2,1,0:T(8,128)(2,1)}, bf16[32,1024,128]{2,1,0:T(8,128)(2,1)S(1)}, u32[]{:S(2)}) copy-start(bf16[32,1024,128]{2,1,0:T(8,128)(2,1)S(1)} %get-tuple-element.67.kernel_t) | copy-start | bytes 25165828
  53.6 1.5 %collective-permute-start = (f32[64,1024]{1,0:T(8,128)S(1)}, f32[64,1024]{1,0:T(8,128)S(1)}, u32[]{:S(2)}, u32[]{:S(2)}) collective-permute-start(f32[64,1024]{1,0:T(8,128)S(1)} %get-tuple-element.74), channel_id=1, source_target_pairs={{0,16},{16,0},{32,48},{48,32},{64,80},{80,64},{96,112},{112,96},{1... | collective-permute-start | bytes 786440 | tf_op jit(solution)/shard_map/ppermute | solution.py:358
  55.2 8.6 %collective-permute-start.1 = (f32[64,1024]{1,0:T(8,128)S(1)}, f32[64,1024]{1,0:T(8,128)S(1)}, u32[]{:S(2)}, u32[]{:S(2)}) collective-permute-start(f32[64,1024]{1,0:T(8,128)S(1)} %add.15), channel_id=1, source_target_pairs={{0,32},{16,48},{32,0},{48,16},{64,96},{80,112},{96,64},{112,80},{1... | collective-permute-start | bytes 786440 | tf_op jit(solution)/shard_map/ppermute | solution.py:361
  55.8 8.8 %all-to-all-start.3 = ((f32[8,8,128]{2,1,0:T(8,128)}), f32[8,8,128]{2,1,0:T(8,128)S(1)}, u32[]{:S(2)}, u32[]{:S(2)}) async-start(f32[8,8,128]{2,1,0:T(8,128)} %get-tuple-element.75), calls=%async_computation.3 | async-start | bytes 65536 | tf_op jit(solution)/shard_map/all_to_all | solution.py:370
  64.6 9.2 %collective-permute-start.4 = (f32[64,1024]{1,0:T(8,128)S(1)}, f32[64,1024]{1,0:T(8,128)S(1)}, u32[]{:S(2)}, u32[]{:S(2)}) collective-permute-start(f32[64,1024]{1,0:T(8,128)S(1)} %add.16), channel_id=1, source_target_pairs={{0,96},{16,112},{32,64},{48,80},{64,32},{80,48},{96,0},{112,16},{1... | collective-permute-start | bytes 786440 | tf_op jit(solution)/shard_map/ppermute | solution.py:361
  66.6 10.4 %copy-start.3 = (bf16[1024,128]{1,0:T(8,128)(2,1)S(1)}, bf16[1024,128]{1,0:T(8,128)(2,1)}, u32[]{:S(2)}) copy-start(bf16[1024,128]{1,0:T(8,128)(2,1)} %tgt.2) | copy-start | bytes 786436
  70.0 13.4 %collective-permute-start.2 = (f32[8,128,128]{2,1,0:T(8,128)S(1)}, f32[8,128,128]{2,1,0:T(8,128)S(1)}, u32[]{:S(2)}, u32[]{:S(2)}) collective-permute-start(f32[8,128,128]{2,1,0:T(8,128)S(1)} %get-tuple-element.83), channel_id=1, source_target_pairs={{0,4},{1,5},{2,6},{3,7},{4,0},{5,1},{6,2},{7,3},{8,12},{9,13},{10,... | collective-permute-start | bytes 1572872 | tf_op jit(solution)/shard_map/ppermute | solution.py:364
  70.3 13.2 %collective-permute-start.3 = (f32[8,128,128]{2,1,0:T(8,128)S(1)}, f32[8,128,128]{2,1,0:T(8,128)S(1)}, u32[]{:S(2)}, u32[]{:S(2)}) collective-permute-start(f32[8,128,128]{2,1,0:T(8,128)S(1)} %get-tuple-element.85), channel_id=1, source_target_pairs={{0,1},{1,0},{2,3},{3,2},{4,5},{5,4},{6,7},{7,6},{8,9},{9,8},{10,11... | collective-permute-start | bytes 1572872 | tf_op jit(solution)/shard_map/ppermute | solution.py:367
  73.9 3.1 %collective-permute-start.5 = (f32[64,1024]{1,0:T(8,128)S(1)}, f32[64,1024]{1,0:T(8,128)S(1)}, u32[]{:S(2)}, u32[]{:S(2)}) collective-permute-start(f32[64,1024]{1,0:T(8,128)S(1)} %add.17.mine), channel_id=1, source_target_pairs={{0,16},{16,0},{32,48},{48,32},{64,80},{80,64},{96,112},{112,96},{1... | collective-permute-start | bytes 786440 | tf_op jit(solution)/shard_map/ppermute | solution.py:358
  83.6 8.7 %collective-permute-start.6 = (f32[576,128]{1,0:T(8,128)S(1)}, f32[576,128]{1,0:T(8,128)S(1)}, u32[]{:S(2)}, u32[]{:S(2)}) collective-permute-start(f32[576,128]{1,0:T(8,128)S(1)} %get-tuple-element.92.sent_a), channel_id=1, source_target_pairs={{0,12},{1,13},{2,14},{3,15},{4,8},{5,9},{6,10},{7,11},{8,4},{9,5},... | collective-permute-start | bytes 884744 | tf_op jit(solution)/shard_map/ppermute | solution.py:364
  84.9 8.1 %collective-permute-start.7 = (f32[576,128]{1,0:T(8,128)S(1)}, f32[576,128]{1,0:T(8,128)S(1)}, u32[]{:S(2)}, u32[]{:S(2)}) collective-permute-start(f32[576,128]{1,0:T(8,128)S(1)} %get-tuple-element.94.sent_b), channel_id=1, source_target_pairs={{0,3},{1,2},{2,1},{3,0},{4,7},{5,6},{6,5},{7,4},{8,11},{9,10},{10,... | collective-permute-start | bytes 884744 | tf_op jit(solution)/shard_map/ppermute | solution.py:367
  93.1 5.4 %collective-permute-start.8 = (f32[320,128]{1,0:T(8,128)S(1)}, f32[320,128]{1,0:T(8,128)S(1)}, u32[]{:S(2)}, u32[]{:S(2)}) collective-permute-start(f32[320,128]{1,0:T(8,128)S(1)} %get-tuple-element.96.sent_a), channel_id=1, source_target_pairs={{0,1},{1,0},{2,3},{3,2},{4,5},{5,4},{6,7},{7,6},{8,9},{9,8},{10,11... | collective-permute-start | bytes 491528 | tf_op jit(solution)/shard_map/ppermute | solution.py:367
  93.2 5.4 %collective-permute-start.9 = (f32[320,128]{1,0:T(8,128)S(1)}, f32[320,128]{1,0:T(8,128)S(1)}, u32[]{:S(2)}, u32[]{:S(2)}) collective-permute-start(f32[320,128]{1,0:T(8,128)S(1)} %get-tuple-element.98.sent_b), channel_id=1, source_target_pairs={{0,4},{1,5},{2,6},{3,7},{4,0},{5,1},{6,2},{7,3},{8,12},{9,13},{10,... | collective-permute-start | bytes 491528 | tf_op jit(solution)/shard_map/ppermute | solution.py:364
  98.6 5.9 %collective-permute-start.10 = (f32[192,128]{1,0:T(8,128)S(1)}, f32[192,128]{1,0:T(8,128)S(1)}, u32[]{:S(2)}, u32[]{:S(2)}) collective-permute-start(f32[192,128]{1,0:T(8,128)S(1)} %get-tuple-element.100.sent_a), channel_id=1, source_target_pairs={{0,3},{1,2},{2,1},{3,0},{4,7},{5,6},{6,5},{7,4},{8,11},{9,10},{10,... | collective-permute-start | bytes 294920 | tf_op jit(solution)/shard_map/ppermute | solution.py:367
  99.8 5.8 %collective-permute-start.11 = (f32[192,128]{1,0:T(8,128)S(1)}, f32[192,128]{1,0:T(8,128)S(1)}, u32[]{:S(2)}, u32[]{:S(2)}) collective-permute-start(f32[192,128]{1,0:T(8,128)S(1)} %get-tuple-element.102.sent_b), channel_id=1, source_target_pairs={{0,12},{1,13},{2,14},{3,15},{4,8},{5,9},{6,10},{7,11},{8,4},{9,5},... | collective-permute-start | bytes 294920 | tf_op jit(solution)/shard_map/ppermute | solution.py:364
  106.3 3.9 %collective-permute-start.12 = (f32[64,128]{1,0:T(8,128)S(1)}, f32[64,128]{1,0:T(8,128)S(1)}, u32[]{:S(2)}, u32[]{:S(2)}) collective-permute-start(f32[64,128]{1,0:T(8,128)S(1)} %get-tuple-element.105), channel_id=1, source_target_pairs={{0,4},{1,5},{2,6},{3,7},{4,0},{5,1},{6,2},{7,3},{8,12},{9,13},{10,... | collective-permute-start | bytes 98312 | tf_op jit(solution)/shard_map/ppermute | solution.py:364
  106.3 3.9 %collective-permute-start.13 = (f32[64,128]{1,0:T(8,128)S(1)}, f32[64,128]{1,0:T(8,128)S(1)}, u32[]{:S(2)}, u32[]{:S(2)}) collective-permute-start(f32[64,128]{1,0:T(8,128)S(1)} %get-tuple-element.106), channel_id=1, source_target_pairs={{0,1},{1,0},{2,3},{3,2},{4,5},{5,4},{6,7},{7,6},{8,9},{9,8},{10,11... | collective-permute-start | bytes 98312 | tf_op jit(solution)/shard_map/ppermute | solution.py:367

commit v3 on v2

--- a/solution.py
+++ b/solution.py
@@ -77,7 +77,7 @@
     return jnp.where(iota((n, n), 0) == iota((n, n), 1), 1.0, 0.0).astype(BF16)
 
 
-def first_rows(src_in, tgt_in, factor_in, start_in, lse, proj_t, aug, src, factor, start, sems):
+def first_rows(src_in, tgt_in, factor_in, start_in, lse, proj_t, aug, start, src, factor, sems):
     copies = [
         pltpu.make_async_copy(factor_in, factor, sems.at[0]),
         pltpu.make_async_copy(src_in, src, sems.at[1]),
@@ -232,38 +232,30 @@
     return first + second
 
 
-def mix(left, kernel_t, scale, held, sems, outs, offsets, src_count):
+def mix(left, kernel_t, scale, outs, offsets, src_count):
     places = halves(offsets)
-    copies = [pltpu.make_async_copy(kernel_t.at[at], held.at[k], sems.at[k]) for k, at in enumerate(places)]
-    for copy in copies:
-        copy.start()
-    factor = left()
-    for copy in copies:
-        copy.wait()
     for k in range(0, len(places), 2):
-        x = jnp.dot(factor, slabs(held, k, 2), preferred_element_type=F32)
+        pair = jnp.concatenate([kernel_t[places[k]], kernel_t[places[k + 1]]], axis=1)
+        x = jnp.dot(left, pair, preferred_element_type=F32)
         for i in range(2):
             out = outs[(k + i) // 8]
             out[(k + i) % 8] = x[:, i * 128 : (i + 1) * 128] * (scale[pl.ds(places[k + i], 1), :] * src_count)
 
 
 def target_send(
-    parts, weight, before, tgt_t, kernel_t, scale, out_a, out_b, left, potential, gain, held, sems, *, src_count, tgt_count
+    parts, weight, before, tgt_t, kernel_t, scale, out_a, out_b, left, potential, gain, *, src_count, tgt_count
 ):
-    def factor():
-        total = jnp.sum(parts[...], axis=0)
-        g = 1.0 / (tgt_count * total)
-        gain[...] = g
-        potential[...] = before[...] - math.log(tgt_count) - jnp.log(total)
-        value = (tgt_t[...].astype(F32) * flat(weight[...] * g)).astype(BF16)
-        left[...] = value
-        return value
-
-    mix(factor, kernel_t, scale, held, sems, (out_a, out_b), (1, 2), src_count)
-
-
-def target_keep(left, kernel_t, scale, out_a, out_b, held, sems, *, src_count):
-    mix(lambda: left[...], kernel_t, scale, held, sems, (out_a, out_b), (0, 3), src_count)
+    total = jnp.sum(parts[...], axis=0)
+    g = 1.0 / (tgt_count * total)
+    gain[...] = g
+    potential[...] = before[...] - math.log(tgt_count) - jnp.log(total)
+    value = (tgt_t[...].astype(F32) * flat(weight[...] * g)).astype(BF16)
+    left[...] = value
+    mix(value, kernel_t, scale, (out_a, out_b), (1, 2), src_count)
+
+
+def target_keep(left, kernel_t, scale, out_a, out_b, *, src_count):
+    mix(left[...], kernel_t, scale, (out_a, out_b), (0, 3), src_count)
 
 
 def finish_sources(mine, other, gain, tgt, moment, out, *, tgt_count):
@@ -352,7 +344,6 @@
     counts = dict(src_count=src_count, tgt_count=tgt_count)
     share = rows // col_size
     row_shape, col_shape = (rows // 128, 128), (cols // 128, 128)
-    start = col_start.reshape(col_shape)
 
     def swap(x):
         return lax.ppermute(x, "row", [(i, i ^ 1) for i in range(row_size)])
@@ -369,14 +360,13 @@
     def exchange(x, axis):
         return lax.all_to_all(x, axis, 0, 0)
 
-    lse, proj_t, aug = call(
+    lse, proj_t, aug, start = call(
         first_rows,
-        [f32(col_size, *row_shape), bf16(width, rows), bf16(cols, 2 * width)],
-        far(src_emb), far(tgt_emb), far(cost_factor), far(start),
+        [f32(col_size, *row_shape), bf16(width, rows), bf16(cols, 2 * width), f32(*col_shape)],
+        far(src_emb), far(tgt_emb), far(cost_factor), far(col_start.reshape(col_shape)),
         scratch=[
             pltpu.VMEM((rows, width), BF16),
             pltpu.VMEM((width, width), BF16),
-            pltpu.VMEM(col_shape, F32),
             pltpu.SemaphoreType.DMA((4,)),
         ],
         spaces={i: pltpu.HBM for i in range(4)},
@@ -407,26 +397,22 @@
     mine = keep + swap(send)
     sums, mine = lax.optimization_barrier((sums, mine))
     parts = exchange(sums, "row")
-    mine = mine + along_y(mine, 1)
-    parts, mine = lax.optimization_barrier((parts, mine))
-    arrived = along_y(mine, 3)
-    held = [pltpu.VMEM((16, cols, 128), BF16), pltpu.SemaphoreType.DMA((16,))]
+    arrived = along_y(mine, 1)
     message = f32(8, width, 128)
     send_a, send_b, left, col_potential, gain = call(
         functools.partial(target_send, **counts),
         [message, message, bf16(width, cols), f32(*col_shape), f32(*col_shape)],
-        parts, weight, before, tgt_t, far(kernel_t), scale,
-        scratch=held, spaces={4: pltpu.HBM},
+        parts, weight, before, tgt_t, near(kernel_t), scale,
     )
     got_a, got_b = along_z(send_a, 1), along_x(send_b, 1)
     keep_a, keep_b = call(
         functools.partial(target_keep, src_count=src_count),
         [message, message],
-        left, far(kernel_t), scale,
-        scratch=held, spaces={1: pltpu.HBM},
-    )
-    mine, gain = lax.optimization_barrier((mine, gain))
+        left, near(kernel_t), scale,
+    )
+    mine, keep_a = lax.optimization_barrier((mine, keep_a))
     mine = mine + arrived
+    mine = mine + along_y(mine, 3)
     moment, bary_tgt = call(
         functools.partial(finish_sources, tgt_count=tgt_count),
         [f32(width, width), bf16(cols, width)],

time: 111 us -> 109 us (0.982)
  blocking collectives: 21.3 us -> 30.1 us
  Pallas kernels: 23.3 us -> 18.8 us
  starting transfers between devices: 22.6 us -> 19.3 us
  waiting for transfers between devices: 39.3 us -> 37 us
    all_to_all x2 -> x3, blocking collectives: 21.3 us -> 30.1 us  [exchange(): return lax.all_to_all(x, axis, 0, 0)]
    pallas_call x12, Pallas kernels: 23.3 us -> 18.8 us  [call(): pl.pallas_call(body, out_shape=outs, in_specs=[pl.BlockSpec(memory_space=...]
    all_to_all x2 -> x1, starting transfers between devices: 11.3 us -> 7.99 us  [exchange(): return lax.all_to_all(x, axis, 0, 0)]
    ppermute x5, waiting for transfers between devices: 15.2 us -> 13.4 us  [along_z(): return lax.ppermute(x, 'col', [(i, i ^ 4 * k) for i in range(col_size)])]
    ppermute x2, waiting for transfers between devices: 1.54 us -> 3.05 us  [swap(): return lax.ppermute(x, 'row', [(i, i ^ 1) for i in range(row_size)])]
    ppermute x2, waiting for transfers between devices: 7.7 us -> 6.57 us  [along_y(): return lax.ppermute(x, 'row', [(i, i ^ 2 * k) for i in range(row_size)])]
    all_to_all x2 -> x1, waiting for transfers between devices: 6.81 us -> 6 us  [exchange(): return lax.all_to_all(x, axis, 0, 0)]
    unnamed x10 -> x6, local copies, waits for them, and re-layouts: 2.86 us -> 2.17 us
  transfers between devices with their start and end apart: 16 -> 15, of which waited for: 14 -> 12; matrix products, arithmetic and copies ran while one was open for 0% -> 0% of each run, Pallas kernels for 7% -> 3%
where the time goes in v3:
time: 109 us
  waiting for transfers between devices  37 us (34%)
  blocking collectives  30.1 us (28%)
  starting transfers between devices  19.3 us (18%)
  Pallas kernels  18.8 us (17%)
  local copies, waits for them, and re-layouts  2.17 us (2%)
    all_to_all x3, blocking collectives, exchange(): return lax.all_to_all(x, axis, 0, 0)  30.1 us
    pallas_call x12, Pallas kernels, call(): pl.pallas_call(body, out_shape=outs, in_specs=[pl.BlockSpec(memory_space=...  18.8 us
    ppermute x5, waiting for transfers between devices, along_z(): return lax.ppermute(x, 'col', [(i, i ^ 4 * k) for i in range(col_size)])  13.4 us
    all_to_all x1, starting transfers between devices, exchange(): return lax.all_to_all(x, axis, 0, 0)  7.99 us
    ppermute x5, waiting for transfers between devices, along_x(): return lax.ppermute(x, 'col', [(i, i ^ k) for i in range(col_size)])  7.97 us
    ppermute x2, waiting for transfers between devices, along_y(): return lax.ppermute(x, 'row', [(i, i ^ 2 * k) for i in range(row_size)])  6.57 us
    all_to_all x1, waiting for transfers between devices, exchange(): return lax.all_to_all(x, axis, 0, 0)  6 us
    ppermute x5, starting transfers between devices, along_z(): return lax.ppermute(x, 'col', [(i, i ^ 4 * k) for i in range(col_size)])  4.35 us
  transfers between devices with their start and end apart: 15, of which 12 were waited for; matrix products, arithmetic and copies ran while one was open for 0% of the time, Pallas kernels for 3%

profile of v3, /device:TPU:0, one launch (start us, length us, event | category | flops | bytes accessed | tf_op | source)
XLA Modules:
  0.0 108.7 jit_solution(14746600537542052435)
XLA Ops:
  0.6 6.6 %shard_map.83 = (f32[16,32,128]{2,1,0:T(8,128)}, bf16[128,4096]{1,0:T(8,128)(2,1)S(1)}, bf16[1024,256]{1,0:T(8,128)(2,1)S(1)}, f32[8,128]{1,0:T(8,128)S(1)}) custom-call(bf16[4096,128]{1,0:T(8,128)(2,1)} %src, bf16[1024,128]{1,0:T(8,128)(2,1)} %tgt.2, bf16[128,128]{1,0:T(8,128)(2,1)} %factor_in.1, f32[8,128]{1,0:T(8,128)} %bitcast.3), custom_call_target="tpu_custom_call" | custom-call | tf_op jit(solution)/shard_map/pallas_call | solution.py:313
  7.3 8.0 %all-to-all-start = ((f32[16,32,128]{2,1,0:T(8,128)}), f32[16,32,128]{2,1,0:T(8,128)S(1)}, u32[]{:S(2)}, u32[]{:S(2)}) async-start(f32[16,32,128]{2,1,0:T(8,128)} %get-tuple-element.56), calls=%async_computation | async-start | bytes 524288 | tf_op jit(solution)/shard_map/all_to_all | solution.py:361
  15.3 1.2 %copy-done = bf16[4096,128]{1,0:T(8,128)(2,1)S(1)} copy-done((bf16[4096,128]{1,0:T(8,128)(2,1)S(1)}, bf16[4096,128]{1,0:T(8,128)(2,1)}, u32[]{:S(2)}) %copy-start) | copy-done | bytes 1048600
  16.5 0.9 copy-done.1
  17.9 6.0 %all-to-all-done.parts = f32[16,32,128]{2,1,0:T(8,128)S(1)} async-done(((f32[16,32,128]{2,1,0:T(8,128)}), f32[16,32,128]{2,1,0:T(8,128)S(1)}, u32[]{:S(2)}, u32[]{:S(2)}) %all-to-all-start) | async-done | bytes 262176 | tf_op jit(solution)/shard_map/all_to_all | solution.py:361
  23.9 2.9 %shard_map.85 = (bf16[32,1024,128]{2,1,0:T(8,128)(2,1)S(1)}, f32[8,8,128]{2,1,0:T(8,128)S(1)}, f32[8,128]{1,0:T(8,128)S(1)}, f32[32,128]{1,0:T(8,128)S(1)}) custom-call(f32[16,32,128]{2,1,0:T(8,128)S(1)} %all-to-all-done.parts, bf16[128,4096]{1,0:T(8,128)(2,1)S(1)} %get-tuple-element.57.proj_t, bf16[1024,256]{1,0:T(8,128)(2,1)S(1)} %get-tuple-element.63.aug, ...), custom_call_target="tpu_custom_call" | custom-call | tf_op jit(solution)/shard_map/pallas_call | solution.py:313
  26.8 9.7 %all_to_all.20.parts = f32[8,8,128]{2,1,0:T(8,128)S(1)} all-to-all(f32[8,8,128]{2,1,0:T(8,128)S(1)} %get-tuple-element.65), channel_id=1, replica_groups=mesh['row'=8,'col'=16] {'row'}, dimensions={0} | all-to-all | bytes 65536 | tf_op jit(solution)/shard_map/all_to_all | solution.py:361
  36.5 1.2 %shard_map.86 = (f32[16,32,128]{2,1,0:T(8,128)S(1)}, f32[8,128]{1,0:T(8,128)S(1)}, f32[8,128]{1,0:T(8,128)S(1)}) custom-call(f32[8,8,128]{2,1,0:T(8,128)S(1)} %all_to_all.20.parts, f32[8,128]{1,0:T(8,128)S(1)} %get-tuple-element.66.shift, bf16[32,1024,128]{2,1,0:T(8,128)(2,1)S(1)} %get-tuple-element.67.kernel_t), custom_call_target="tpu_custom_call" | custom-call | tf_op jit(solution)/shard_map/pallas_call | solution.py:313
  37.8 11.6 %all_to_all.21.parts = f32[16,32,128]{2,1,0:T(8,128)S(1)} all-to-all(f32[16,32,128]{2,1,0:T(8,128)S(1)} %get-tuple-element.68), channel_id=1, replica_groups=mesh['row'=8,'col'=16] {'col'}, dimensions={0} | all-to-all | bytes 524288 | tf_op jit(solution)/shard_map/all_to_all | solution.py:361
  49.4 3.4 %shard_map.87 = (f32[8,8,128]{2,1,0:T(8,128)S(1)}, f32[64,1024]{1,0:T(8,128)S(1)}, f32[64,1024]{1,0:T(8,128)S(1)}, f32[32,128]{1,0:T(8,128)S(1)}, f32[32,128]{1,0:T(8,128)}) custom-call(f32[16,32,128]{2,1,0:T(8,128)S(1)} %all_to_all.21.parts, f32[32,128]{1,0:T(8,128)S(1)} %get-tuple-element.69.rho, bf16[32,1024,128]{2,1,0:T(8,128)(2,1)S(1)} %get-tuple-element.67.kernel_t, ...), custom_call_target="tpu_custom_call" | custom-call | tf_op jit(solution)/shard_map/pallas_call | solution.py:313
  52.8 1.5 %collective-permute-done = f32[64,1024]{1,0:T(8,128)S(1)} collective-permute-done((f32[64,1024]{1,0:T(8,128)S(1)}, f32[64,1024]{1,0:T(8,128)S(1)}, u32[]{:S(2)}, u32[]{:S(2)}) %collective-permute-start) | collective-permute-done | bytes 262176 | tf_op jit(solution)/shard_map/ppermute | solution.py:349
  55.0 8.7 %all_to_all.22.parts = f32[8,8,128]{2,1,0:T(8,128)S(1)} all-to-all(f32[8,8,128]{2,1,0:T(8,128)S(1)} %get-tuple-element.76), channel_id=1, replica_groups=mesh['row'=8,'col'=16] {'row'}, dimensions={0} | all-to-all | bytes 65536 | tf_op jit(solution)/shard_map/all_to_all | solution.py:361
  63.7 1.2 %shard_map.88 = (f32[8,128,128]{2,1,0:T(8,128)S(1)}, f32[8,128,128]{2,1,0:T(8,128)S(1)}, bf16[128,1024]{1,0:T(8,128)(2,1)S(1)}, f32[8,128]{1,0:T(8,128)}, f32[8,128]{1,0:T(8,128)S(1)}) custom-call(f32[8,8,128]{2,1,0:T(8,128)S(1)} %all_to_all.22.parts, f32[8,128]{1,0:T(8,128)S(1)} %get-tuple-element.71.weight, f32[8,128]{1,0:T(8,128)S(1)} %get-tuple-element.77.before, ...), custom_call_target="tpu_custom_call" | custom-call | tf_op jit(solution)/shard_map/pallas_call | solution.py:313
  64.9 0.7 shard_map.89
  65.7 2.1 %collective-permute-start.4 = (f32[64,1024]{1,0:T(8,128)S(1)}, f32[64,1024]{1,0:T(8,128)S(1)}, u32[]{:S(2)}, u32[]{:S(2)}) collective-permute-start(f32[64,1024]{1,0:T(8,128)S(1)} %add.16), channel_id=1, source_target_pairs={{0,96},{16,112},{32,64},{48,80},{64,32},{80,48},{96,0},{112,16},{1... | collective-permute-start | bytes 786440 | tf_op jit(solution)/shard_map/ppermute | solution.py:352
  68.4 6.6 %collective-permute-done.4 = f32[64,1024]{1,0:T(8,128)S(1)} collective-permute-done((f32[64,1024]{1,0:T(8,128)S(1)}, f32[64,1024]{1,0:T(8,128)S(1)}, u32[]{:S(2)}, u32[]{:S(2)}) %collective-permute-start.4) | collective-permute-done | bytes 262176 | tf_op jit(solution)/shard_map/ppermute | solution.py:352
  75.1 1.5 %collective-permute-done.5.other = f32[64,1024]{1,0:T(8,128)S(1)} collective-permute-done((f32[64,1024]{1,0:T(8,128)S(1)}, f32[64,1024]{1,0:T(8,128)S(1)}, u32[]{:S(2)}, u32[]{:S(2)}) %collective-permute-start.5) | collective-permute-done | bytes 262176 | tf_op jit(solution)/shard_map/ppermute | solution.py:349
  76.7 1.3 %shard_map.90 = (f32[128,128]{1,0:T(8,128)S(1)}, bf16[1024,128]{1,0:T(8,128)(2,1)}) custom-call(f32[64,1024]{1,0:T(8,128)S(1)} %add.17.mine, f32[64,1024]{1,0:T(8,128)S(1)} %collective-permute-done.5.other, f32[8,128]{1,0:T(8,128)S(1)} %get-tuple-element.87.gain, bf16[1024,128]{1,0:T(8,128)(2,1)S(1)} %copy-done.2), custom_call_target="tpu_custom_call" | custom-call | tf_op jit(solution)/shard_map/pallas_call | solution.py:313
  77.9 3.3 %collective-permute-done.1.got_a = f32[8,128,128]{2,1,0:T(8,128)S(1)} collective-permute-done((f32[8,128,128]{2,1,0:T(8,128)S(1)}, f32[8,128,128]{2,1,0:T(8,128)S(1)}, u32[]{:S(2)}, u32[]{:S(2)}) %collective-permute-start.1) | collective-permute-done | bytes 524320 | tf_op jit(solution)/shard_map/ppermute | solution.py:355
  81.3 1.4 %collective-permute-start.6 = (f32[576,128]{1,0:T(8,128)S(1)}, f32[576,128]{1,0:T(8,128)S(1)}, u32[]{:S(2)}, u32[]{:S(2)}) collective-permute-start(f32[576,128]{1,0:T(8,128)S(1)} %get-tuple-element.90.sent_a), channel_id=1, source_target_pairs={{0,12},{1,13},{2,14},{3,15},{4,8},{5,9},{6,10},{7,11},{8,4},{9,5},... | collective-permute-start | bytes 884744 | tf_op jit(solution)/shard_map/ppermute | solution.py:355
  82.7 1.1 %collective-permute-start.7 = (f32[576,128]{1,0:T(8,128)S(1)}, f32[576,128]{1,0:T(8,128)S(1)}, u32[]{:S(2)}, u32[]{:S(2)}) collective-permute-start(f32[576,128]{1,0:T(8,128)S(1)} %get-tuple-element.92.sent_b), channel_id=1, source_target_pairs={{0,3},{1,2},{2,1},{3,0},{4,7},{5,6},{6,5},{7,4},{8,11},{9,10},{10,... | collective-permute-start | bytes 884744 | tf_op jit(solution)/shard_map/ppermute | solution.py:358
  83.8 6.3 %collective-permute-done.6.got_a = f32[576,128]{1,0:T(8,128)S(1)} collective-permute-done((f32[576,128]{1,0:T(8,128)S(1)}, f32[576,128]{1,0:T(8,128)S(1)}, u32[]{:S(2)}, u32[]{:S(2)}) %collective-permute-start.6) | collective-permute-done | bytes 294944 | tf_op jit(solution)/shard_map/ppermute | solution.py:355
  90.1 0.7 collective-permute-done.7.got_b
  91.0 0.9 collective-permute-start.9
  91.9 4.4 %collective-permute-done.8.got_a = f32[320,128]{1,0:T(8,128)S(1)} collective-permute-done((f32[320,128]{1,0:T(8,128)S(1)}, f32[320,128]{1,0:T(8,128)S(1)}, u32[]{:S(2)}, u32[]{:S(2)}) %collective-permute-start.8) | collective-permute-done | bytes 163872 | tf_op jit(solution)/shard_map/ppermute | solution.py:358
  96.4 1.2 %collective-permute-start.10 = (f32[192,128]{1,0:T(8,128)S(1)}, f32[192,128]{1,0:T(8,128)S(1)}, u32[]{:S(2)}, u32[]{:S(2)}) collective-permute-start(f32[192,128]{1,0:T(8,128)S(1)} %get-tuple-element.98.sent_a), channel_id=1, source_target_pairs={{0,3},{1,2},{2,1},{3,0},{4,7},{5,6},{6,5},{7,4},{8,11},{9,10},{10,... | collective-permute-start | bytes 294920 | tf_op jit(solution)/shard_map/ppermute | solution.py:358
  97.6 1.9 %collective-permute-start.11 = (f32[192,128]{1,0:T(8,128)S(1)}, f32[192,128]{1,0:T(8,128)S(1)}, u32[]{:S(2)}, u32[]{:S(2)}) collective-permute-start(f32[192,128]{1,0:T(8,128)S(1)} %get-tuple-element.100.sent_b), channel_id=1, source_target_pairs={{0,12},{1,13},{2,14},{3,15},{4,8},{5,9},{6,10},{7,11},{8,4},{9,5},... | collective-permute-start | bytes 294920 | tf_op jit(solution)/shard_map/ppermute | solution.py:355
  99.5 2.8 %collective-permute-done.10.got_a = f32[192,128]{1,0:T(8,128)S(1)} collective-permute-done((f32[192,128]{1,0:T(8,128)S(1)}, f32[192,128]{1,0:T(8,128)S(1)}, u32[]{:S(2)}, u32[]{:S(2)}) %collective-permute-start.10) | collective-permute-done | bytes 98336 | tf_op jit(solution)/shard_map/ppermute | solution.py:358
  102.3 1.1 %collective-permute-done.11.got_b = f32[192,128]{1,0:T(8,128)S(1)} collective-permute-done((f32[192,128]{1,0:T(8,128)S(1)}, f32[192,128]{1,0:T(8,128)S(1)}, u32[]{:S(2)}, u32[]{:S(2)}) %collective-permute-start.11) | collective-permute-done | bytes 98336 | tf_op jit(solution)/shard_map/ppermute | solution.py:355
  103.4 0.7 shard_map.94
  104.2 1.3 %collective-permute-start.13 = (f32[64,128]{1,0:T(8,128)S(1)}, f32[64,128]{1,0:T(8,128)S(1)}, u32[]{:S(2)}, u32[]{:S(2)}) collective-permute-start(f32[64,128]{1,0:T(8,128)S(1)} %get-tuple-element.104), channel_id=1, source_target_pairs={{0,1},{1,0},{2,3},{3,2},{4,5},{5,4},{6,7},{7,6},{8,9},{9,8},{10,11... | collective-permute-start | bytes 98312 | tf_op jit(solution)/shard_map/ppermute | solution.py:358
  105.5 2.6 %collective-permute-done.12 = f32[64,128]{1,0:T(8,128)S(1)} collective-permute-done((f32[64,128]{1,0:T(8,128)S(1)}, f32[64,128]{1,0:T(8,128)S(1)}, u32[]{:S(2)}, u32[]{:S(2)}) %collective-permute-start.12) | collective-permute-done | bytes 32800 | tf_op jit(solution)/shard_map/ppermute | solution.py:355
  (25 shorter events, 2.9 us)
Async XLA Ops:
  7.3 16.7 %all-to-all-start = ((f32[16,32,128]{2,1,0:T(8,128)}), f32[16,32,128]{2,1,0:T(8,128)S(1)}, u32[]{:S(2)}, u32[]{:S(2)}) async-start(f32[16,32,128]{2,1,0:T(8,128)} %get-tuple-element.56), calls=%async_computation | async-start | bytes 524288 | tf_op jit(solution)/shard_map/all_to_all | solution.py:361
  15.3 1.2 %copy-start = (bf16[4096,128]{1,0:T(8,128)(2,1)S(1)}, bf16[4096,128]{1,0:T(8,128)(2,1)}, u32[]{:S(2)}) copy-start(bf16[4096,128]{1,0:T(8,128)(2,1)} %src) | copy-start | bytes 3145732
  16.5 0.9 copy-start.1
  52.8 1.5 %collective-permute-start = (f32[64,1024]{1,0:T(8,128)S(1)}, f32[64,1024]{1,0:T(8,128)S(1)}, u32[]{:S(2)}, u32[]{:S(2)}) collective-permute-start(f32[64,1024]{1,0:T(8,128)S(1)} %get-tuple-element.74), channel_id=1, source_target_pairs={{0,16},{16,0},{32,48},{48,32},{64,80},{80,64},{96,112},{112,96},{1... | collective-permute-start | bytes 786440 | tf_op jit(solution)/shard_map/ppermute | solution.py:349
  54.3 11.3 %collective-permute-start.3 = (f32[64,1024]{1,0:T(8,128)S(1)}, f32[64,1024]{1,0:T(8,128)S(1)}, u32[]{:S(2)}, u32[]{:S(2)}) collective-permute-start(f32[64,1024]{1,0:T(8,128)S(1)} %add.15), channel_id=1, source_target_pairs={{0,32},{16,48},{32,0},{48,16},{64,96},{80,112},{96,64},{112,80},{1... | collective-permute-start | bytes 786440 | tf_op jit(solution)/shard_map/ppermute | solution.py:352
  63.7 12.9 %copy-start.2 = (bf16[1024,128]{1,0:T(8,128)(2,1)S(1)}, bf16[1024,128]{1,0:T(8,128)(2,1)}, u32[]{:S(2)}) copy-start(bf16[1024,128]{1,0:T(8,128)(2,1)} %tgt.2) | copy-start | bytes 786436
  65.7 9.3 %collective-permute-start.4 = (f32[64,1024]{1,0:T(8,128)S(1)}, f32[64,1024]{1,0:T(8,128)S(1)}, u32[]{:S(2)}, u32[]{:S(2)}) collective-permute-start(f32[64,1024]{1,0:T(8,128)S(1)} %add.16), channel_id=1, source_target_pairs={{0,96},{16,112},{32,64},{48,80},{64,32},{80,48},{96,0},{112,16},{1... | collective-permute-start | bytes 786440 | tf_op jit(solution)/shard_map/ppermute | solution.py:352
  67.9 13.3 %collective-permute-start.1 = (f32[8,128,128]{2,1,0:T(8,128)S(1)}, f32[8,128,128]{2,1,0:T(8,128)S(1)}, u32[]{:S(2)}, u32[]{:S(2)}) collective-permute-start(f32[8,128,128]{2,1,0:T(8,128)S(1)} %get-tuple-element.83), channel_id=1, source_target_pairs={{0,4},{1,5},{2,6},{3,7},{4,0},{5,1},{6,2},{7,3},{8,12},{9,13},{10,... | collective-permute-start | bytes 1572872 | tf_op jit(solution)/shard_map/ppermute | solution.py:355
  68.1 13.1 %collective-permute-start.2 = (f32[8,128,128]{2,1,0:T(8,128)S(1)}, f32[8,128,128]{2,1,0:T(8,128)S(1)}, u32[]{:S(2)}, u32[]{:S(2)}) collective-permute-start(f32[8,128,128]{2,1,0:T(8,128)S(1)} %get-tuple-element.85), channel_id=1, source_target_pairs={{0,1},{1,0},{2,3},{3,2},{4,5},{5,4},{6,7},{7,6},{8,9},{9,8},{10,11... | collective-permute-start | bytes 1572872 | tf_op jit(solution)/shard_map/ppermute | solution.py:358
  75.0 1.6 %collective-permute-start.5 = (f32[64,1024]{1,0:T(8,128)S(1)}, f32[64,1024]{1,0:T(8,128)S(1)}, u32[]{:S(2)}, u32[]{:S(2)}) collective-permute-start(f32[64,1024]{1,0:T(8,128)S(1)} %add.17.mine), channel_id=1, source_target_pairs={{0,16},{16,0},{32,48},{48,32},{64,80},{80,64},{96,112},{112,96},{1... | collective-permute-start | bytes 786440 | tf_op jit(solution)/shard_map/ppermute | solution.py:349
  81.3 8.8 %collective-permute-start.6 = (f32[576,128]{1,0:T(8,128)S(1)}, f32[576,128]{1,0:T(8,128)S(1)}, u32[]{:S(2)}, u32[]{:S(2)}) collective-permute-start(f32[576,128]{1,0:T(8,128)S(1)} %get-tuple-element.90.sent_a), channel_id=1, source_target_pairs={{0,12},{1,13},{2,14},{3,15},{4,8},{5,9},{6,10},{7,11},{8,4},{9,5},... | collective-permute-start | bytes 884744 | tf_op jit(solution)/shard_map/ppermute | solution.py:355
  82.7 8.1 %collective-permute-start.7 = (f32[576,128]{1,0:T(8,128)S(1)}, f32[576,128]{1,0:T(8,128)S(1)}, u32[]{:S(2)}, u32[]{:S(2)}) collective-permute-start(f32[576,128]{1,0:T(8,128)S(1)} %get-tuple-element.92.sent_b), channel_id=1, source_target_pairs={{0,3},{1,2},{2,1},{3,0},{4,7},{5,6},{6,5},{7,4},{8,11},{9,10},{10,... | collective-permute-start | bytes 884744 | tf_op jit(solution)/shard_map/ppermute | solution.py:358
  90.9 5.4 %collective-permute-start.8 = (f32[320,128]{1,0:T(8,128)S(1)}, f32[320,128]{1,0:T(8,128)S(1)}, u32[]{:S(2)}, u32[]{:S(2)}) collective-permute-start(f32[320,128]{1,0:T(8,128)S(1)} %get-tuple-element.94.sent_a), channel_id=1, source_target_pairs={{0,1},{1,0},{2,3},{3,2},{4,5},{5,4},{6,7},{7,6},{8,9},{9,8},{10,11... | collective-permute-start | bytes 491528 | tf_op jit(solution)/shard_map/ppermute | solution.py:358
  91.0 5.4 %collective-permute-start.9 = (f32[320,128]{1,0:T(8,128)S(1)}, f32[320,128]{1,0:T(8,128)S(1)}, u32[]{:S(2)}, u32[]{:S(2)}) collective-permute-start(f32[320,128]{1,0:T(8,128)S(1)} %get-tuple-element.96.sent_b), channel_id=1, source_target_pairs={{0,4},{1,5},{2,6},{3,7},{4,0},{5,1},{6,2},{7,3},{8,12},{9,13},{10,... | collective-permute-start | bytes 491528 | tf_op jit(solution)/shard_map/ppermute | solution.py:355
  96.4 5.9 %collective-permute-start.10 = (f32[192,128]{1,0:T(8,128)S(1)}, f32[192,128]{1,0:T(8,128)S(1)}, u32[]{:S(2)}, u32[]{:S(2)}) collective-permute-start(f32[192,128]{1,0:T(8,128)S(1)} %get-tuple-element.98.sent_a), channel_id=1, source_target_pairs={{0,3},{1,2},{2,1},{3,0},{4,7},{5,6},{6,5},{7,4},{8,11},{9,10},{10,... | collective-permute-start | bytes 294920 | tf_op jit(solution)/shard_map/ppermute | solution.py:358
  97.6 5.8 %collective-permute-start.11 = (f32[192,128]{1,0:T(8,128)S(1)}, f32[192,128]{1,0:T(8,128)S(1)}, u32[]{:S(2)}, u32[]{:S(2)}) collective-permute-start(f32[192,128]{1,0:T(8,128)S(1)} %get-tuple-element.100.sent_b), channel_id=1, source_target_pairs={{0,12},{1,13},{2,14},{3,15},{4,8},{5,9},{6,10},{7,11},{8,4},{9,5},... | collective-permute-start | bytes 294920 | tf_op jit(solution)/shard_map/ppermute | solution.py:355
  104.2 3.9 %collective-permute-start.12 = (f32[64,128]{1,0:T(8,128)S(1)}, f32[64,128]{1,0:T(8,128)S(1)}, u32[]{:S(2)}, u32[]{:S(2)}) collective-permute-start(f32[64,128]{1,0:T(8,128)S(1)} %get-tuple-element.103), channel_id=1, source_target_pairs={{0,4},{1,5},{2,6},{3,7},{4,0},{5,1},{6,2},{7,3},{8,12},{9,13},{10,... | collective-permute-start | bytes 98312 | tf_op jit(solution)/shard_map/ppermute | solution.py:355
  104.2 3.9 %collective-permute-start.13 = (f32[64,128]{1,0:T(8,128)S(1)}, f32[64,128]{1,0:T(8,128)S(1)}, u32[]{:S(2)}, u32[]{:S(2)}) collective-permute-start(f32[64,128]{1,0:T(8,128)S(1)} %get-tuple-element.104), channel_id=1, source_target_pairs={{0,1},{1,0},{2,3},{3,2},{4,5},{5,4},{6,7},{7,6},{8,9},{9,8},{10,11... | collective-permute-start | bytes 98312 | tf_op jit(solution)/shard_map/ppermute | solution.py:358

commit v4 on v3

--- a/solution.py
+++ b/solution.py
@@ -221,25 +221,30 @@
     send[...] = total[pl.ds(pl.multiple_of(half - own, half), half), :] * w
 
 
+def on_first_core():
+    return lax.rem(lax.axis_index("row"), 2) == 0
+
+
 def share_of(major, minor):
+    first = on_first_core()
     col = lax.axis_index("col")
-    return ((col // 4) ^ major) * 4 + ((col % 4) ^ minor)
-
-
-def halves(offsets):
-    first = [2 * share_of(a, b) for a in offsets for b in range(4)]
-    second = [2 * share_of(b, a) + 1 for a in offsets for b in range(4)]
-    return first + second
+    z = (col // 4) ^ jnp.where(first, major, minor)
+    x = (col % 4) ^ jnp.where(first, minor, major)
+    return z * 4 + x
+
+
+SEND = ((1, 2), (3, 2))
+STAY = ((0, 3), (0, 1))
 
 
 def mix(left, kernel_t, scale, outs, offsets, src_count):
-    places = halves(offsets)
-    for k in range(0, len(places), 2):
-        pair = jnp.concatenate([kernel_t[places[k]], kernel_t[places[k + 1]]], axis=1)
+    for k in range(8):
+        at = [share_of(offsets[h][k // 4], k % 4) * 2 + h for h in range(2)]
+        pair = jnp.concatenate([kernel_t[i] for i in at], axis=1)
         x = jnp.dot(left, pair, preferred_element_type=F32)
-        for i in range(2):
-            out = outs[(k + i) // 8]
-            out[(k + i) % 8] = x[:, i * 128 : (i + 1) * 128] * (scale[pl.ds(places[k + i], 1), :] * src_count)
+        for h in range(2):
+            u = scale[pl.ds(at[h], 1), :] * src_count
+            outs[h][k * 128 : (k + 1) * 128, :] = x[:, h * 128 : (h + 1) * 128] * u
 
 
 def target_send(
@@ -251,61 +256,57 @@
     potential[...] = before[...] - math.log(tgt_count) - jnp.log(total)
     value = (tgt_t[...].astype(F32) * flat(weight[...] * g)).astype(BF16)
     left[...] = value
-    mix(value, kernel_t, scale, (out_a, out_b), (1, 2), src_count)
+    mix(value, kernel_t, scale, (out_a, out_b), SEND, src_count)
 
 
 def target_keep(left, kernel_t, scale, out_a, out_b, *, src_count):
-    mix(left[...], kernel_t, scale, (out_a, out_b), (0, 3), src_count)
-
-
-def finish_sources(mine, other, gain, tgt, moment, out, *, tgt_count):
-    even = lax.rem(lax.axis_index("row"), 2) == 0
-    low = jnp.where(even, mine[...], other[...])
-    high = jnp.where(even, other[...], mine[...])
-    full = jnp.concatenate([low, high], axis=0) * flat(gain[...])
-    moment[...] = jnp.dot(
-        full, tgt[...].astype(F32), precision=lax.Precision.HIGHEST, preferred_element_type=F32
-    )
-    out[...] = (full * tgt_count).T.astype(BF16)
-
-
-def merge_first(keep_a, got_a, keep_b, got_b, moment, send_a, hold_a, send_b, hold_b):
-    for i, (keep, got, send, hold) in enumerate(((keep_a, got_a, send_a, hold_a), (keep_b, got_b, send_b, hold_b))):
-        for k in range(4):
-            hold[k] = keep[k] + got[k]
-            send[k * 128 : (k + 1) * 128, :] = keep[4 + k] + got[4 + k]
-        send[512:576, :] = moment[i * 64 : (i + 1) * 64, :]
-
-
-def merge_second(hold_a, sent_a, got_a, hold_b, sent_b, got_b, send_a, next_a, send_b, next_b):
-    for hold, sent, got, send, after in (
-        (hold_a, sent_a, got_a, send_a, next_a),
-        (hold_b, sent_b, got_b, send_b, next_b),
+    mix(left[...], kernel_t, scale, (out_a, out_b), STAY, src_count)
+
+
+def moment_half(mine, gain, tgt, out):
+    out[...] = jnp.dot(
+        mine[...] * flat(gain[...]), tgt[...].astype(F32), precision=lax.Precision.HIGHEST, preferred_element_type=F32
+    )
+
+
+def in_order(mine, other):
+    first = on_first_core()
+    return jnp.concatenate([jnp.where(first, mine, other), jnp.where(first, other, mine)], axis=0)
+
+
+def finish_sources(mine, other, gain, out, *, tgt_count):
+    out[...] = (in_order(mine[...], other[...]) * (flat(gain[...]) * tgt_count)).T.astype(BF16)
+
+
+def merge_first(keep_a, got_a, keep_b, got_b, send_a, hold_a, send_b, hold_b):
+    for keep, got, send, hold in ((keep_a, got_a, send_a, hold_a), (keep_b, got_b, send_b, hold_b)):
+        hold[...] = keep[:512, :] + got[:512, :]
+        send[...] = keep[512:, :] + got[512:, :]
+
+
+def merge_second(hold_a, got_a, hold_b, got_b, send_a, next_a, send_b, next_b):
+    for half, (hold, got, send, after) in enumerate(
+        ((hold_a, got_a, send_a, next_a), (hold_b, got_b, send_b, next_b))
     ):
-        for k in range(4):
-            value = hold[k] + got[k * 128 : (k + 1) * 128, :]
-            if k in (1, 2):
-                send[(k - 1) * 128 : k * 128, :] = value
-            else:
-                after[k // 3] = value
-        send[256:320, :] = sent[512:576, :] + got[512:576, :]
-
-
-def merge_third(hold_a, sent_a, got_a, hold_b, sent_b, got_b, send_a, next_a, send_b, next_b):
-    for hold, sent, got, send, after in (
-        (hold_a, sent_a, got_a, send_a, next_a),
-        (hold_b, sent_b, got_b, send_b, next_b),
-    ):
-        after[...] = hold[0] + got[:128, :]
-        send[:128, :] = hold[1] + got[128:256, :]
-        send[128:192, :] = sent[256:320, :] + got[256:320, :]
-
-
-def merge_last(hold_a, sent_a, got_a, hold_b, sent_b, got_b, bary, moment_a, moment_b):
-    bary[:128, :] = (hold_a[...] + got_a[:128, :]).T.astype(BF16)
-    bary[128:, :] = (hold_b[...] + got_b[:128, :]).T.astype(BF16)
-    moment_a[...] = sent_a[128:192, :] + got_a[128:192, :]
-    moment_b[...] = sent_b[128:192, :] + got_b[128:192, :]
+        for out, offsets in ((send, SEND[half]), (after, STAY[half])):
+            for k, minor in enumerate(offsets):
+                rows = slice(minor * 128, (minor + 1) * 128)
+                out[k * 128 : (k + 1) * 128, :] = hold[rows, :] + got[rows, :]
+
+
+def merge_third(hold_a, got_a, hold_b, got_b, send_a, next_a, send_b, next_b):
+    for hold, got, send, after in ((hold_a, got_a, send_a, next_a), (hold_b, got_b, send_b, next_b)):
+        after[...] = hold[:128, :] + got[:128, :]
+        send[...] = hold[128:, :] + got[128:, :]
+
+
+def merge_last(hold_a, got_a, hold_b, got_b, bary):
+    bary[:128, :] = (hold_a[...] + got_a[...]).T.astype(BF16)
+    bary[128:, :] = (hold_b[...] + got_b[...]).T.astype(BF16)
+
+
+def finish_moment(mine, other, out):
+    out[...] = in_order(mine[...], other[...])
 
 
 def call(body, outs, *args, scratch=(), spaces=None):
@@ -316,6 +317,7 @@
         in_specs=[pl.BlockSpec(memory_space=spaces.get(i, pltpu.VMEM)) for i in range(len(args))],
         out_specs=jax.tree.map(lambda _: pl.BlockSpec(memory_space=pltpu.VMEM), outs),
         scratch_shapes=list(scratch),
+        cost_estimate=pl.CostEstimate(flops=1, bytes_accessed=1, transcendentals=0),
         compiler_params=pltpu.CompilerParams(vmem_limit_bytes=VMEM_LIMIT),
     )(*args)
 
@@ -348,14 +350,22 @@
     def swap(x):
         return lax.ppermute(x, "row", [(i, i ^ 1) for i in range(row_size)])
 
+    def by_core(x, step):
+        pairs = []
+        for i in range(row_size * col_size):
+            row, col = divmod(i, col_size)
+            y, z, w = step(row % 2, row // 2, col // 4, col % 4)
+            pairs.append((i, (y * 2 + row % 2) * col_size + z * 4 + w))
+        return lax.ppermute(x, ("row", "col"), pairs)
+
+    def major(x, k):
+        return by_core(x, lambda c, y, z, w: (y, z, w ^ k) if c else (y, z ^ k, w))
+
+    def minor(x, k):
+        return by_core(x, lambda c, y, z, w: (y, z ^ k, w) if c else (y, z, w ^ k))
+
     def along_y(x, k):
-        return lax.ppermute(x, "row", [(i, i ^ (2 * k)) for i in range(row_size)])
-
-    def along_z(x, k):
-        return lax.ppermute(x, "col", [(i, i ^ (4 * k)) for i in range(col_size)])
-
-    def along_x(x, k):
-        return lax.ppermute(x, "col", [(i, i ^ k) for i in range(col_size)])
+        return by_core(x, lambda c, y, z, w: (y ^ k ^ 2 * c, z, w))
 
     def exchange(x, axis):
         return lax.all_to_all(x, axis, 0, 0)
@@ -394,48 +404,45 @@
         parts, rho, near(kernel_t), src_t, weight,
         scratch=[pltpu.VMEM((width + 16, cols), F32)],
     )
-    mine = keep + swap(send)
-    sums, mine = lax.optimization_barrier((sums, mine))
     parts = exchange(sums, "row")
-    arrived = along_y(mine, 1)
-    message = f32(8, width, 128)
+    message = f32(8 * width, share // 2)
     send_a, send_b, left, col_potential, gain = call(
         functools.partial(target_send, **counts),
         [message, message, bf16(width, cols), f32(*col_shape), f32(*col_shape)],
         parts, weight, before, tgt_t, near(kernel_t), scale,
     )
-    got_a, got_b = along_z(send_a, 1), along_x(send_b, 1)
+    got_a, got_b = major(send_a, 1), major(send_b, 3)
     keep_a, keep_b = call(
-        functools.partial(target_keep, src_count=src_count),
-        [message, message],
-        left, near(kernel_t), scale,
-    )
-    mine, keep_a = lax.optimization_barrier((mine, keep_a))
-    mine = mine + arrived
+        functools.partial(target_keep, src_count=src_count), [message, message], left, near(kernel_t), scale
+    )
+    send, _ = lax.optimization_barrier((send, left))
+    mine = keep + swap(send)
+    mine = mine + along_y(mine, 1)
+    keep_a, mine = lax.optimization_barrier((keep_a, mine))
     mine = mine + along_y(mine, 3)
-    moment, bary_tgt = call(
-        functools.partial(finish_sources, tgt_count=tgt_count),
-        [f32(width, width), bf16(cols, width)],
-        mine, swap(mine), gain, tgt_emb,
-    )
-    send_a, hold_a, send_b, hold_b = call(
-        merge_first, [f32(576, 128), f32(4, 128, 128)] * 2, keep_a, got_a, keep_b, got_b, moment
-    )
-    got_a, got_b = along_z(send_a, 3), along_x(send_b, 3)
-    send_a, hold_a, send_b, hold_b = call(
-        merge_second, [f32(320, 128), f32(2, 128, 128)] * 2, hold_a, send_a, got_a, hold_b, send_b, got_b
-    )
-    got_a, got_b = along_x(send_a, 1), along_z(send_b, 1)
-    send_a, hold_a, send_b, hold_b = call(
-        merge_third, [f32(192, 128), f32(128, 128)] * 2, hold_a, send_a, got_a, hold_b, send_b, got_b
-    )
-    got_a, got_b = along_x(send_a, 3), along_z(send_b, 3)
-    bary_src, moment_a, moment_b = call(
-        merge_last,
-        [bf16(share, width), f32(64, 128), f32(64, 128)],
-        hold_a, send_a, got_a, hold_b, send_b, got_b,
-    )
-    moment = jnp.concatenate([moment_a + along_z(moment_a, 1), moment_b + along_x(moment_b, 1)], axis=0)
+    moment, = call(moment_half, [f32(width // 2, width)], mine, gain, tgt_emb)
+    bary_tgt, = call(
+        functools.partial(finish_sources, tgt_count=tgt_count), [bf16(cols, width)], mine, swap(mine), gain
+    )
+    send_a, hold_a, send_b, hold_b = call(merge_first, [f32(512, 128)] * 4, keep_a, got_a, keep_b, got_b)
+    got_a, got_b = major(send_a, 3), major(send_b, 1)
+    hold_a, moment = lax.optimization_barrier((hold_a, moment))
+    rest = major(moment, 1)
+    send_a, hold_a, send_b, hold_b = call(merge_second, [f32(256, 128)] * 4, hold_a, got_a, hold_b, got_b)
+    got_a, got_b = minor(send_a, 1), minor(send_b, 3)
+    hold_a, bary_tgt, moment = lax.optimization_barrier((hold_a, bary_tgt, moment))
+    moment = moment + rest
+    moment = moment + major(moment, 3)
+    hold_a, moment = lax.optimization_barrier((hold_a, moment))
+    rest = minor(moment, 1)
+    send_a, hold_a, send_b, hold_b = call(merge_third, [f32(128, 128)] * 4, hold_a, got_a, hold_b, got_b)
+    got_a, got_b = minor(send_a, 3), minor(send_b, 1)
+    hold_a, moment = lax.optimization_barrier((hold_a, moment))
+    moment = moment + rest
+    moment = moment + minor(moment, 3)
+    bary_src, = call(merge_last, [bf16(share, width)], hold_a, got_a, hold_b, got_b)
+    bary_src, moment = lax.optimization_barrier((bary_src, moment))
+    moment, = call(finish_moment, [f32(width, width)], moment, swap(moment))
     return (bary_src, bary_tgt, moment, row_potential.reshape(rows), col_potential.reshape(cols))
 
 

time: 109 us -> 104 us (0.954)
  waiting for transfers between devices: 37 us -> 29.6 us
  starting transfers between devices: 19.3 us -> 21.9 us
    ppermute x12 -> x14, waiting for transfers between devices: 27.9 us -> 22.3 us  [by_core(): return lax.ppermute(x, ('row', 'col'), pairs)]
    ppermute x12 -> x14, starting transfers between devices: 11.2 us -> 13.8 us  [by_core(): return lax.ppermute(x, ('row', 'col'), pairs)]
    ppermute x2 -> x3, waiting for transfers between devices: 3.05 us -> 1.21 us  [swap(): return lax.ppermute(x, 'row', [(i, i ^ 1) for i in range(row_size)])]
    pallas_call x12 -> x14, Pallas kernels: 18.8 us -> 19.4 us  [call(): pl.pallas_call(body, out_shape=outs, in_specs=[pl.BlockSpec(memory_space=...]
  transfers between devices with their start and end apart: 15 -> 18, of which waited for: 12 -> 11; matrix products, arithmetic and copies ran while one was open for 0% -> 0% of each run, Pallas kernels for 3% -> 3%
where the time goes in v4:
time: 104 us; the launch traced here: 103 us
  waiting for transfers between devices  29.6 us (28%)
  blocking collectives  29.1 us (28%)
  starting transfers between devices  21.9 us (21%)
  Pallas kernels  19.4 us (19%)
  local copies, waits for them, and re-layouts  2.17 us (2%)
    all_to_all x3, blocking collectives, exchange(): return lax.all_to_all(x, axis, 0, 0)  29.1 us
    ppermute x14, waiting for transfers between devices, by_core(): return lax.ppermute(x, ('row', 'col'), pairs)  22.3 us
    pallas_call x14, Pallas kernels, call(): pl.pallas_call(body, out_shape=outs, in_specs=[pl.BlockSpec(memory_space=...  19.4 us
    ppermute x14, starting transfers between devices, by_core(): return lax.ppermute(x, ('row', 'col'), pairs)  13.8 us
    all_to_all x1, starting transfers between devices, exchange(): return lax.all_to_all(x, axis, 0, 0)  7.99 us
    all_to_all x1, waiting for transfers between devices, exchange(): return lax.all_to_all(x, axis, 0, 0)  6 us
    unnamed x6, local copies, waits for them, and re-layouts  2.17 us
  transfers between devices with their start and end apart: 18, of which 11 were waited for; matrix products, arithmetic and copies ran while one was open for 0% of the time, Pallas kernels for 3%

profile of v4, /device:TPU:0, one launch (start us, length us, event | category | flops | bytes accessed | tf_op | source)
XLA Modules:
  0.0 103.0 jit_solution(8838122868779268254)
XLA Ops:
  0.6 6.6 %shard_map.83 = (f32[16,32,128]{2,1,0:T(8,128)}, bf16[128,4096]{1,0:T(8,128)(2,1)S(1)}, bf16[1024,256]{1,0:T(8,128)(2,1)S(1)}, f32[8,128]{1,0:T(8,128)S(1)}) custom-call(bf16[4096,128]{1,0:T(8,128)(2,1)} %src, bf16[1024,128]{1,0:T(8,128)(2,1)} %tgt.2, bf16[128,128]{1,0:T(8,128)(2,1)} %factor_in.1, f32[8,128]{1,0:T(8,128)} %bitcast.3), custom_call_target="tpu_custom_call" | custom-call | flops 1 | bytes 1 | tf_op jit(solution)/shard_map/pallas_call | solution.py:314
  7.3 8.0 %all-to-all-start = ((f32[16,32,128]{2,1,0:T(8,128)}), f32[16,32,128]{2,1,0:T(8,128)S(1)}, u32[]{:S(2)}, u32[]{:S(2)}) async-start(f32[16,32,128]{2,1,0:T(8,128)} %get-tuple-element.61), calls=%async_computation | async-start | bytes 524288 | tf_op jit(solution)/shard_map/all_to_all | solution.py:371
  15.3 1.2 %copy-done = bf16[4096,128]{1,0:T(8,128)(2,1)S(1)} copy-done((bf16[4096,128]{1,0:T(8,128)(2,1)S(1)}, bf16[4096,128]{1,0:T(8,128)(2,1)}, u32[]{:S(2)}) %copy-start) | copy-done | bytes 1048600
  16.5 0.9 copy-done.1
  17.9 6.0 %all-to-all-done.parts = f32[16,32,128]{2,1,0:T(8,128)S(1)} async-done(((f32[16,32,128]{2,1,0:T(8,128)}), f32[16,32,128]{2,1,0:T(8,128)S(1)}, u32[]{:S(2)}, u32[]{:S(2)}) %all-to-all-start) | async-done | bytes 262176 | tf_op jit(solution)/shard_map/all_to_all | solution.py:371
  23.9 2.9 %shard_map.85 = (bf16[32,1024,128]{2,1,0:T(8,128)(2,1)S(1)}, f32[8,8,128]{2,1,0:T(8,128)S(1)}, f32[8,128]{1,0:T(8,128)S(1)}, f32[32,128]{1,0:T(8,128)S(1)}) custom-call(f32[16,32,128]{2,1,0:T(8,128)S(1)} %all-to-all-done.parts, bf16[128,4096]{1,0:T(8,128)(2,1)S(1)} %get-tuple-element.62.proj_t, bf16[1024,256]{1,0:T(8,128)(2,1)S(1)} %get-tuple-element.68.aug, ...), custom_call_target="tpu_custom_call" | custom-call | flops 1 | bytes 1 | tf_op jit(solution)/shard_map/pallas_call | solution.py:314
  26.8 9.7 %all_to_all.20.parts = f32[8,8,128]{2,1,0:T(8,128)S(1)} all-to-all(f32[8,8,128]{2,1,0:T(8,128)S(1)} %get-tuple-element.70), channel_id=1, replica_groups=mesh['row'=8,'col'=16] {'row'}, dimensions={0} | all-to-all | bytes 65536 | tf_op jit(solution)/shard_map/all_to_all | solution.py:371
  36.5 1.2 %shard_map.86 = (f32[16,32,128]{2,1,0:T(8,128)S(1)}, f32[8,128]{1,0:T(8,128)S(1)}, f32[8,128]{1,0:T(8,128)S(1)}) custom-call(f32[8,8,128]{2,1,0:T(8,128)S(1)} %all_to_all.20.parts, f32[8,128]{1,0:T(8,128)S(1)} %get-tuple-element.71.shift, bf16[32,1024,128]{2,1,0:T(8,128)(2,1)S(1)} %get-tuple-element.72.kernel_t), custom_call_target="tpu_custom_call" | custom-call | flops 1 | bytes 1 | tf_op jit(solution)/shard_map/pallas_call | solution.py:314
  37.8 11.6 %all_to_all.21.parts = f32[16,32,128]{2,1,0:T(8,128)S(1)} all-to-all(f32[16,32,128]{2,1,0:T(8,128)S(1)} %get-tuple-element.73), channel_id=1, replica_groups=mesh['row'=8,'col'=16] {'col'}, dimensions={0} | all-to-all | bytes 524288 | tf_op jit(solution)/shard_map/all_to_all | solution.py:371
  49.4 3.4 %shard_map.87 = (f32[8,8,128]{2,1,0:T(8,128)S(1)}, f32[64,1024]{1,0:T(8,128)S(1)}, f32[64,1024]{1,0:T(8,128)S(1)}, f32[32,128]{1,0:T(8,128)S(1)}, f32[32,128]{1,0:T(8,128)}) custom-call(f32[16,32,128]{2,1,0:T(8,128)S(1)} %all_to_all.21.parts, f32[32,128]{1,0:T(8,128)S(1)} %get-tuple-element.74.rho, bf16[32,1024,128]{2,1,0:T(8,128)(2,1)S(1)} %get-tuple-element.72.kernel_t, ...), custom_call_target="tpu_custom_call" | custom-call | flops 1 | bytes 1 | tf_op jit(solution)/shard_map/pallas_call | solution.py:314
  52.8 7.8 %all_to_all.22.parts = f32[8,8,128]{2,1,0:T(8,128)S(1)} all-to-all(f32[8,8,128]{2,1,0:T(8,128)S(1)} %get-tuple-element.77), channel_id=1, replica_groups=mesh['row'=8,'col'=16] {'row'}, dimensions={0} | all-to-all | bytes 65536 | tf_op jit(solution)/shard_map/all_to_all | solution.py:371
  60.6 1.2 %shard_map.88 = (f32[1024,128]{1,0:T(8,128)S(1)}, f32[1024,128]{1,0:T(8,128)S(1)}, bf16[128,1024]{1,0:T(8,128)(2,1)S(1)}, f32[8,128]{1,0:T(8,128)}, f32[8,128]{1,0:T(8,128)S(1)}) custom-call(f32[8,8,128]{2,1,0:T(8,128)S(1)} %all_to_all.22.parts, f32[8,128]{1,0:T(8,128)S(1)} %get-tuple-element.76.weight, f32[8,128]{1,0:T(8,128)S(1)} %get-tuple-element.78.before, ...), custom_call_target="tpu_custom_call" | custom-call | flops 1 | bytes 1 | tf_op jit(solution)/shard_map/pallas_call | solution.py:314
  62.0 1.4 %collective-permute-start.3 = (f32[1024,128]{1,0:T(8,128)S(1)}, f32[1024,128]{1,0:T(8,128)S(1)}, u32[]{:S(2)}, u32[]{:S(2)}) collective-permute-start(f32[1024,128]{1,0:T(8,128)S(1)} %get-tuple-element.89), channel_id=1, source_target_pairs={{0,12},{1,13},{2,14},{3,15},{4,8},{5,9},{6,10},{7,11},{8,4},{9,5},... | collective-permute-start | bytes 1572872 | tf_op jit(solution)/shard_map/ppermute | solution.py:359
  63.4 0.6 collective-permute-start.1
  64.0 0.7 shard_map.89
  64.8 5.1 %collective-permute-done.1 = f32[64,1024]{1,0:T(8,128)S(1)} collective-permute-done((f32[64,1024]{1,0:T(8,128)S(1)}, f32[64,1024]{1,0:T(8,128)S(1)}, u32[]{:S(2)}, u32[]{:S(2)}) %collective-permute-start.1) | collective-permute-done | bytes 262176 | tf_op jit(solution)/shard_map/ppermute | solution.py:359
  69.9 1.2 %collective-permute-start.4 = (f32[64,1024]{1,0:T(8,128)S(1)}, f32[64,1024]{1,0:T(8,128)S(1)}, u32[]{:S(2)}, u32[]{:S(2)}) collective-permute-start(f32[64,1024]{1,0:T(8,128)S(1)} %add.22), channel_id=1, source_target_pairs={{0,96},{1,97},{2,98},{3,99},{4,100},{5,101},{6,102},{7,103},{8,104... | collective-permute-start | bytes 786440 | tf_op jit(solution)/shard_map/ppermute | solution.py:359
  71.1 1.3 %collective-permute-done.3.got_b = f32[1024,128]{1,0:T(8,128)S(1)} collective-permute-done((f32[1024,128]{1,0:T(8,128)S(1)}, f32[1024,128]{1,0:T(8,128)S(1)}, u32[]{:S(2)}, u32[]{:S(2)}) %collective-permute-start.3) | collective-permute-done | bytes 524320 | tf_op jit(solution)/shard_map/ppermute | solution.py:359
  72.5 1.4 %collective-permute-start.5 = (f32[512,128]{1,0:T(8,128)S(1)}, f32[512,128]{1,0:T(8,128)S(1)}, u32[]{:S(2)}, u32[]{:S(2)}) collective-permute-start(f32[512,128]{1,0:T(8,128)S(1)} %get-tuple-element.94), channel_id=1, source_target_pairs={{0,12},{1,13},{2,14},{3,15},{4,8},{5,9},{6,10},{7,11},{8,4},{9,5},... | collective-permute-start | bytes 786440 | tf_op jit(solution)/shard_map/ppermute | solution.py:359
  73.9 3.6 %collective-permute-done.4 = f32[64,1024]{1,0:T(8,128)S(1)} collective-permute-done((f32[64,1024]{1,0:T(8,128)S(1)}, f32[64,1024]{1,0:T(8,128)S(1)}, u32[]{:S(2)}, u32[]{:S(2)}) %collective-permute-start.4) | collective-permute-done | bytes 262176 | tf_op jit(solution)/shard_map/ppermute | solution.py:359
  78.1 2.1 %collective-permute-done.5.got_a = f32[512,128]{1,0:T(8,128)S(1)} collective-permute-done((f32[512,128]{1,0:T(8,128)S(1)}, f32[512,128]{1,0:T(8,128)S(1)}, u32[]{:S(2)}, u32[]{:S(2)}) %collective-permute-start.5) | collective-permute-done | bytes 262176 | tf_op jit(solution)/shard_map/ppermute | solution.py:359
  80.9 1.4 %collective-permute-start.11 = (f32[256,128]{1,0:T(8,128)S(1)}, f32[256,128]{1,0:T(8,128)S(1)}, u32[]{:S(2)}, u32[]{:S(2)}) collective-permute-start(f32[256,128]{1,0:T(8,128)S(1)} %get-tuple-element.104), channel_id=1, source_target_pairs={{0,3},{1,2},{2,1},{3,0},{4,7},{5,6},{6,5},{7,4},{8,11},{9,10},{10,... | collective-permute-start | bytes 393224 | tf_op jit(solution)/shard_map/ppermute | solution.py:359
  82.3 0.9 shard_map.93
  83.2 3.1 %collective-permute-done.8 = f32[64,128]{1,0:T(8,128)S(1)} collective-permute-done((f32[64,128]{1,0:T(8,128)S(1)}, f32[64,128]{1,0:T(8,128)S(1)}, u32[]{:S(2)}, u32[]{:S(2)}) %collective-permute-start.8) | collective-permute-done | bytes 32800 | tf_op jit(solution)/shard_map/ppermute | solution.py:359
  86.2 1.9 %collective-permute-start.9 = (f32[64,128]{1,0:T(8,128)S(1)}, f32[64,128]{1,0:T(8,128)S(1)}, u32[]{:S(2)}, u32[]{:S(2)}) collective-permute-start(f32[64,128]{1,0:T(8,128)S(1)} %add.24), channel_id=1, source_target_pairs={{0,12},{1,13},{2,14},{3,15},{4,8},{5,9},{6,10},{7,11},{8,4},{9,5},... | collective-permute-start | bytes 98312 | tf_op jit(solution)/shard_map/ppermute | solution.py:359
  88.1 3.2 %collective-permute-done.9 = f32[64,128]{1,0:T(8,128)S(1)} collective-permute-done((f32[64,128]{1,0:T(8,128)S(1)}, f32[64,128]{1,0:T(8,128)S(1)}, u32[]{:S(2)}, u32[]{:S(2)}) %collective-permute-start.9) | collective-permute-done | bytes 32800 | tf_op jit(solution)/shard_map/ppermute | solution.py:359
  91.4 0.8 collective-permute-start.14
  92.2 2.2 %collective-permute-start.12 = (f32[128,128]{1,0:T(8,128)S(1)}, f32[128,128]{1,0:T(8,128)S(1)}, u32[]{:S(2)}, u32[]{:S(2)}) collective-permute-start(f32[128,128]{1,0:T(8,128)S(1)} %get-tuple-element.108), channel_id=1, source_target_pairs={{0,3},{1,2},{2,1},{3,0},{4,7},{5,6},{6,5},{7,4},{8,11},{9,10},{10,... | collective-permute-start | bytes 196616 | tf_op jit(solution)/shard_map/ppermute | solution.py:359
  95.3 1.8 %collective-permute-start.15 = (f32[64,128]{1,0:T(8,128)S(1)}, f32[64,128]{1,0:T(8,128)S(1)}, u32[]{:S(2)}, u32[]{:S(2)}) collective-permute-start(f32[64,128]{1,0:T(8,128)S(1)} %add.26), channel_id=1, source_target_pairs={{0,3},{1,2},{2,1},{3,0},{4,7},{5,6},{6,5},{7,4},{8,11},{9,10},{10,... | collective-permute-start | bytes 98312 | tf_op jit(solution)/shard_map/ppermute | solution.py:359
  97.1 3.3 %collective-permute-done.15 = f32[64,128]{1,0:T(8,128)S(1)} collective-permute-done((f32[64,128]{1,0:T(8,128)S(1)}, f32[64,128]{1,0:T(8,128)S(1)}, u32[]{:S(2)}, u32[]{:S(2)}) %collective-permute-start.15) | collective-permute-done | bytes 32800 | tf_op jit(solution)/shard_map/ppermute | solution.py:359
  100.4 0.7 shard_map.95
  101.2 1.2 %collective-permute-done.16.other = f32[64,128]{1,0:T(8,128)S(1)} collective-permute-done((f32[64,128]{1,0:T(8,128)S(1)}, f32[64,128]{1,0:T(8,128)S(1)}, u32[]{:S(2)}, u32[]{:S(2)}) %collective-permute-start.16) | collective-permute-done | bytes 32800 | tf_op jit(solution)/shard_map/ppermute | solution.py:351
  (34 shorter events, 3.8 us)
Async XLA Ops:
  7.3 16.7 %all-to-all-start = ((f32[16,32,128]{2,1,0:T(8,128)}), f32[16,32,128]{2,1,0:T(8,128)S(1)}, u32[]{:S(2)}, u32[]{:S(2)}) async-start(f32[16,32,128]{2,1,0:T(8,128)} %get-tuple-element.61), calls=%async_computation | async-start | bytes 524288 | tf_op jit(solution)/shard_map/all_to_all | solution.py:371
  15.3 1.2 %copy-start = (bf16[4096,128]{1,0:T(8,128)(2,1)S(1)}, bf16[4096,128]{1,0:T(8,128)(2,1)}, u32[]{:S(2)}) copy-start(bf16[4096,128]{1,0:T(8,128)(2,1)} %src) | copy-start | bytes 3145732
  16.5 0.9 copy-start.1
  61.8 15.9 %copy-start.2 = (bf16[1024,128]{1,0:T(8,128)(2,1)S(1)}, bf16[1024,128]{1,0:T(8,128)(2,1)}, u32[]{:S(2)}) copy-start(bf16[1024,128]{1,0:T(8,128)(2,1)} %tgt.2) | copy-start | bytes 786436
  61.8 1.6 %collective-permute-start = (f32[64,1024]{1,0:T(8,128)S(1)}, f32[64,1024]{1,0:T(8,128)S(1)}, u32[]{:S(2)}, u32[]{:S(2)}) collective-permute-start(f32[64,1024]{1,0:T(8,128)S(1)} %get-tuple-element.85), channel_id=1, source_target_pairs={{0,16},{16,0},{32,48},{48,32},{64,80},{80,64},{96,112},{112,96},{1... | collective-permute-start | bytes 786440 | tf_op jit(solution)/shard_map/ppermute | solution.py:351
  61.8 9.3 %collective-permute-start.2 = (f32[1024,128]{1,0:T(8,128)S(1)}, f32[1024,128]{1,0:T(8,128)S(1)}, u32[]{:S(2)}, u32[]{:S(2)}) collective-permute-start(f32[1024,128]{1,0:T(8,128)S(1)} %get-tuple-element.87), channel_id=1, source_target_pairs={{0,4},{1,5},{2,6},{3,7},{4,0},{5,1},{6,2},{7,3},{8,12},{9,13},{10,... | collective-permute-start | bytes 1572872 | tf_op jit(solution)/shard_map/ppermute | solution.py:359
  62.0 10.4 %collective-permute-start.3 = (f32[1024,128]{1,0:T(8,128)S(1)}, f32[1024,128]{1,0:T(8,128)S(1)}, u32[]{:S(2)}, u32[]{:S(2)}) collective-permute-start(f32[1024,128]{1,0:T(8,128)S(1)} %get-tuple-element.89), channel_id=1, source_target_pairs={{0,12},{1,13},{2,14},{3,15},{4,8},{5,9},{6,10},{7,11},{8,4},{9,5},... | collective-permute-start | bytes 1572872 | tf_op jit(solution)/shard_map/ppermute | solution.py:359
  63.4 6.5 %collective-permute-start.1 = (f32[64,1024]{1,0:T(8,128)S(1)}, f32[64,1024]{1,0:T(8,128)S(1)}, u32[]{:S(2)}, u32[]{:S(2)}) collective-permute-start(f32[64,1024]{1,0:T(8,128)S(1)} %add.21), channel_id=1, source_target_pairs={{0,32},{1,33},{2,34},{3,35},{4,36},{5,37},{6,38},{7,39},{8,40},{9,... | collective-permute-start | bytes 786440 | tf_op jit(solution)/shard_map/ppermute | solution.py:359
  69.9 7.7 %collective-permute-start.4 = (f32[64,1024]{1,0:T(8,128)S(1)}, f32[64,1024]{1,0:T(8,128)S(1)}, u32[]{:S(2)}, u32[]{:S(2)}) collective-permute-start(f32[64,1024]{1,0:T(8,128)S(1)} %add.22), channel_id=1, source_target_pairs={{0,96},{1,97},{2,98},{3,99},{4,100},{5,101},{6,102},{7,103},{8,104... | collective-permute-start | bytes 786440 | tf_op jit(solution)/shard_map/ppermute | solution.py:359
  72.5 7.7 %collective-permute-start.5 = (f32[512,128]{1,0:T(8,128)S(1)}, f32[512,128]{1,0:T(8,128)S(1)}, u32[]{:S(2)}, u32[]{:S(2)}) collective-permute-start(f32[512,128]{1,0:T(8,128)S(1)} %get-tuple-element.94), channel_id=1, source_target_pairs={{0,12},{1,13},{2,14},{3,15},{4,8},{5,9},{6,10},{7,11},{8,4},{9,5},... | collective-permute-start | bytes 786440 | tf_op jit(solution)/shard_map/ppermute | solution.py:359
  73.9 6.4 %collective-permute-start.6 = (f32[512,128]{1,0:T(8,128)S(1)}, f32[512,128]{1,0:T(8,128)S(1)}, u32[]{:S(2)}, u32[]{:S(2)}) collective-permute-start(f32[512,128]{1,0:T(8,128)S(1)} %get-tuple-element.96), channel_id=1, source_target_pairs={{0,4},{1,5},{2,6},{3,7},{4,0},{5,1},{6,2},{7,3},{8,12},{9,13},{10,... | collective-permute-start | bytes 786440 | tf_op jit(solution)/shard_map/ppermute | solution.py:359
  77.6 4.7 %collective-permute-start.7 = (f32[64,1024]{1,0:T(8,128)S(1)}, f32[64,1024]{1,0:T(8,128)S(1)}, u32[]{:S(2)}, u32[]{:S(2)}) collective-permute-start(f32[64,1024]{1,0:T(8,128)S(1)} %add.23.mine), channel_id=1, source_target_pairs={{0,16},{16,0},{32,48},{48,32},{64,80},{80,64},{96,112},{112,96},{1... | collective-permute-start | bytes 786440 | tf_op jit(solution)/shard_map/ppermute | solution.py:351
  80.4 11.7 %collective-permute-start.10 = (f32[256,128]{1,0:T(8,128)S(1)}, f32[256,128]{1,0:T(8,128)S(1)}, u32[]{:S(2)}, u32[]{:S(2)}) collective-permute-start(f32[256,128]{1,0:T(8,128)S(1)} %get-tuple-element.102), channel_id=1, source_target_pairs={{0,1},{1,0},{2,3},{3,2},{4,5},{5,4},{6,7},{7,6},{8,9},{9,8},{10,11... | collective-permute-start | bytes 393224 | tf_op jit(solution)/shard_map/ppermute | solution.py:359
  80.9 11.3 %collective-permute-start.11 = (f32[256,128]{1,0:T(8,128)S(1)}, f32[256,128]{1,0:T(8,128)S(1)}, u32[]{:S(2)}, u32[]{:S(2)}) collective-permute-start(f32[256,128]{1,0:T(8,128)S(1)} %get-tuple-element.104), channel_id=1, source_target_pairs={{0,3},{1,2},{2,1},{3,0},{4,7},{5,6},{6,5},{7,4},{8,11},{9,10},{10,... | collective-permute-start | bytes 393224 | tf_op jit(solution)/shard_map/ppermute | solution.py:359
  82.3 3.9 %collective-permute-start.8 = (f32[64,128]{1,0:T(8,128)S(1)}, f32[64,128]{1,0:T(8,128)S(1)}, u32[]{:S(2)}, u32[]{:S(2)}) collective-permute-start(f32[64,128]{1,0:T(8,128)S(1)} %shard_map.91), channel_id=1, source_target_pairs={{0,4},{1,5},{2,6},{3,7},{4,0},{5,1},{6,2},{7,3},{8,12},{9,13},{10,... | collective-permute-start | bytes 98312 | tf_op jit(solution)/shard_map/ppermute | solution.py:359
  86.2 5.1 %collective-permute-start.9 = (f32[64,128]{1,0:T(8,128)S(1)}, f32[64,128]{1,0:T(8,128)S(1)}, u32[]{:S(2)}, u32[]{:S(2)}) collective-permute-start(f32[64,128]{1,0:T(8,128)S(1)} %add.24), channel_id=1, source_target_pairs={{0,12},{1,13},{2,14},{3,15},{4,8},{5,9},{6,10},{7,11},{8,4},{9,5},... | collective-permute-start | bytes 98312 | tf_op jit(solution)/shard_map/ppermute | solution.py:359
  91.4 3.9 %collective-permute-start.14 = (f32[64,128]{1,0:T(8,128)S(1)}, f32[64,128]{1,0:T(8,128)S(1)}, u32[]{:S(2)}, u32[]{:S(2)}) collective-permute-start(f32[64,128]{1,0:T(8,128)S(1)} %add.25), channel_id=1, source_target_pairs={{0,1},{1,0},{2,3},{3,2},{4,5},{5,4},{6,7},{7,6},{8,9},{9,8},{10,11... | collective-permute-start | bytes 98312 | tf_op jit(solution)/shard_map/ppermute | solution.py:359
  92.2 8.2 %collective-permute-start.12 = (f32[128,128]{1,0:T(8,128)S(1)}, f32[128,128]{1,0:T(8,128)S(1)}, u32[]{:S(2)}, u32[]{:S(2)}) collective-permute-start(f32[128,128]{1,0:T(8,128)S(1)} %get-tuple-element.108), channel_id=1, source_target_pairs={{0,3},{1,2},{2,1},{3,0},{4,7},{5,6},{6,5},{7,4},{8,11},{9,10},{10,... | collective-permute-start | bytes 196616 | tf_op jit(solution)/shard_map/ppermute | solution.py:359
  94.3 6.1 %collective-permute-start.13 = (f32[128,128]{1,0:T(8,128)S(1)}, f32[128,128]{1,0:T(8,128)S(1)}, u32[]{:S(2)}, u32[]{:S(2)}) collective-permute-start(f32[128,128]{1,0:T(8,128)S(1)} %get-tuple-element.110), channel_id=1, source_target_pairs={{0,1},{1,0},{2,3},{3,2},{4,5},{5,4},{6,7},{7,6},{8,9},{9,8},{10,11... | collective-permute-start | bytes 196616 | tf_op jit(solution)/shard_map/ppermute | solution.py:359
  95.3 5.1 %collective-permute-start.15 = (f32[64,128]{1,0:T(8,128)S(1)}, f32[64,128]{1,0:T(8,128)S(1)}, u32[]{:S(2)}, u32[]{:S(2)}) collective-permute-start(f32[64,128]{1,0:T(8,128)S(1)} %add.26), channel_id=1, source_target_pairs={{0,3},{1,2},{2,1},{3,0},{4,7},{5,6},{6,5},{7,4},{8,11},{9,10},{10,... | collective-permute-start | bytes 98312 | tf_op jit(solution)/shard_map/ppermute | solution.py:359
  101.2 1.2 %collective-permute-start.16 = (f32[64,128]{1,0:T(8,128)S(1)}, f32[64,128]{1,0:T(8,128)S(1)}, u32[]{:S(2)}, u32[]{:S(2)}) collective-permute-start(f32[64,128]{1,0:T(8,128)S(1)} %add.27.mine), channel_id=1, source_target_pairs={{0,16},{16,0},{32,48},{48,32},{64,80},{80,64},{96,112},{112,96},{1... | collective-permute-start | bytes 98312 | tf_op jit(solution)/shard_map/ppermute | solution.py:351

commit v5 on v4

--- a/solution.py
+++ b/solution.py
@@ -12,6 +12,8 @@
 BF16 = jnp.bfloat16
 NT = (((1,), (1,)), ((), ()))
 TINY = 2.0**-80
+SMALL, LARGE = 1e-30, 1e30
+GUESS = 0.3
 BLK = 512
 CHUNK = 256
 SLABS = BLK // 128
@@ -79,33 +81,65 @@
 
 def first_rows(src_in, tgt_in, factor_in, start_in, lse, proj_t, aug, start, src, factor, sems):
     copies = [
-        pltpu.make_async_copy(factor_in, factor, sems.at[0]),
-        pltpu.make_async_copy(src_in, src, sems.at[1]),
-        pltpu.make_async_copy(start_in, start, sems.at[2]),
+        pltpu.make_async_copy(start_in, start, sems.at[0]),
+        pltpu.make_async_copy(factor_in, factor, sems.at[1]),
+        pltpu.make_async_copy(src_in, src, sems.at[2]),
         pltpu.make_async_copy(tgt_in, aug.at[:, pl.ds(0, 128)], sems.at[3]),
     ]
     for copy in copies:
         copy.start()
-    under = aug_rows(jnp.zeros((1, BLK), F32))
-    for copy in copies:
+    copies[0].wait()
+    aug[:, 128:] = aug_columns(column(flat(start[...])))
+    for copy in copies[1:]:
         copy.wait()
     factor_t = factor[...].astype(F32).T.astype(BF16)
     proj_t[...] = lax.dot_general(factor_t, src[...], NT, preferred_element_type=F32).astype(BF16)
-    aug[:, 128:] = aug_columns(column(flat(start[...])))
-    values = []
-    for b in range(src.shape[0] // BLK):
-        right = jnp.concatenate([proj_t[:, b * BLK : (b + 1) * BLK], under], axis=0)
-        largest = jnp.full((8, BLK), -jnp.inf, F32)
+    blocks = src.shape[0] // BLK
+    chunks = aug.shape[0] // CHUNK
+
+    def scores(c, right):
+        x = jnp.dot(aug[c * CHUNK : (c + 1) * CHUNK, :], right, preferred_element_type=F32)
+        return x.reshape(CHUNK // 8, 8, BLK)
+
+    tgt = aug[:, :128].astype(F32)
+    reach = GUESS * jnp.sqrt(jnp.max(jnp.sum(tgt * tgt, axis=1, keepdims=True), axis=0, keepdims=True))
+    totals, values = [], []
+    for b in range(blocks):
+        proj = proj_t[:, b * BLK : (b + 1) * BLK]
+        wide = proj.astype(F32)
+        shift = reach * jnp.sqrt(jnp.sum(wide * wide, axis=0, keepdims=True))
+        right = jnp.concatenate([proj, aug_rows(-shift)], axis=0)
         total = jnp.zeros((8, BLK), F32)
-        for c in range(aug.shape[0] // CHUNK):
-            x = jnp.dot(aug[c * CHUNK : (c + 1) * CHUNK, :], right, preferred_element_type=F32)
-            x = x.reshape(CHUNK // 8, 8, BLK)
-            new = jnp.maximum(largest, jnp.max(x, axis=0))
-            total = total * jnp.exp(largest - new) + jnp.sum(jnp.exp(x - new[None]), axis=0)
-            largest = new
-        top = jnp.max(largest, axis=0, keepdims=True)
-        values.append(top + jnp.log(jnp.sum(total * jnp.exp(largest - top), axis=0, keepdims=True)))
-    lse[...] = jnp.broadcast_to(jnp.concatenate([stack(v, 128) for v in values], axis=0)[None], lse.shape)
+        for c in range(chunks):
+            total += jnp.sum(jnp.exp(scores(c, right)), axis=0)
+        total = jnp.sum(total, axis=0, keepdims=True)
+        totals.append(total)
+        values.append(stack(shift + jnp.log(total), 128))
+    lse[...] = jnp.broadcast_to(jnp.concatenate(values, axis=0)[None], lse.shape)
+    totals = jnp.concatenate(totals, axis=0)
+    good = jnp.where((totals > SMALL) & (totals < LARGE), 1.0, 0.0)
+
+    @pl.when(jnp.min(good) < 0.5)
+    def _():
+        under = aug_rows(jnp.zeros((1, BLK), F32))
+
+        def block(b, carry):
+            right = jnp.concatenate([proj_t[:, lanes(b, BLK)], under], axis=0)
+            largest = jnp.full((8, BLK), -jnp.inf, F32)
+            total = jnp.zeros((8, BLK), F32)
+            for c in range(chunks):
+                x = scores(c, right)
+                new = jnp.maximum(largest, jnp.max(x, axis=0))
+                total = total * jnp.exp(largest - new) + jnp.sum(jnp.exp(x - new[None]), axis=0)
+                largest = new
+            top = jnp.max(largest, axis=0, keepdims=True)
+            value = top + jnp.log(jnp.sum(total * jnp.exp(largest - top), axis=0, keepdims=True))
+            for i in range(SLABS):
+                row = jnp.broadcast_to(value[:, i * 128 : (i + 1) * 128][None], (lse.shape[0], 1, 128))
+                lse[:, pl.ds(b * SLABS + i, 1), :] = row
+            return carry
+
+        lax.fori_loop(0, blocks, block, 0)
 
 
 def transposes(src, tgt, src_t, tgt_t):

time: 104 us -> 108 us (1.038)
  Pallas kernels: 19.4 us -> 23.1 us
    pallas_call x14, Pallas kernels: 19.4 us -> 23.1 us  [call(): pl.pallas_call(body, out_shape=outs, in_specs=[pl.BlockSpec(memory_space=...]
where the time goes in v5:
time: 108 us; the launch traced here: 107 us
  waiting for transfers between devices  29.6 us (27%)
  blocking collectives  29.1 us (27%)
  Pallas kernels  23.1 us (21%)
  starting transfers between devices  21.9 us (20%)
  local copies, waits for them, and re-layouts  2.17 us (2%)
    all_to_all x3, blocking collectives, exchange(): return lax.all_to_all(x, axis, 0, 0)  29.1 us
    pallas_call x14, Pallas kernels, call(): pl.pallas_call(body, out_shape=outs, in_specs=[pl.BlockSpec(memory_space=...  23.1 us
    ppermute x14, waiting for transfers between devices, by_core(): return lax.ppermute(x, ('row', 'col'), pairs)  22.3 us
    ppermute x14, starting transfers between devices, by_core(): return lax.ppermute(x, ('row', 'col'), pairs)  13.8 us
    all_to_all x1, starting transfers between devices, exchange(): return lax.all_to_all(x, axis, 0, 0)  7.97 us
    all_to_all x1, waiting for transfers between devices, exchange(): return lax.all_to_all(x, axis, 0, 0)  6 us
    unnamed x6, local copies, waits for them, and re-layouts  2.17 us
  transfers between devices with their start and end apart: 18, of which 11 were waited for; matrix products, arithmetic and copies ran while one was open for 0% of the time, Pallas kernels for 3%

profile of v5, /device:TPU:0, one launch (start us, length us, event | category | flops | bytes accessed | tf_op | source)
XLA Modules:
  0.0 106.7 jit_solution(5233760137301585302)
XLA Ops:
  0.6 10.3 %shard_map.83 = (f32[16,32,128]{2,1,0:T(8,128)}, bf16[128,4096]{1,0:T(8,128)(2,1)S(1)}, bf16[1024,256]{1,0:T(8,128)(2,1)S(1)}, f32[8,128]{1,0:T(8,128)S(1)}) custom-call(bf16[4096,128]{1,0:T(8,128)(2,1)} %src, bf16[1024,128]{1,0:T(8,128)(2,1)} %tgt.2, bf16[128,128]{1,0:T(8,128)(2,1)} %factor_in.1, f32[8,128]{1,0:T(8,128)} %bitcast.3), custom_call_target="tpu_custom_call" | custom-call | flops 1 | bytes 1 | tf_op jit(solution)/shard_map/pallas_call | solution.py:348
  11.0 8.0 %all-to-all-start = ((f32[16,32,128]{2,1,0:T(8,128)}), f32[16,32,128]{2,1,0:T(8,128)S(1)}, u32[]{:S(2)}, u32[]{:S(2)}) async-start(f32[16,32,128]{2,1,0:T(8,128)} %get-tuple-element.61), calls=%async_computation | async-start | bytes 524288 | tf_op jit(solution)/shard_map/all_to_all | solution.py:405
  19.0 1.2 %copy-done = bf16[4096,128]{1,0:T(8,128)(2,1)S(1)} copy-done((bf16[4096,128]{1,0:T(8,128)(2,1)S(1)}, bf16[4096,128]{1,0:T(8,128)(2,1)}, u32[]{:S(2)}) %copy-start) | copy-done | bytes 1048600
  20.2 0.9 copy-done.1
  21.6 6.0 %all-to-all-done.parts = f32[16,32,128]{2,1,0:T(8,128)S(1)} async-done(((f32[16,32,128]{2,1,0:T(8,128)}), f32[16,32,128]{2,1,0:T(8,128)S(1)}, u32[]{:S(2)}, u32[]{:S(2)}) %all-to-all-start) | async-done | bytes 262176 | tf_op jit(solution)/shard_map/all_to_all | solution.py:405
  27.6 2.9 %shard_map.85 = (bf16[32,1024,128]{2,1,0:T(8,128)(2,1)S(1)}, f32[8,8,128]{2,1,0:T(8,128)S(1)}, f32[8,128]{1,0:T(8,128)S(1)}, f32[32,128]{1,0:T(8,128)S(1)}) custom-call(f32[16,32,128]{2,1,0:T(8,128)S(1)} %all-to-all-done.parts, bf16[128,4096]{1,0:T(8,128)(2,1)S(1)} %get-tuple-element.62.proj_t, bf16[1024,256]{1,0:T(8,128)(2,1)S(1)} %get-tuple-element.68.aug, ...), custom_call_target="tpu_custom_call" | custom-call | flops 1 | bytes 1 | tf_op jit(solution)/shard_map/pallas_call | solution.py:348
  30.5 9.7 %all_to_all.20.parts = f32[8,8,128]{2,1,0:T(8,128)S(1)} all-to-all(f32[8,8,128]{2,1,0:T(8,128)S(1)} %get-tuple-element.70), channel_id=1, replica_groups=mesh['row'=8,'col'=16] {'row'}, dimensions={0} | all-to-all | bytes 65536 | tf_op jit(solution)/shard_map/all_to_all | solution.py:405
  40.2 1.2 %shard_map.86 = (f32[16,32,128]{2,1,0:T(8,128)S(1)}, f32[8,128]{1,0:T(8,128)S(1)}, f32[8,128]{1,0:T(8,128)S(1)}) custom-call(f32[8,8,128]{2,1,0:T(8,128)S(1)} %all_to_all.20.parts, f32[8,128]{1,0:T(8,128)S(1)} %get-tuple-element.71.shift, bf16[32,1024,128]{2,1,0:T(8,128)(2,1)S(1)} %get-tuple-element.72.kernel_t), custom_call_target="tpu_custom_call" | custom-call | flops 1 | bytes 1 | tf_op jit(solution)/shard_map/pallas_call | solution.py:348
  41.5 11.6 %all_to_all.21.parts = f32[16,32,128]{2,1,0:T(8,128)S(1)} all-to-all(f32[16,32,128]{2,1,0:T(8,128)S(1)} %get-tuple-element.73), channel_id=1, replica_groups=mesh['row'=8,'col'=16] {'col'}, dimensions={0} | all-to-all | bytes 524288 | tf_op jit(solution)/shard_map/all_to_all | solution.py:405
  53.1 3.4 %shard_map.87 = (f32[8,8,128]{2,1,0:T(8,128)S(1)}, f32[64,1024]{1,0:T(8,128)S(1)}, f32[64,1024]{1,0:T(8,128)S(1)}, f32[32,128]{1,0:T(8,128)S(1)}, f32[32,128]{1,0:T(8,128)}) custom-call(f32[16,32,128]{2,1,0:T(8,128)S(1)} %all_to_all.21.parts, f32[32,128]{1,0:T(8,128)S(1)} %get-tuple-element.74.rho, bf16[32,1024,128]{2,1,0:T(8,128)(2,1)S(1)} %get-tuple-element.72.kernel_t, ...), custom_call_target="tpu_custom_call" | custom-call | flops 1 | bytes 1 | tf_op jit(solution)/shard_map/pallas_call | solution.py:348
  56.5 7.8 %all_to_all.22.parts = f32[8,8,128]{2,1,0:T(8,128)S(1)} all-to-all(f32[8,8,128]{2,1,0:T(8,128)S(1)} %get-tuple-element.77), channel_id=1, replica_groups=mesh['row'=8,'col'=16] {'row'}, dimensions={0} | all-to-all | bytes 65536 | tf_op jit(solution)/shard_map/all_to_all | solution.py:405
  64.3 1.2 %shard_map.88 = (f32[1024,128]{1,0:T(8,128)S(1)}, f32[1024,128]{1,0:T(8,128)S(1)}, bf16[128,1024]{1,0:T(8,128)(2,1)S(1)}, f32[8,128]{1,0:T(8,128)}, f32[8,128]{1,0:T(8,128)S(1)}) custom-call(f32[8,8,128]{2,1,0:T(8,128)S(1)} %all_to_all.22.parts, f32[8,128]{1,0:T(8,128)S(1)} %get-tuple-element.76.weight, f32[8,128]{1,0:T(8,128)S(1)} %get-tuple-element.78.before, ...), custom_call_target="tpu_custom_call" | custom-call | flops 1 | bytes 1 | tf_op jit(solution)/shard_map/pallas_call | solution.py:348
  65.7 1.3 %collective-permute-start.3 = (f32[1024,128]{1,0:T(8,128)S(1)}, f32[1024,128]{1,0:T(8,128)S(1)}, u32[]{:S(2)}, u32[]{:S(2)}) collective-permute-start(f32[1024,128]{1,0:T(8,128)S(1)} %get-tuple-element.89), channel_id=1, source_target_pairs={{0,12},{1,13},{2,14},{3,15},{4,8},{5,9},{6,10},{7,11},{8,4},{9,5},... | collective-permute-start | bytes 1572872 | tf_op jit(solution)/shard_map/ppermute | solution.py:393
  67.1 0.7 collective-permute-start.1
  67.7 0.7 shard_map.89
  68.5 5.1 %collective-permute-done.1 = f32[64,1024]{1,0:T(8,128)S(1)} collective-permute-done((f32[64,1024]{1,0:T(8,128)S(1)}, f32[64,1024]{1,0:T(8,128)S(1)}, u32[]{:S(2)}, u32[]{:S(2)}) %collective-permute-start.1) | collective-permute-done | bytes 262176 | tf_op jit(solution)/shard_map/ppermute | solution.py:393
  73.6 1.2 %collective-permute-start.4 = (f32[64,1024]{1,0:T(8,128)S(1)}, f32[64,1024]{1,0:T(8,128)S(1)}, u32[]{:S(2)}, u32[]{:S(2)}) collective-permute-start(f32[64,1024]{1,0:T(8,128)S(1)} %add.22), channel_id=1, source_target_pairs={{0,96},{1,97},{2,98},{3,99},{4,100},{5,101},{6,102},{7,103},{8,104... | collective-permute-start | bytes 786440 | tf_op jit(solution)/shard_map/ppermute | solution.py:393
  74.8 1.3 %collective-permute-done.3.got_b = f32[1024,128]{1,0:T(8,128)S(1)} collective-permute-done((f32[1024,128]{1,0:T(8,128)S(1)}, f32[1024,128]{1,0:T(8,128)S(1)}, u32[]{:S(2)}, u32[]{:S(2)}) %collective-permute-start.3) | collective-permute-done | bytes 524320 | tf_op jit(solution)/shard_map/ppermute | solution.py:393
  76.2 1.4 %collective-permute-start.5 = (f32[512,128]{1,0:T(8,128)S(1)}, f32[512,128]{1,0:T(8,128)S(1)}, u32[]{:S(2)}, u32[]{:S(2)}) collective-permute-start(f32[512,128]{1,0:T(8,128)S(1)} %get-tuple-element.94), channel_id=1, source_target_pairs={{0,12},{1,13},{2,14},{3,15},{4,8},{5,9},{6,10},{7,11},{8,4},{9,5},... | collective-permute-start | bytes 786440 | tf_op jit(solution)/shard_map/ppermute | solution.py:393
  77.6 3.6 %collective-permute-done.4 = f32[64,1024]{1,0:T(8,128)S(1)} collective-permute-done((f32[64,1024]{1,0:T(8,128)S(1)}, f32[64,1024]{1,0:T(8,128)S(1)}, u32[]{:S(2)}, u32[]{:S(2)}) %collective-permute-start.4) | collective-permute-done | bytes 262176 | tf_op jit(solution)/shard_map/ppermute | solution.py:393
  81.8 2.1 %collective-permute-done.5.got_a = f32[512,128]{1,0:T(8,128)S(1)} collective-permute-done((f32[512,128]{1,0:T(8,128)S(1)}, f32[512,128]{1,0:T(8,128)S(1)}, u32[]{:S(2)}, u32[]{:S(2)}) %collective-permute-start.5) | collective-permute-done | bytes 262176 | tf_op jit(solution)/shard_map/ppermute | solution.py:393
  84.6 1.4 %collective-permute-start.11 = (f32[256,128]{1,0:T(8,128)S(1)}, f32[256,128]{1,0:T(8,128)S(1)}, u32[]{:S(2)}, u32[]{:S(2)}) collective-permute-start(f32[256,128]{1,0:T(8,128)S(1)} %get-tuple-element.104), channel_id=1, source_target_pairs={{0,3},{1,2},{2,1},{3,0},{4,7},{5,6},{6,5},{7,4},{8,11},{9,10},{10,... | collective-permute-start | bytes 393224 | tf_op jit(solution)/shard_map/ppermute | solution.py:393
  86.0 0.9 shard_map.93
  86.9 3.1 %collective-permute-done.8 = f32[64,128]{1,0:T(8,128)S(1)} collective-permute-done((f32[64,128]{1,0:T(8,128)S(1)}, f32[64,128]{1,0:T(8,128)S(1)}, u32[]{:S(2)}, u32[]{:S(2)}) %collective-permute-start.8) | collective-permute-done | bytes 32800 | tf_op jit(solution)/shard_map/ppermute | solution.py:393
  89.9 1.9 %collective-permute-start.9 = (f32[64,128]{1,0:T(8,128)S(1)}, f32[64,128]{1,0:T(8,128)S(1)}, u32[]{:S(2)}, u32[]{:S(2)}) collective-permute-start(f32[64,128]{1,0:T(8,128)S(1)} %add.24), channel_id=1, source_target_pairs={{0,12},{1,13},{2,14},{3,15},{4,8},{5,9},{6,10},{7,11},{8,4},{9,5},... | collective-permute-start | bytes 98312 | tf_op jit(solution)/shard_map/ppermute | solution.py:393
  91.8 3.2 %collective-permute-done.9 = f32[64,128]{1,0:T(8,128)S(1)} collective-permute-done((f32[64,128]{1,0:T(8,128)S(1)}, f32[64,128]{1,0:T(8,128)S(1)}, u32[]{:S(2)}, u32[]{:S(2)}) %collective-permute-start.9) | collective-permute-done | bytes 32800 | tf_op jit(solution)/shard_map/ppermute | solution.py:393
  95.1 0.8 collective-permute-start.14
  95.9 2.2 %collective-permute-start.12 = (f32[128,128]{1,0:T(8,128)S(1)}, f32[128,128]{1,0:T(8,128)S(1)}, u32[]{:S(2)}, u32[]{:S(2)}) collective-permute-start(f32[128,128]{1,0:T(8,128)S(1)} %get-tuple-element.108), channel_id=1, source_target_pairs={{0,3},{1,2},{2,1},{3,0},{4,7},{5,6},{6,5},{7,4},{8,11},{9,10},{10,... | collective-permute-start | bytes 196616 | tf_op jit(solution)/shard_map/ppermute | solution.py:393
  99.0 1.8 %collective-permute-start.15 = (f32[64,128]{1,0:T(8,128)S(1)}, f32[64,128]{1,0:T(8,128)S(1)}, u32[]{:S(2)}, u32[]{:S(2)}) collective-permute-start(f32[64,128]{1,0:T(8,128)S(1)} %add.26), channel_id=1, source_target_pairs={{0,3},{1,2},{2,1},{3,0},{4,7},{5,6},{6,5},{7,4},{8,11},{9,10},{10,... | collective-permute-start | bytes 98312 | tf_op jit(solution)/shard_map/ppermute | solution.py:393
  100.8 3.3 %collective-permute-done.15 = f32[64,128]{1,0:T(8,128)S(1)} collective-permute-done((f32[64,128]{1,0:T(8,128)S(1)}, f32[64,128]{1,0:T(8,128)S(1)}, u32[]{:S(2)}, u32[]{:S(2)}) %collective-permute-start.15) | collective-permute-done | bytes 32800 | tf_op jit(solution)/shard_map/ppermute | solution.py:393
  104.1 0.7 shard_map.95
  104.9 1.2 %collective-permute-done.16.other = f32[64,128]{1,0:T(8,128)S(1)} collective-permute-done((f32[64,128]{1,0:T(8,128)S(1)}, f32[64,128]{1,0:T(8,128)S(1)}, u32[]{:S(2)}, u32[]{:S(2)}) %collective-permute-start.16) | collective-permute-done | bytes 32800 | tf_op jit(solution)/shard_map/ppermute | solution.py:385
  (34 shorter events, 3.7 us)
Async XLA Ops:
  11.0 16.7 %all-to-all-start = ((f32[16,32,128]{2,1,0:T(8,128)}), f32[16,32,128]{2,1,0:T(8,128)S(1)}, u32[]{:S(2)}, u32[]{:S(2)}) async-start(f32[16,32,128]{2,1,0:T(8,128)} %get-tuple-element.61), calls=%async_computation | async-start | bytes 524288 | tf_op jit(solution)/shard_map/all_to_all | solution.py:405
  19.0 1.2 %copy-start = (bf16[4096,128]{1,0:T(8,128)(2,1)S(1)}, bf16[4096,128]{1,0:T(8,128)(2,1)}, u32[]{:S(2)}) copy-start(bf16[4096,128]{1,0:T(8,128)(2,1)} %src) | copy-start | bytes 3145732
  20.2 0.9 copy-start.1
  65.5 15.9 %copy-start.2 = (bf16[1024,128]{1,0:T(8,128)(2,1)S(1)}, bf16[1024,128]{1,0:T(8,128)(2,1)}, u32[]{:S(2)}) copy-start(bf16[1024,128]{1,0:T(8,128)(2,1)} %tgt.2) | copy-start | bytes 786436
  65.5 1.6 %collective-permute-start = (f32[64,1024]{1,0:T(8,128)S(1)}, f32[64,1024]{1,0:T(8,128)S(1)}, u32[]{:S(2)}, u32[]{:S(2)}) collective-permute-start(f32[64,1024]{1,0:T(8,128)S(1)} %get-tuple-element.85), channel_id=1, source_target_pairs={{0,16},{16,0},{32,48},{48,32},{64,80},{80,64},{96,112},{112,96},{1... | collective-permute-start | bytes 786440 | tf_op jit(solution)/shard_map/ppermute | solution.py:385
  65.5 9.3 %collective-permute-start.2 = (f32[1024,128]{1,0:T(8,128)S(1)}, f32[1024,128]{1,0:T(8,128)S(1)}, u32[]{:S(2)}, u32[]{:S(2)}) collective-permute-start(f32[1024,128]{1,0:T(8,128)S(1)} %get-tuple-element.87), channel_id=1, source_target_pairs={{0,4},{1,5},{2,6},{3,7},{4,0},{5,1},{6,2},{7,3},{8,12},{9,13},{10,... | collective-permute-start | bytes 1572872 | tf_op jit(solution)/shard_map/ppermute | solution.py:393
  65.7 10.4 %collective-permute-start.3 = (f32[1024,128]{1,0:T(8,128)S(1)}, f32[1024,128]{1,0:T(8,128)S(1)}, u32[]{:S(2)}, u32[]{:S(2)}) collective-permute-start(f32[1024,128]{1,0:T(8,128)S(1)} %get-tuple-element.89), channel_id=1, source_target_pairs={{0,12},{1,13},{2,14},{3,15},{4,8},{5,9},{6,10},{7,11},{8,4},{9,5},... | collective-permute-start | bytes 1572872 | tf_op jit(solution)/shard_map/ppermute | solution.py:393
  67.1 6.5 %collective-permute-start.1 = (f32[64,1024]{1,0:T(8,128)S(1)}, f32[64,1024]{1,0:T(8,128)S(1)}, u32[]{:S(2)}, u32[]{:S(2)}) collective-permute-start(f32[64,1024]{1,0:T(8,128)S(1)} %add.21), channel_id=1, source_target_pairs={{0,32},{1,33},{2,34},{3,35},{4,36},{5,37},{6,38},{7,39},{8,40},{9,... | collective-permute-start | bytes 786440 | tf_op jit(solution)/shard_map/ppermute | solution.py:393
  73.6 7.7 %collective-permute-start.4 = (f32[64,1024]{1,0:T(8,128)S(1)}, f32[64,1024]{1,0:T(8,128)S(1)}, u32[]{:S(2)}, u32[]{:S(2)}) collective-permute-start(f32[64,1024]{1,0:T(8,128)S(1)} %add.22), channel_id=1, source_target_pairs={{0,96},{1,97},{2,98},{3,99},{4,100},{5,101},{6,102},{7,103},{8,104... | collective-permute-start | bytes 786440 | tf_op jit(solution)/shard_map/ppermute | solution.py:393
  76.2 7.7 %collective-permute-start.5 = (f32[512,128]{1,0:T(8,128)S(1)}, f32[512,128]{1,0:T(8,128)S(1)}, u32[]{:S(2)}, u32[]{:S(2)}) collective-permute-start(f32[512,128]{1,0:T(8,128)S(1)} %get-tuple-element.94), channel_id=1, source_target_pairs={{0,12},{1,13},{2,14},{3,15},{4,8},{5,9},{6,10},{7,11},{8,4},{9,5},... | collective-permute-start | bytes 786440 | tf_op jit(solution)/shard_map/ppermute | solution.py:393
  77.6 6.4 %collective-permute-start.6 = (f32[512,128]{1,0:T(8,128)S(1)}, f32[512,128]{1,0:T(8,128)S(1)}, u32[]{:S(2)}, u32[]{:S(2)}) collective-permute-start(f32[512,128]{1,0:T(8,128)S(1)} %get-tuple-element.96), channel_id=1, source_target_pairs={{0,4},{1,5},{2,6},{3,7},{4,0},{5,1},{6,2},{7,3},{8,12},{9,13},{10,... | collective-permute-start | bytes 786440 | tf_op jit(solution)/shard_map/ppermute | solution.py:393
  81.3 4.7 %collective-permute-start.7 = (f32[64,1024]{1,0:T(8,128)S(1)}, f32[64,1024]{1,0:T(8,128)S(1)}, u32[]{:S(2)}, u32[]{:S(2)}) collective-permute-start(f32[64,1024]{1,0:T(8,128)S(1)} %add.23.mine), channel_id=1, source_target_pairs={{0,16},{16,0},{32,48},{48,32},{64,80},{80,64},{96,112},{112,96},{1... | collective-permute-start | bytes 786440 | tf_op jit(solution)/shard_map/ppermute | solution.py:385
  84.1 11.7 %collective-permute-start.10 = (f32[256,128]{1,0:T(8,128)S(1)}, f32[256,128]{1,0:T(8,128)S(1)}, u32[]{:S(2)}, u32[]{:S(2)}) collective-permute-start(f32[256,128]{1,0:T(8,128)S(1)} %get-tuple-element.102), channel_id=1, source_target_pairs={{0,1},{1,0},{2,3},{3,2},{4,5},{5,4},{6,7},{7,6},{8,9},{9,8},{10,11... | collective-permute-start | bytes 393224 | tf_op jit(solution)/shard_map/ppermute | solution.py:393
  84.6 11.2 %collective-permute-start.11 = (f32[256,128]{1,0:T(8,128)S(1)}, f32[256,128]{1,0:T(8,128)S(1)}, u32[]{:S(2)}, u32[]{:S(2)}) collective-permute-start(f32[256,128]{1,0:T(8,128)S(1)} %get-tuple-element.104), channel_id=1, source_target_pairs={{0,3},{1,2},{2,1},{3,0},{4,7},{5,6},{6,5},{7,4},{8,11},{9,10},{10,... | collective-permute-start | bytes 393224 | tf_op jit(solution)/shard_map/ppermute | solution.py:393
  86.0 3.9 %collective-permute-start.8 = (f32[64,128]{1,0:T(8,128)S(1)}, f32[64,128]{1,0:T(8,128)S(1)}, u32[]{:S(2)}, u32[]{:S(2)}) collective-permute-start(f32[64,128]{1,0:T(8,128)S(1)} %shard_map.91), channel_id=1, source_target_pairs={{0,4},{1,5},{2,6},{3,7},{4,0},{5,1},{6,2},{7,3},{8,12},{9,13},{10,... | collective-permute-start | bytes 98312 | tf_op jit(solution)/shard_map/ppermute | solution.py:393
  89.9 5.1 %collective-permute-start.9 = (f32[64,128]{1,0:T(8,128)S(1)}, f32[64,128]{1,0:T(8,128)S(1)}, u32[]{:S(2)}, u32[]{:S(2)}) collective-permute-start(f32[64,128]{1,0:T(8,128)S(1)} %add.24), channel_id=1, source_target_pairs={{0,12},{1,13},{2,14},{3,15},{4,8},{5,9},{6,10},{7,11},{8,4},{9,5},... | collective-permute-start | bytes 98312 | tf_op jit(solution)/shard_map/ppermute | solution.py:393
  95.1 3.9 %collective-permute-start.14 = (f32[64,128]{1,0:T(8,128)S(1)}, f32[64,128]{1,0:T(8,128)S(1)}, u32[]{:S(2)}, u32[]{:S(2)}) collective-permute-start(f32[64,128]{1,0:T(8,128)S(1)} %add.25), channel_id=1, source_target_pairs={{0,1},{1,0},{2,3},{3,2},{4,5},{5,4},{6,7},{7,6},{8,9},{9,8},{10,11... | collective-permute-start | bytes 98312 | tf_op jit(solution)/shard_map/ppermute | solution.py:393
  95.9 8.3 %collective-permute-start.12 = (f32[128,128]{1,0:T(8,128)S(1)}, f32[128,128]{1,0:T(8,128)S(1)}, u32[]{:S(2)}, u32[]{:S(2)}) collective-permute-start(f32[128,128]{1,0:T(8,128)S(1)} %get-tuple-element.108), channel_id=1, source_target_pairs={{0,3},{1,2},{2,1},{3,0},{4,7},{5,6},{6,5},{7,4},{8,11},{9,10},{10,... | collective-permute-start | bytes 196616 | tf_op jit(solution)/shard_map/ppermute | solution.py:393
  98.0 6.1 %collective-permute-start.13 = (f32[128,128]{1,0:T(8,128)S(1)}, f32[128,128]{1,0:T(8,128)S(1)}, u32[]{:S(2)}, u32[]{:S(2)}) collective-permute-start(f32[128,128]{1,0:T(8,128)S(1)} %get-tuple-element.110), channel_id=1, source_target_pairs={{0,1},{1,0},{2,3},{3,2},{4,5},{5,4},{6,7},{7,6},{8,9},{9,8},{10,11... | collective-permute-start | bytes 196616 | tf_op jit(solution)/shard_map/ppermute | solution.py:393
  99.0 5.1 %collective-permute-start.15 = (f32[64,128]{1,0:T(8,128)S(1)}, f32[64,128]{1,0:T(8,128)S(1)}, u32[]{:S(2)}, u32[]{:S(2)}) collective-permute-start(f32[64,128]{1,0:T(8,128)S(1)} %add.26), channel_id=1, source_target_pairs={{0,3},{1,2},{2,1},{3,0},{4,7},{5,6},{6,5},{7,4},{8,11},{9,10},{10,... | collective-permute-start | bytes 98312 | tf_op jit(solution)/shard_map/ppermute | solution.py:393
  104.9 1.2 %collective-permute-start.16 = (f32[64,128]{1,0:T(8,128)S(1)}, f32[64,128]{1,0:T(8,128)S(1)}, u32[]{:S(2)}, u32[]{:S(2)}) collective-permute-start(f32[64,128]{1,0:T(8,128)S(1)} %add.27.mine), channel_id=1, source_target_pairs={{0,16},{16,0},{32,48},{48,32},{64,80},{80,64},{96,112},{112,96},{1... | collective-permute-start | bytes 98312 | tf_op jit(solution)/shard_map/ppermute | solution.py:385

commit v6 on v5

--- a/solution.py
+++ b/solution.py
@@ -312,13 +312,14 @@
     out[...] = (in_order(mine[...], other[...]) * (flat(gain[...]) * tgt_count)).T.astype(BF16)
 
 
-def merge_first(keep_a, got_a, keep_b, got_b, send_a, hold_a, send_b, hold_b):
+def merge_first(keep_a, got_a, keep_b, got_b, moment, send_a, hold_a, send_b, hold_b):
     for keep, got, send, hold in ((keep_a, got_a, send_a, hold_a), (keep_b, got_b, send_b, hold_b)):
         hold[...] = keep[:512, :] + got[:512, :]
-        send[...] = keep[512:, :] + got[512:, :]
-
-
-def merge_second(hold_a, got_a, hold_b, got_b, send_a, next_a, send_b, next_b):
+        send[:512, :] = keep[512:, :] + got[512:, :]
+        send[512:, :] = moment[...]
+
+
+def merge_second(hold_a, got_a, hold_b, got_b, moment, across, send_a, next_a, send_b, next_b):
     for half, (hold, got, send, after) in enumerate(
         ((hold_a, got_a, send_a, next_a), (hold_b, got_b, send_b, next_b))
     ):
@@ -326,16 +327,22 @@
             for k, minor in enumerate(offsets):
                 rows = slice(minor * 128, (minor + 1) * 128)
                 out[k * 128 : (k + 1) * 128, :] = hold[rows, :] + got[rows, :]
-
-
-def merge_third(hold_a, got_a, hold_b, got_b, send_a, next_a, send_b, next_b):
+    send_a[256:, :] = (moment[...] + got_b[512:, :]) + (across[...] + got_a[512:, :])
+
+
+def merge_third(hold_a, sent_a, got_a, hold_b, got_b, send_a, next_a, send_b, next_b):
     for hold, got, send, after in ((hold_a, got_a, send_a, next_a), (hold_b, got_b, send_b, next_b)):
         after[...] = hold[:128, :] + got[:128, :]
-        send[...] = hold[128:, :] + got[128:, :]
+        send[:128, :] = hold[128:, :] + got[128:256, :]
+    send_a[128:, :] = sent_a[256:, :] + got_a[256:, :]
+
+
+def merge_moment(sent, got, out):
+    out[...] = sent[128:, :] + got[128:, :]
 
 
 def merge_last(hold_a, got_a, hold_b, got_b, bary):
-    bary[:128, :] = (hold_a[...] + got_a[...]).T.astype(BF16)
+    bary[:128, :] = (hold_a[...] + got_a[:128, :]).T.astype(BF16)
     bary[128:, :] = (hold_b[...] + got_b[...]).T.astype(BF16)
 
 
@@ -451,32 +458,36 @@
     )
     send, _ = lax.optimization_barrier((send, left))
     mine = keep + swap(send)
-    mine = mine + along_y(mine, 1)
-    keep_a, mine = lax.optimization_barrier((keep_a, mine))
-    mine = mine + along_y(mine, 3)
     moment, = call(moment_half, [f32(width // 2, width)], mine, gain, tgt_emb)
+    moment = moment + along_y(moment, 1)
+    moment = moment + along_y(moment, 3)
+    keep_a, moment, mine = lax.optimization_barrier((keep_a, moment, mine))
+    both = [f32(576, 128), f32(512, 128)] * 2
+    send_a, hold_a, send_b, hold_b = call(merge_first, both, keep_a, got_a, keep_b, got_b, moment)
+    got_a, got_b, across = major(send_a, 3), major(send_b, 1), major(moment, 2)
+    hold_a, mine = lax.optimization_barrier((hold_a, mine))
+    rest = along_y(mine, 1)
+    both = [f32(320, 128), f32(256, 128), f32(256, 128), f32(256, 128)]
+    send_a, hold_a, send_b, hold_b = call(merge_second, both, hold_a, got_a, hold_b, got_b, moment, across)
+    sent_a = send_a
+    got_a, got_b = minor(send_a, 1), minor(send_b, 3)
+    hold_a, mine = lax.optimization_barrier((hold_a, mine))
+    mine = mine + rest
+    rest = along_y(mine, 3)
+    both = [f32(192, 128), f32(128, 128), f32(128, 128), f32(128, 128)]
+    send_a, hold_a, send_b, hold_b = call(merge_third, both, hold_a, sent_a, got_a, hold_b, got_b)
+    got_a, got_b = minor(send_a, 3), minor(send_b, 1)
+    hold_a, mine = lax.optimization_barrier((hold_a, mine))
+    mine = mine + rest
     bary_tgt, = call(
         functools.partial(finish_sources, tgt_count=tgt_count), [bf16(cols, width)], mine, swap(mine), gain
     )
-    send_a, hold_a, send_b, hold_b = call(merge_first, [f32(512, 128)] * 4, keep_a, got_a, keep_b, got_b)
-    got_a, got_b = major(send_a, 3), major(send_b, 1)
-    hold_a, moment = lax.optimization_barrier((hold_a, moment))
-    rest = major(moment, 1)
-    send_a, hold_a, send_b, hold_b = call(merge_second, [f32(256, 128)] * 4, hold_a, got_a, hold_b, got_b)
-    got_a, got_b = minor(send_a, 1), minor(send_b, 3)
-    hold_a, bary_tgt, moment = lax.optimization_barrier((hold_a, bary_tgt, moment))
-    moment = moment + rest
-    moment = moment + major(moment, 3)
-    hold_a, moment = lax.optimization_barrier((hold_a, moment))
-    rest = minor(moment, 1)
-    send_a, hold_a, send_b, hold_b = call(merge_third, [f32(128, 128)] * 4, hold_a, got_a, hold_b, got_b)
-    got_a, got_b = minor(send_a, 3), minor(send_b, 1)
-    hold_a, moment = lax.optimization_barrier((hold_a, moment))
-    moment = moment + rest
-    moment = moment + minor(moment, 3)
+    hold_a, send_a, bary_tgt = lax.optimization_barrier((hold_a, send_a, bary_tgt))
+    moment, = call(merge_moment, [f32(width // 2, width)], send_a, got_a)
+    other = swap(moment)
     bary_src, = call(merge_last, [bf16(share, width)], hold_a, got_a, hold_b, got_b)
     bary_src, moment = lax.optimization_barrier((bary_src, moment))
-    moment, = call(finish_moment, [f32(width, width)], moment, swap(moment))
+    moment, = call(finish_moment, [f32(width, width)], moment, other)
     return (bary_src, bary_tgt, moment, row_potential.reshape(rows), col_potential.reshape(cols))
 
 

time: 108 us -> 106 us (0.981)
  waiting for transfers between devices: 29.6 us -> 27.7 us
    ppermute x14 -> x13, waiting for transfers between devices: 22.3 us -> 19.7 us  [by_core(): return lax.ppermute(x, ('row', 'col'), pairs)]
    ppermute x14 -> x13, starting transfers between devices: 13.8 us -> 12.9 us  [by_core(): return lax.ppermute(x, ('row', 'col'), pairs)]
    pallas_call x14 -> x15, Pallas kernels: 23.1 us -> 23.1 us  [call(): pl.pallas_call(body, out_shape=outs, in_specs=[pl.BlockSpec(memory_space=...]
  transfers between devices with their start and end apart: 18 -> 17, of which waited for: 11 -> 8; matrix products, arithmetic and copies ran while one was open for 0% -> 0% of each run, Pallas kernels for 3% -> 3%
where the time goes in v6:
time: 106 us; the launch traced here: 104 us
  blocking collectives  29.1 us (27%)
  waiting for transfers between devices  27.7 us (26%)
  Pallas kernels  23.1 us (22%)
  starting transfers between devices  21 us (20%)
  local copies, waits for them, and re-layouts  2.17 us (2%)
    all_to_all x3, blocking collectives, exchange(): return lax.all_to_all(x, axis, 0, 0)  29.1 us
    pallas_call x15, Pallas kernels, call(): pl.pallas_call(body, out_shape=outs, in_specs=[pl.BlockSpec(memory_space=...  23.1 us
    ppermute x13, waiting for transfers between devices, by_core(): return lax.ppermute(x, ('row', 'col'), pairs)  19.7 us
    ppermute x13, starting transfers between devices, by_core(): return lax.ppermute(x, ('row', 'col'), pairs)  12.9 us
    all_to_all x1, starting transfers between devices, exchange(): return lax.all_to_all(x, axis, 0, 0)  7.97 us
    all_to_all x1, waiting for transfers between devices, exchange(): return lax.all_to_all(x, axis, 0, 0)  6 us
    unnamed x6, local copies, waits for them, and re-layouts  2.17 us
  transfers between devices with their start and end apart: 17, of which 8 were waited for; matrix products, arithmetic and copies ran while one was open for 0% of the time, Pallas kernels for 3%

profile of v6, /device:TPU:0, one launch (start us, length us, event | category | flops | bytes accessed | tf_op | source)
XLA Modules:
  0.0 104.0 jit_solution(14477761727754199427)
XLA Ops:
  0.6 10.3 %shard_map.83 = (f32[16,32,128]{2,1,0:T(8,128)}, bf16[128,4096]{1,0:T(8,128)(2,1)S(1)}, bf16[1024,256]{1,0:T(8,128)(2,1)S(1)}, f32[8,128]{1,0:T(8,128)S(1)}) custom-call(bf16[4096,128]{1,0:T(8,128)(2,1)} %src, bf16[1024,128]{1,0:T(8,128)(2,1)} %tgt.2, bf16[128,128]{1,0:T(8,128)(2,1)} %factor_in.1, f32[8,128]{1,0:T(8,128)} %bitcast.3), custom_call_target="tpu_custom_call" | custom-call | flops 1 | bytes 1 | tf_op jit(solution)/shard_map/pallas_call | solution.py:355
  11.0 8.0 %all-to-all-start = ((f32[16,32,128]{2,1,0:T(8,128)}), f32[16,32,128]{2,1,0:T(8,128)S(1)}, u32[]{:S(2)}, u32[]{:S(2)}) async-start(f32[16,32,128]{2,1,0:T(8,128)} %get-tuple-element.62), calls=%async_computation | async-start | bytes 524288 | tf_op jit(solution)/shard_map/all_to_all | solution.py:412
  19.0 1.2 %copy-done = bf16[4096,128]{1,0:T(8,128)(2,1)S(1)} copy-done((bf16[4096,128]{1,0:T(8,128)(2,1)S(1)}, bf16[4096,128]{1,0:T(8,128)(2,1)}, u32[]{:S(2)}) %copy-start) | copy-done | bytes 1048600
  20.2 0.9 copy-done.1
  21.1 0.5 shard_map.84
  21.6 6.0 %all-to-all-done.parts = f32[16,32,128]{2,1,0:T(8,128)S(1)} async-done(((f32[16,32,128]{2,1,0:T(8,128)}), f32[16,32,128]{2,1,0:T(8,128)S(1)}, u32[]{:S(2)}, u32[]{:S(2)}) %all-to-all-start) | async-done | bytes 262176 | tf_op jit(solution)/shard_map/all_to_all | solution.py:412
  27.6 2.9 %shard_map.85 = (bf16[32,1024,128]{2,1,0:T(8,128)(2,1)S(1)}, f32[8,8,128]{2,1,0:T(8,128)S(1)}, f32[8,128]{1,0:T(8,128)S(1)}, f32[32,128]{1,0:T(8,128)S(1)}) custom-call(f32[16,32,128]{2,1,0:T(8,128)S(1)} %all-to-all-done.parts, bf16[128,4096]{1,0:T(8,128)(2,1)S(1)} %get-tuple-element.63.proj_t, bf16[1024,256]{1,0:T(8,128)(2,1)S(1)} %get-tuple-element.69.aug, ...), custom_call_target="tpu_custom_call" | custom-call | flops 1 | bytes 1 | tf_op jit(solution)/shard_map/pallas_call | solution.py:355
  30.5 9.7 %all_to_all.20.parts = f32[8,8,128]{2,1,0:T(8,128)S(1)} all-to-all(f32[8,8,128]{2,1,0:T(8,128)S(1)} %get-tuple-element.71), channel_id=1, replica_groups=mesh['row'=8,'col'=16] {'row'}, dimensions={0} | all-to-all | bytes 65536 | tf_op jit(solution)/shard_map/all_to_all | solution.py:412
  40.2 1.2 %shard_map.86 = (f32[16,32,128]{2,1,0:T(8,128)S(1)}, f32[8,128]{1,0:T(8,128)S(1)}, f32[8,128]{1,0:T(8,128)S(1)}) custom-call(f32[8,8,128]{2,1,0:T(8,128)S(1)} %all_to_all.20.parts, f32[8,128]{1,0:T(8,128)S(1)} %get-tuple-element.72.shift, bf16[32,1024,128]{2,1,0:T(8,128)(2,1)S(1)} %get-tuple-element.73.kernel_t), custom_call_target="tpu_custom_call" | custom-call | flops 1 | bytes 1 | tf_op jit(solution)/shard_map/pallas_call | solution.py:355
  41.5 11.6 %all_to_all.21.parts = f32[16,32,128]{2,1,0:T(8,128)S(1)} all-to-all(f32[16,32,128]{2,1,0:T(8,128)S(1)} %get-tuple-element.74), channel_id=1, replica_groups=mesh['row'=8,'col'=16] {'col'}, dimensions={0} | all-to-all | bytes 524288 | tf_op jit(solution)/shard_map/all_to_all | solution.py:412
  53.1 3.4 %shard_map.87 = (f32[8,8,128]{2,1,0:T(8,128)S(1)}, f32[64,1024]{1,0:T(8,128)S(1)}, f32[64,1024]{1,0:T(8,128)S(1)}, f32[32,128]{1,0:T(8,128)S(1)}, f32[32,128]{1,0:T(8,128)}) custom-call(f32[16,32,128]{2,1,0:T(8,128)S(1)} %all_to_all.21.parts, f32[32,128]{1,0:T(8,128)S(1)} %get-tuple-element.75.rho, bf16[32,1024,128]{2,1,0:T(8,128)(2,1)S(1)} %get-tuple-element.73.kernel_t, ...), custom_call_target="tpu_custom_call" | custom-call | flops 1 | bytes 1 | tf_op jit(solution)/shard_map/pallas_call | solution.py:355
  56.5 7.8 %all_to_all.22.parts = f32[8,8,128]{2,1,0:T(8,128)S(1)} all-to-all(f32[8,8,128]{2,1,0:T(8,128)S(1)} %get-tuple-element.78), channel_id=1, replica_groups=mesh['row'=8,'col'=16] {'row'}, dimensions={0} | all-to-all | bytes 65536 | tf_op jit(solution)/shard_map/all_to_all | solution.py:412
  64.3 1.2 %shard_map.88 = (f32[1024,128]{1,0:T(8,128)S(1)}, f32[1024,128]{1,0:T(8,128)S(1)}, bf16[128,1024]{1,0:T(8,128)(2,1)S(1)}, f32[8,128]{1,0:T(8,128)}, f32[8,128]{1,0:T(8,128)S(1)}) custom-call(f32[8,8,128]{2,1,0:T(8,128)S(1)} %all_to_all.22.parts, f32[8,128]{1,0:T(8,128)S(1)} %get-tuple-element.77.weight, f32[8,128]{1,0:T(8,128)S(1)} %get-tuple-element.79.before, ...), custom_call_target="tpu_custom_call" | custom-call | flops 1 | bytes 1 | tf_op jit(solution)/shard_map/pallas_call | solution.py:355
  65.7 1.3 %collective-permute-start.4 = (f32[1024,128]{1,0:T(8,128)S(1)}, f32[1024,128]{1,0:T(8,128)S(1)}, u32[]{:S(2)}, u32[]{:S(2)}) collective-permute-start(f32[1024,128]{1,0:T(8,128)S(1)} %get-tuple-element.91), channel_id=1, source_target_pairs={{0,12},{1,13},{2,14},{3,15},{4,8},{5,9},{6,10},{7,11},{8,4},{9,5},... | collective-permute-start | bytes 1572872 | tf_op jit(solution)/shard_map/ppermute | solution.py:400
  67.1 1.5 %collective-permute-done = f32[64,1024]{1,0:T(8,128)S(1)} collective-permute-done((f32[64,1024]{1,0:T(8,128)S(1)}, f32[64,1024]{1,0:T(8,128)S(1)}, u32[]{:S(2)}, u32[]{:S(2)}) %collective-permute-start) | collective-permute-done | bytes 262176 | tf_op jit(solution)/shard_map/ppermute | solution.py:392
  69.0 0.7 collective-permute-start.1
  69.7 3.3 %collective-permute-done.1 = f32[64,128]{1,0:T(8,128)S(1)} collective-permute-done((f32[64,128]{1,0:T(8,128)S(1)}, f32[64,128]{1,0:T(8,128)S(1)}, u32[]{:S(2)}, u32[]{:S(2)}) %collective-permute-start.1) | collective-permute-done | bytes 32800 | tf_op jit(solution)/shard_map/ppermute | solution.py:400
  73.0 1.2 %collective-permute-start.2 = (f32[64,128]{1,0:T(8,128)S(1)}, f32[64,128]{1,0:T(8,128)S(1)}, u32[]{:S(2)}, u32[]{:S(2)}) collective-permute-start(f32[64,128]{1,0:T(8,128)S(1)} %add.16), channel_id=1, source_target_pairs={{0,96},{1,97},{2,98},{3,99},{4,100},{5,101},{6,102},{7,103},{8,104... | collective-permute-start | bytes 98312 | tf_op jit(solution)/shard_map/ppermute | solution.py:400
  74.2 0.7 shard_map.89
  74.9 3.2 %collective-permute-done.2 = f32[64,128]{1,0:T(8,128)S(1)} collective-permute-done((f32[64,128]{1,0:T(8,128)S(1)}, f32[64,128]{1,0:T(8,128)S(1)}, u32[]{:S(2)}, u32[]{:S(2)}) %collective-permute-start.2) | collective-permute-done | bytes 32800 | tf_op jit(solution)/shard_map/ppermute | solution.py:400
  78.3 2.0 %collective-permute-start.5 = (f32[576,128]{1,0:T(8,128)S(1)}, f32[576,128]{1,0:T(8,128)S(1)}, u32[]{:S(2)}, u32[]{:S(2)}) collective-permute-start(f32[576,128]{1,0:T(8,128)S(1)} %get-tuple-element.96), channel_id=1, source_target_pairs={{0,12},{1,13},{2,14},{3,15},{4,8},{5,9},{6,10},{7,11},{8,4},{9,5},... | collective-permute-start | bytes 884744 | tf_op jit(solution)/shard_map/ppermute | solution.py:400
  80.3 0.6 collective-permute-start.6
  80.9 2.2 %collective-permute-start.7 = (f32[64,128]{1,0:T(8,128)S(1)}, f32[64,128]{1,0:T(8,128)S(1)}, u32[]{:S(2)}, u32[]{:S(2)}) collective-permute-start(f32[64,128]{1,0:T(8,128)S(1)} %add.17.moment), channel_id=1, source_target_pairs={{0,8},{1,9},{2,10},{3,11},{4,12},{5,13},{6,14},{7,15},{8,0},{9,1},... | collective-permute-start | bytes 98312 | tf_op jit(solution)/shard_map/ppermute | solution.py:400
  83.1 5.0 %collective-permute-done.7.across = f32[64,128]{1,0:T(8,128)S(1)} collective-permute-done((f32[64,128]{1,0:T(8,128)S(1)}, f32[64,128]{1,0:T(8,128)S(1)}, u32[]{:S(2)}, u32[]{:S(2)}) %collective-permute-start.7) | collective-permute-done | bytes 32800 | tf_op jit(solution)/shard_map/ppermute | solution.py:400
  88.2 1.2 %collective-permute-start.11 = (f32[64,1024]{1,0:T(8,128)S(1)}, f32[64,1024]{1,0:T(8,128)S(1)}, u32[]{:S(2)}, u32[]{:S(2)}) collective-permute-start(f32[64,1024]{1,0:T(8,128)S(1)} %add.18), channel_id=1, source_target_pairs={{0,96},{1,97},{2,98},{3,99},{4,100},{5,101},{6,102},{7,103},{8,104... | collective-permute-start | bytes 786440 | tf_op jit(solution)/shard_map/ppermute | solution.py:400
  89.9 1.5 %collective-permute-start.9 = (f32[256,128]{1,0:T(8,128)S(1)}, f32[256,128]{1,0:T(8,128)S(1)}, u32[]{:S(2)}, u32[]{:S(2)}) collective-permute-start(f32[256,128]{1,0:T(8,128)S(1)} %get-tuple-element.104), channel_id=1, source_target_pairs={{0,3},{1,2},{2,1},{3,0},{4,7},{5,6},{6,5},{7,4},{8,11},{9,10},{10,... | collective-permute-start | bytes 393224 | tf_op jit(solution)/shard_map/ppermute | solution.py:400
  91.4 4.7 %collective-permute-done.9.got_b = f32[256,128]{1,0:T(8,128)S(1)} collective-permute-done((f32[256,128]{1,0:T(8,128)S(1)}, f32[256,128]{1,0:T(8,128)S(1)}, u32[]{:S(2)}, u32[]{:S(2)}) %collective-permute-start.9) | collective-permute-done | bytes 131104 | tf_op jit(solution)/shard_map/ppermute | solution.py:400
  96.3 1.6 %collective-permute-start.13 = (f32[192,128]{1,0:T(8,128)S(1)}, f32[192,128]{1,0:T(8,128)S(1)}, u32[]{:S(2)}, u32[]{:S(2)}) collective-permute-start(f32[192,128]{1,0:T(8,128)S(1)} %get-tuple-element.113.sent), channel_id=1, source_target_pairs={{0,3},{1,2},{2,1},{3,0},{4,7},{5,6},{6,5},{7,4},{8,11},{9,10},{10,... | collective-permute-start | bytes 294920 | tf_op jit(solution)/shard_map/ppermute | solution.py:400
  97.9 0.9 shard_map.94
  98.7 3.5 %collective-permute-done.13.got_a.got = f32[192,128]{1,0:T(8,128)S(1)} collective-permute-done((f32[192,128]{1,0:T(8,128)S(1)}, f32[192,128]{1,0:T(8,128)S(1)}, u32[]{:S(2)}, u32[]{:S(2)}) %collective-permute-start.13) | collective-permute-done | bytes 98336 | tf_op jit(solution)/shard_map/ppermute | solution.py:400
  102.2 0.7 shard_map.95
  103.4 0.6 shard_map.97
  (31 shorter events, 1.9 us)
Async XLA Ops:
  11.0 16.7 %all-to-all-start = ((f32[16,32,128]{2,1,0:T(8,128)}), f32[16,32,128]{2,1,0:T(8,128)S(1)}, u32[]{:S(2)}, u32[]{:S(2)}) async-start(f32[16,32,128]{2,1,0:T(8,128)} %get-tuple-element.62), calls=%async_computation | async-start | bytes 524288 | tf_op jit(solution)/shard_map/all_to_all | solution.py:412
  19.0 1.2 %copy-start = (bf16[4096,128]{1,0:T(8,128)(2,1)S(1)}, bf16[4096,128]{1,0:T(8,128)(2,1)}, u32[]{:S(2)}) copy-start(bf16[4096,128]{1,0:T(8,128)(2,1)} %src) | copy-start | bytes 3145732
  20.2 0.9 copy-start.1
  53.1 15.5 %copy-start.2 = (bf16[1024,128]{1,0:T(8,128)(2,1)S(1)}, bf16[1024,128]{1,0:T(8,128)(2,1)}, u32[]{:S(2)}) copy-start(bf16[1024,128]{1,0:T(8,128)(2,1)} %tgt.2) | copy-start | bytes 786436
  65.5 12.7 %collective-permute-start.3 = (f32[1024,128]{1,0:T(8,128)S(1)}, f32[1024,128]{1,0:T(8,128)S(1)}, u32[]{:S(2)}, u32[]{:S(2)}) collective-permute-start(f32[1024,128]{1,0:T(8,128)S(1)} %get-tuple-element.89), channel_id=1, source_target_pairs={{0,4},{1,5},{2,6},{3,7},{4,0},{5,1},{6,2},{7,3},{8,12},{9,13},{10,... | collective-permute-start | bytes 1572872 | tf_op jit(solution)/shard_map/ppermute | solution.py:400
  65.7 12.5 %collective-permute-start.4 = (f32[1024,128]{1,0:T(8,128)S(1)}, f32[1024,128]{1,0:T(8,128)S(1)}, u32[]{:S(2)}, u32[]{:S(2)}) collective-permute-start(f32[1024,128]{1,0:T(8,128)S(1)} %get-tuple-element.91), channel_id=1, source_target_pairs={{0,12},{1,13},{2,14},{3,15},{4,8},{5,9},{6,10},{7,11},{8,4},{9,5},... | collective-permute-start | bytes 1572872 | tf_op jit(solution)/shard_map/ppermute | solution.py:400
  67.0 1.5 %collective-permute-start = (f32[64,1024]{1,0:T(8,128)S(1)}, f32[64,1024]{1,0:T(8,128)S(1)}, u32[]{:S(2)}, u32[]{:S(2)}) collective-permute-start(f32[64,1024]{1,0:T(8,128)S(1)} %get-tuple-element.86), channel_id=1, source_target_pairs={{0,16},{16,0},{32,48},{48,32},{64,80},{80,64},{96,112},{112,96},{1... | collective-permute-start | bytes 786440 | tf_op jit(solution)/shard_map/ppermute | solution.py:392
  69.0 4.0 %collective-permute-start.1 = (f32[64,128]{1,0:T(8,128)S(1)}, f32[64,128]{1,0:T(8,128)S(1)}, u32[]{:S(2)}, u32[]{:S(2)}) collective-permute-start(f32[64,128]{1,0:T(8,128)S(1)} %shard_map.90), channel_id=1, source_target_pairs={{0,32},{1,33},{2,34},{3,35},{4,36},{5,37},{6,38},{7,39},{8,40},{9,... | collective-permute-start | bytes 98312 | tf_op jit(solution)/shard_map/ppermute | solution.py:400
  73.0 5.1 %collective-permute-start.2 = (f32[64,128]{1,0:T(8,128)S(1)}, f32[64,128]{1,0:T(8,128)S(1)}, u32[]{:S(2)}, u32[]{:S(2)}) collective-permute-start(f32[64,128]{1,0:T(8,128)S(1)} %add.16), channel_id=1, source_target_pairs={{0,96},{1,97},{2,98},{3,99},{4,100},{5,101},{6,102},{7,103},{8,104... | collective-permute-start | bytes 98312 | tf_op jit(solution)/shard_map/ppermute | solution.py:400
  78.3 9.8 %collective-permute-start.5 = (f32[576,128]{1,0:T(8,128)S(1)}, f32[576,128]{1,0:T(8,128)S(1)}, u32[]{:S(2)}, u32[]{:S(2)}) collective-permute-start(f32[576,128]{1,0:T(8,128)S(1)} %get-tuple-element.96), channel_id=1, source_target_pairs={{0,12},{1,13},{2,14},{3,15},{4,8},{5,9},{6,10},{7,11},{8,4},{9,5},... | collective-permute-start | bytes 884744 | tf_op jit(solution)/shard_map/ppermute | solution.py:400
  80.3 7.9 %collective-permute-start.6 = (f32[576,128]{1,0:T(8,128)S(1)}, f32[576,128]{1,0:T(8,128)S(1)}, u32[]{:S(2)}, u32[]{:S(2)}) collective-permute-start(f32[576,128]{1,0:T(8,128)S(1)} %get-tuple-element.98), channel_id=1, source_target_pairs={{0,4},{1,5},{2,6},{3,7},{4,0},{5,1},{6,2},{7,3},{8,12},{9,13},{10,... | collective-permute-start | bytes 884744 | tf_op jit(solution)/shard_map/ppermute | solution.py:400
  80.9 7.3 %collective-permute-start.10 = (f32[64,1024]{1,0:T(8,128)S(1)}, f32[64,1024]{1,0:T(8,128)S(1)}, u32[]{:S(2)}, u32[]{:S(2)}) collective-permute-start(f32[64,1024]{1,0:T(8,128)S(1)} %add.15.mine), channel_id=1, source_target_pairs={{0,32},{1,33},{2,34},{3,35},{4,36},{5,37},{6,38},{7,39},{8,40},{9,... | collective-permute-start | bytes 786440 | tf_op jit(solution)/shard_map/ppermute | solution.py:400
  80.9 7.3 %collective-permute-start.7 = (f32[64,128]{1,0:T(8,128)S(1)}, f32[64,128]{1,0:T(8,128)S(1)}, u32[]{:S(2)}, u32[]{:S(2)}) collective-permute-start(f32[64,128]{1,0:T(8,128)S(1)} %add.17.moment), channel_id=1, source_target_pairs={{0,8},{1,9},{2,10},{3,11},{4,12},{5,13},{6,14},{7,15},{8,0},{9,1},... | collective-permute-start | bytes 98312 | tf_op jit(solution)/shard_map/ppermute | solution.py:400
  88.2 7.9 %collective-permute-start.11 = (f32[64,1024]{1,0:T(8,128)S(1)}, f32[64,1024]{1,0:T(8,128)S(1)}, u32[]{:S(2)}, u32[]{:S(2)}) collective-permute-start(f32[64,1024]{1,0:T(8,128)S(1)} %add.18), channel_id=1, source_target_pairs={{0,96},{1,97},{2,98},{3,99},{4,100},{5,101},{6,102},{7,103},{8,104... | collective-permute-start | bytes 786440 | tf_op jit(solution)/shard_map/ppermute | solution.py:400
  89.5 6.6 %collective-permute-start.8 = (f32[320,128]{1,0:T(8,128)S(1)}, f32[320,128]{1,0:T(8,128)S(1)}, u32[]{:S(2)}, u32[]{:S(2)}) collective-permute-start(f32[320,128]{1,0:T(8,128)S(1)} %get-tuple-element.102.sent_a), channel_id=1, source_target_pairs={{0,1},{1,0},{2,3},{3,2},{4,5},{5,4},{6,7},{7,6},{8,9},{9,8},{10,11... | collective-permute-start | bytes 491528 | tf_op jit(solution)/shard_map/ppermute | solution.py:400
  89.9 6.2 %collective-permute-start.9 = (f32[256,128]{1,0:T(8,128)S(1)}, f32[256,128]{1,0:T(8,128)S(1)}, u32[]{:S(2)}, u32[]{:S(2)}) collective-permute-start(f32[256,128]{1,0:T(8,128)S(1)} %get-tuple-element.104), channel_id=1, source_target_pairs={{0,3},{1,2},{2,1},{3,0},{4,7},{5,6},{6,5},{7,4},{8,11},{9,10},{10,... | collective-permute-start | bytes 393224 | tf_op jit(solution)/shard_map/ppermute | solution.py:400
  96.2 1.7 %collective-permute-start.12 = (f32[64,1024]{1,0:T(8,128)S(1)}, f32[64,1024]{1,0:T(8,128)S(1)}, u32[]{:S(2)}, u32[]{:S(2)}) collective-permute-start(f32[64,1024]{1,0:T(8,128)S(1)} %add.19.mine), channel_id=1, source_target_pairs={{0,16},{16,0},{32,48},{48,32},{64,80},{80,64},{96,112},{112,96},{1... | collective-permute-start | bytes 786440 | tf_op jit(solution)/shard_map/ppermute | solution.py:392
  96.3 5.9 %collective-permute-start.13 = (f32[192,128]{1,0:T(8,128)S(1)}, f32[192,128]{1,0:T(8,128)S(1)}, u32[]{:S(2)}, u32[]{:S(2)}) collective-permute-start(f32[192,128]{1,0:T(8,128)S(1)} %get-tuple-element.113.sent), channel_id=1, source_target_pairs={{0,3},{1,2},{2,1},{3,0},{4,7},{5,6},{6,5},{7,4},{8,11},{9,10},{10,... | collective-permute-start | bytes 294920 | tf_op jit(solution)/shard_map/ppermute | solution.py:400
  97.9 4.3 %collective-permute-start.14 = (f32[128,128]{1,0:T(8,128)S(1)}, f32[128,128]{1,0:T(8,128)S(1)}, u32[]{:S(2)}, u32[]{:S(2)}) collective-permute-start(f32[128,128]{1,0:T(8,128)S(1)} %get-tuple-element.112), channel_id=1, source_target_pairs={{0,1},{1,0},{2,3},{3,2},{4,5},{5,4},{6,7},{7,6},{8,9},{9,8},{10,11... | collective-permute-start | bytes 196616 | tf_op jit(solution)/shard_map/ppermute | solution.py:400
  102.2 1.2 %collective-permute-start.15 = (f32[64,128]{1,0:T(8,128)S(1)}, f32[64,128]{1,0:T(8,128)S(1)}, u32[]{:S(2)}, u32[]{:S(2)}) collective-permute-start(f32[64,128]{1,0:T(8,128)S(1)} %shard_map.96.mine), channel_id=1, source_target_pairs={{0,16},{16,0},{32,48},{48,32},{64,80},{80,64},{96,112},{112,96},{1... | collective-permute-start | bytes 98312 | tf_op jit(solution)/shard_map/ppermute | solution.py:392

commit v7 on v6

--- a/solution.py
+++ b/solution.py
@@ -319,38 +319,31 @@
         send[512:, :] = moment[...]
 
 
-def merge_second(hold_a, got_a, hold_b, got_b, moment, across, send_a, next_a, send_b, next_b):
-    for half, (hold, got, send, after) in enumerate(
-        ((hold_a, got_a, send_a, next_a), (hold_b, got_b, send_b, next_b))
-    ):
-        for out, offsets in ((send, SEND[half]), (after, STAY[half])):
-            for k, minor in enumerate(offsets):
-                rows = slice(minor * 128, (minor + 1) * 128)
-                out[k * 128 : (k + 1) * 128, :] = hold[rows, :] + got[rows, :]
-    send_a[256:, :] = (moment[...] + got_b[512:, :]) + (across[...] + got_a[512:, :])
-
-
-def merge_third(hold_a, sent_a, got_a, hold_b, got_b, send_a, next_a, send_b, next_b):
-    for hold, got, send, after in ((hold_a, got_a, send_a, next_a), (hold_b, got_b, send_b, next_b)):
-        after[...] = hold[:128, :] + got[:128, :]
-        send[:128, :] = hold[128:, :] + got[128:256, :]
-    send_a[128:, :] = sent_a[256:, :] + got_a[256:, :]
-
-
-def merge_moment(sent, got, out):
-    out[...] = sent[128:, :] + got[128:, :]
-
-
-def merge_last(hold_a, got_a, hold_b, got_b, bary):
-    bary[:128, :] = (hold_a[...] + got_a[:128, :]).T.astype(BF16)
-    bary[128:, :] = (hold_b[...] + got_b[...]).T.astype(BF16)
+def merge_second(hold_a, got_a, hold_b, got_b, moment, across, send_1, send_2, send_3, stay):
+    total = (moment[...] + got_b[512:, :]) + (across[...] + got_a[512:, :])
+    for minor, out in enumerate((stay, send_1, send_2, send_3)):
+        rows = slice(minor * 128, (minor + 1) * 128)
+        out[:128, :] = hold_a[rows, :] + got_a[rows, :]
+        out[128:256, :] = hold_b[rows, :] + got_b[rows, :]
+        out[256:, :] = total
+
+
+def merge_moment(stay, got_1, got_2, got_3, out):
+    out[...] = (stay[256:, :] + got_1[256:, :]) + (got_2[256:, :] + got_3[256:, :])
+
+
+def merge_last(stay, got_1, got_2, got_3, bary):
+    for half in range(2):
+        rows = slice(half * 128, (half + 1) * 128)
+        x = (stay[rows, :] + got_1[rows, :]) + (got_2[rows, :] + got_3[rows, :])
+        bary[rows, :] = x.T.astype(BF16)
 
 
 def finish_moment(mine, other, out):
     out[...] = in_order(mine[...], other[...])
 
 
-def call(body, outs, *args, scratch=(), spaces=None):
+def call(body, outs, *args, scratch=(), spaces=None, flops=1):
     spaces = spaces or {}
     return pl.pallas_call(
         body,
@@ -358,7 +351,7 @@
         in_specs=[pl.BlockSpec(memory_space=spaces.get(i, pltpu.VMEM)) for i in range(len(args))],
         out_specs=jax.tree.map(lambda _: pl.BlockSpec(memory_space=pltpu.VMEM), outs),
         scratch_shapes=list(scratch),
-        cost_estimate=pl.CostEstimate(flops=1, bytes_accessed=1, transcendentals=0),
+        cost_estimate=pl.CostEstimate(flops=flops, bytes_accessed=1, transcendentals=0),
         compiler_params=pltpu.CompilerParams(vmem_limit_bytes=VMEM_LIMIT),
     )(*args)
 
@@ -404,6 +397,9 @@
 
     def minor(x, k):
         return by_core(x, lambda c, y, z, w: (y, z ^ k, w) if c else (y, z, w ^ k))
+
+    def opposite_y(x):
+        return by_core(x, lambda c, y, z, w: (y ^ 2, z, w))
 
     def along_y(x, k):
         return by_core(x, lambda c, y, z, w: (y ^ k ^ 2 * c, z, w))
@@ -446,46 +442,43 @@
         scratch=[pltpu.VMEM((width + 16, cols), F32)],
     )
     parts = exchange(sums, "row")
+    parts, send = lax.optimization_barrier((parts, send))
+    other = swap(send)
     message = f32(8 * width, share // 2)
     send_a, send_b, left, col_potential, gain = call(
         functools.partial(target_send, **counts),
         [message, message, bf16(width, cols), f32(*col_shape), f32(*col_shape)],
         parts, weight, before, tgt_t, near(kernel_t), scale,
+        flops=4 * width * cols * rows,
     )
     got_a, got_b = major(send_a, 1), major(send_b, 3)
     keep_a, keep_b = call(
         functools.partial(target_keep, src_count=src_count), [message, message], left, near(kernel_t), scale
     )
-    send, _ = lax.optimization_barrier((send, left))
-    mine = keep + swap(send)
+    mine = keep + other
     moment, = call(moment_half, [f32(width // 2, width)], mine, gain, tgt_emb)
-    moment = moment + along_y(moment, 1)
-    moment = moment + along_y(moment, 3)
+    mine, moment = lax.optimization_barrier((mine, moment))
+    rest = along_y(mine, 1)
+    moment = (moment + along_y(moment, 1)) + (opposite_y(moment) + along_y(moment, 3))
     keep_a, moment, mine = lax.optimization_barrier((keep_a, moment, mine))
     both = [f32(576, 128), f32(512, 128)] * 2
     send_a, hold_a, send_b, hold_b = call(merge_first, both, keep_a, got_a, keep_b, got_b, moment)
     got_a, got_b, across = major(send_a, 3), major(send_b, 1), major(moment, 2)
     hold_a, mine = lax.optimization_barrier((hold_a, mine))
-    rest = along_y(mine, 1)
-    both = [f32(320, 128), f32(256, 128), f32(256, 128), f32(256, 128)]
-    send_a, hold_a, send_b, hold_b = call(merge_second, both, hold_a, got_a, hold_b, got_b, moment, across)
-    sent_a = send_a
-    got_a, got_b = minor(send_a, 1), minor(send_b, 3)
-    hold_a, mine = lax.optimization_barrier((hold_a, mine))
     mine = mine + rest
     rest = along_y(mine, 3)
-    both = [f32(192, 128), f32(128, 128), f32(128, 128), f32(128, 128)]
-    send_a, hold_a, send_b, hold_b = call(merge_third, both, hold_a, sent_a, got_a, hold_b, got_b)
-    got_a, got_b = minor(send_a, 3), minor(send_b, 1)
-    hold_a, mine = lax.optimization_barrier((hold_a, mine))
+    sends = call(merge_second, [f32(320, 128)] * 4, hold_a, got_a, hold_b, got_b, moment, across)
+    stay = sends[3]
+    got = [minor(sends[0], 1), minor(sends[1], 2), minor(sends[2], 3)]
+    stay, mine = lax.optimization_barrier((stay, mine))
     mine = mine + rest
     bary_tgt, = call(
         functools.partial(finish_sources, tgt_count=tgt_count), [bf16(cols, width)], mine, swap(mine), gain
     )
-    hold_a, send_a, bary_tgt = lax.optimization_barrier((hold_a, send_a, bary_tgt))
-    moment, = call(merge_moment, [f32(width // 2, width)], send_a, got_a)
+    stay, bary_tgt = lax.optimization_barrier((stay, bary_tgt))
+    moment, = call(merge_moment, [f32(width // 2, width)], stay, *got)
     other = swap(moment)
-    bary_src, = call(merge_last, [bf16(share, width)], hold_a, got_a, hold_b, got_b)
+    bary_src, = call(merge_last, [bf16(share, width)], stay, *got)
     bary_src, moment = lax.optimization_barrier((bary_src, moment))
     moment, = call(finish_moment, [f32(width, width)], moment, other)
     return (bary_src, bary_tgt, moment, row_potential.reshape(rows), col_potential.reshape(cols))

time: 106 us -> 102 us (0.962)
  waiting for transfers between devices: 27.7 us -> 20 us
  starting transfers between devices: 21 us -> 24.9 us
    ppermute x13, waiting for transfers between devices: 19.7 us -> 12.1 us  [by_core(): return lax.ppermute(x, ('row', 'col'), pairs)]
    ppermute x13, starting transfers between devices: 12.9 us -> 16.7 us  [by_core(): return lax.ppermute(x, ('row', 'col'), pairs)]
    pallas_call x15 -> x14, Pallas kernels: 23.1 us -> 23.1 us  [call(): pl.pallas_call(body, out_shape=outs, in_specs=[pl.BlockSpec(memory_space=...]
  transfers between devices with their start and end apart: 17 -> 17, of which waited for: 8 -> 11; matrix products, arithmetic and copies ran while one was open for 0% -> 0% of each run, Pallas kernels for 3% -> 3%
where the time goes in v7:
time: 102 us; the launch traced here: 100 us
  blocking collectives  29.1 us (29%)
  starting transfers between devices  24.9 us (24%)
  Pallas kernels  23.1 us (23%)
  waiting for transfers between devices  20 us (20%)
  local copies, waits for them, and re-layouts  2.17 us (2%)
    all_to_all x3, blocking collectives, exchange(): return lax.all_to_all(x, axis, 0, 0)  29.1 us
    pallas_call x14, Pallas kernels, call(): pl.pallas_call(body, out_shape=outs, in_specs=[pl.BlockSpec(memory_space=...  23.1 us
    ppermute x13, starting transfers between devices, by_core(): return lax.ppermute(x, ('row', 'col'), pairs)  16.7 us
    ppermute x13, waiting for transfers between devices, by_core(): return lax.ppermute(x, ('row', 'col'), pairs)  12.1 us
    all_to_all x1, starting transfers between devices, exchange(): return lax.all_to_all(x, axis, 0, 0)  7.97 us
    all_to_all x1, waiting for transfers between devices, exchange(): return lax.all_to_all(x, axis, 0, 0)  6 us
    unnamed x6, local copies, waits for them, and re-layouts  2.17 us
  transfers between devices with their start and end apart: 17, of which 11 were waited for; matrix products, arithmetic and copies ran while one was open for 0% of the time, Pallas kernels for 3%

profile of v7, /device:TPU:0, one launch (start us, length us, event | category | flops | bytes accessed | tf_op | source)
XLA Modules:
  0.0 100.1 jit_solution(6857442873460911936)
XLA Ops:
  0.6 10.3 %shard_map.83 = (f32[16,32,128]{2,1,0:T(8,128)}, bf16[128,4096]{1,0:T(8,128)(2,1)S(1)}, bf16[1024,256]{1,0:T(8,128)(2,1)S(1)}, f32[8,128]{1,0:T(8,128)S(1)}) custom-call(bf16[4096,128]{1,0:T(8,128)(2,1)} %src, bf16[1024,128]{1,0:T(8,128)(2,1)} %tgt.2, bf16[128,128]{1,0:T(8,128)(2,1)} %factor_in.1, f32[8,128]{1,0:T(8,128)} %bitcast.3), custom_call_target="tpu_custom_call" | custom-call | flops 1 | bytes 1 | tf_op jit(solution)/shard_map/pallas_call | solution.py:348
  11.0 8.0 %all-to-all-start = ((f32[16,32,128]{2,1,0:T(8,128)}), f32[16,32,128]{2,1,0:T(8,128)S(1)}, u32[]{:S(2)}, u32[]{:S(2)}) async-start(f32[16,32,128]{2,1,0:T(8,128)} %get-tuple-element.58), calls=%async_computation | async-start | bytes 524288 | tf_op jit(solution)/shard_map/all_to_all | solution.py:408
  19.0 1.2 %copy-done = bf16[4096,128]{1,0:T(8,128)(2,1)S(1)} copy-done((bf16[4096,128]{1,0:T(8,128)(2,1)S(1)}, bf16[4096,128]{1,0:T(8,128)(2,1)}, u32[]{:S(2)}) %copy-start) | copy-done | bytes 1048600
  20.2 0.9 copy-done.1
  21.6 6.0 %all-to-all-done.parts = f32[16,32,128]{2,1,0:T(8,128)S(1)} async-done(((f32[16,32,128]{2,1,0:T(8,128)}), f32[16,32,128]{2,1,0:T(8,128)S(1)}, u32[]{:S(2)}, u32[]{:S(2)}) %all-to-all-start) | async-done | bytes 262176 | tf_op jit(solution)/shard_map/all_to_all | solution.py:408
  27.6 2.9 %shard_map.85 = (bf16[32,1024,128]{2,1,0:T(8,128)(2,1)S(1)}, f32[8,8,128]{2,1,0:T(8,128)S(1)}, f32[8,128]{1,0:T(8,128)S(1)}, f32[32,128]{1,0:T(8,128)S(1)}) custom-call(f32[16,32,128]{2,1,0:T(8,128)S(1)} %all-to-all-done.parts, bf16[128,4096]{1,0:T(8,128)(2,1)S(1)} %get-tuple-element.59.proj_t, bf16[1024,256]{1,0:T(8,128)(2,1)S(1)} %get-tuple-element.65.aug, ...), custom_call_target="tpu_custom_call" | custom-call | flops 1 | bytes 1 | tf_op jit(solution)/shard_map/pallas_call | solution.py:348
  30.5 9.7 %all_to_all.20.parts = f32[8,8,128]{2,1,0:T(8,128)S(1)} all-to-all(f32[8,8,128]{2,1,0:T(8,128)S(1)} %get-tuple-element.67), channel_id=1, replica_groups=mesh['row'=8,'col'=16] {'row'}, dimensions={0} | all-to-all | bytes 65536 | tf_op jit(solution)/shard_map/all_to_all | solution.py:408
  40.2 1.2 %shard_map.86 = (f32[16,32,128]{2,1,0:T(8,128)S(1)}, f32[8,128]{1,0:T(8,128)S(1)}, f32[8,128]{1,0:T(8,128)S(1)}) custom-call(f32[8,8,128]{2,1,0:T(8,128)S(1)} %all_to_all.20.parts, f32[8,128]{1,0:T(8,128)S(1)} %get-tuple-element.68.shift, bf16[32,1024,128]{2,1,0:T(8,128)(2,1)S(1)} %get-tuple-element.69.kernel_t), custom_call_target="tpu_custom_call" | custom-call | flops 1 | bytes 1 | tf_op jit(solution)/shard_map/pallas_call | solution.py:348
  41.5 11.6 %all_to_all.21.parts = f32[16,32,128]{2,1,0:T(8,128)S(1)} all-to-all(f32[16,32,128]{2,1,0:T(8,128)S(1)} %get-tuple-element.70), channel_id=1, replica_groups=mesh['row'=8,'col'=16] {'col'}, dimensions={0} | all-to-all | bytes 524288 | tf_op jit(solution)/shard_map/all_to_all | solution.py:408
  53.1 3.4 %shard_map.87 = (f32[8,8,128]{2,1,0:T(8,128)S(1)}, f32[64,1024]{1,0:T(8,128)S(1)}, f32[64,1024]{1,0:T(8,128)S(1)}, f32[32,128]{1,0:T(8,128)S(1)}, f32[32,128]{1,0:T(8,128)}) custom-call(f32[16,32,128]{2,1,0:T(8,128)S(1)} %all_to_all.21.parts, f32[32,128]{1,0:T(8,128)S(1)} %get-tuple-element.71.rho, bf16[32,1024,128]{2,1,0:T(8,128)(2,1)S(1)} %get-tuple-element.69.kernel_t, ...), custom_call_target="tpu_custom_call" | custom-call | flops 1 | bytes 1 | tf_op jit(solution)/shard_map/pallas_call | solution.py:348
  56.5 7.8 %all_to_all.22.parts = f32[8,8,128]{2,1,0:T(8,128)S(1)} all-to-all(f32[8,8,128]{2,1,0:T(8,128)S(1)} %get-tuple-element.74), channel_id=1, replica_groups=mesh['row'=8,'col'=16] {'row'}, dimensions={0} | all-to-all | bytes 65536 | tf_op jit(solution)/shard_map/all_to_all | solution.py:408
  64.3 1.2 %shard_map.88 = (f32[1024,128]{1,0:T(8,128)S(1)}, f32[1024,128]{1,0:T(8,128)S(1)}, bf16[128,1024]{1,0:T(8,128)(2,1)S(1)}, f32[8,128]{1,0:T(8,128)}, f32[8,128]{1,0:T(8,128)S(1)}) custom-call(f32[8,8,128]{2,1,0:T(8,128)S(1)} %all_to_all.22.parts, f32[8,128]{1,0:T(8,128)S(1)} %get-tuple-element.73.weight, f32[8,128]{1,0:T(8,128)S(1)} %get-tuple-element.77.before, ...), custom_call_target="tpu_custom_call" | custom-call | flops 2147483648 | bytes 1 | tf_op jit(solution)/shard_map/pallas_call | solution.py:348
  65.7 1.3 %collective-permute-start.5 = (f32[1024,128]{1,0:T(8,128)S(1)}, f32[1024,128]{1,0:T(8,128)S(1)}, u32[]{:S(2)}, u32[]{:S(2)}) collective-permute-start(f32[1024,128]{1,0:T(8,128)S(1)} %get-tuple-element.90), channel_id=1, source_target_pairs={{0,12},{1,13},{2,14},{3,15},{4,8},{5,9},{6,10},{7,11},{8,4},{9,5},... | collective-permute-start | bytes 1572872 | tf_op jit(solution)/shard_map/ppermute | solution.py:393
  67.1 1.5 %collective-permute-done = f32[64,1024]{1,0:T(8,128)S(1)} collective-permute-done((f32[64,1024]{1,0:T(8,128)S(1)}, f32[64,1024]{1,0:T(8,128)S(1)}, u32[]{:S(2)}, u32[]{:S(2)}) %collective-permute-start) | collective-permute-done | bytes 262176 | tf_op jit(solution)/shard_map/ppermute | solution.py:385
  69.0 1.2 %collective-permute-start.3 = (f32[64,128]{1,0:T(8,128)S(1)}, f32[64,128]{1,0:T(8,128)S(1)}, u32[]{:S(2)}, u32[]{:S(2)}) collective-permute-start(f32[64,128]{1,0:T(8,128)S(1)} %shard_map.90), channel_id=1, source_target_pairs={{0,96},{1,97},{2,98},{3,99},{4,100},{5,101},{6,102},{7,103},{8,104... | collective-permute-start | bytes 98312 | tf_op jit(solution)/shard_map/ppermute | solution.py:393
  70.3 1.5 %collective-permute-start.2 = (f32[64,128]{1,0:T(8,128)S(1)}, f32[64,128]{1,0:T(8,128)S(1)}, u32[]{:S(2)}, u32[]{:S(2)}) collective-permute-start(f32[64,128]{1,0:T(8,128)S(1)} %shard_map.90), channel_id=1, source_target_pairs={{0,64},{1,65},{2,66},{3,67},{4,68},{5,69},{6,70},{7,71},{8,72},{9,... | collective-permute-start | bytes 98312 | tf_op jit(solution)/shard_map/ppermute | solution.py:393
  71.7 1.5 %collective-permute-start.1 = (f32[64,128]{1,0:T(8,128)S(1)}, f32[64,128]{1,0:T(8,128)S(1)}, u32[]{:S(2)}, u32[]{:S(2)}) collective-permute-start(f32[64,128]{1,0:T(8,128)S(1)} %shard_map.90), channel_id=1, source_target_pairs={{0,32},{1,33},{2,34},{3,35},{4,36},{5,37},{6,38},{7,39},{8,40},{9,... | collective-permute-start | bytes 98312 | tf_op jit(solution)/shard_map/ppermute | solution.py:393
  73.2 1.1 %collective-permute-done.3 = f32[64,128]{1,0:T(8,128)S(1)} collective-permute-done((f32[64,128]{1,0:T(8,128)S(1)}, f32[64,128]{1,0:T(8,128)S(1)}, u32[]{:S(2)}, u32[]{:S(2)}) %collective-permute-start.3) | collective-permute-done | bytes 32800 | tf_op jit(solution)/shard_map/ppermute | solution.py:393
  74.3 0.7 shard_map.89
  75.1 0.7 collective-permute-done.2
  76.2 1.7 %collective-permute-start.6 = (f32[576,128]{1,0:T(8,128)S(1)}, f32[576,128]{1,0:T(8,128)S(1)}, u32[]{:S(2)}, u32[]{:S(2)}) collective-permute-start(f32[576,128]{1,0:T(8,128)S(1)} %get-tuple-element.95), channel_id=1, source_target_pairs={{0,12},{1,13},{2,14},{3,15},{4,8},{5,9},{6,10},{7,11},{8,4},{9,5},... | collective-permute-start | bytes 884744 | tf_op jit(solution)/shard_map/ppermute | solution.py:393
  78.5 2.2 %collective-permute-done.9 = f32[64,1024]{1,0:T(8,128)S(1)} collective-permute-done((f32[64,1024]{1,0:T(8,128)S(1)}, f32[64,1024]{1,0:T(8,128)S(1)}, u32[]{:S(2)}, u32[]{:S(2)}) %collective-permute-start.9) | collective-permute-done | bytes 262176 | tf_op jit(solution)/shard_map/ppermute | solution.py:393
  80.7 1.3 %collective-permute-start.10 = (f32[64,1024]{1,0:T(8,128)S(1)}, f32[64,1024]{1,0:T(8,128)S(1)}, u32[]{:S(2)}, u32[]{:S(2)}) collective-permute-start(f32[64,1024]{1,0:T(8,128)S(1)} %add.22), channel_id=1, source_target_pairs={{0,96},{1,97},{2,98},{3,99},{4,100},{5,101},{6,102},{7,103},{8,104... | collective-permute-start | bytes 786440 | tf_op jit(solution)/shard_map/ppermute | solution.py:393
  82.0 2.5 %collective-permute-start.8 = (f32[64,128]{1,0:T(8,128)S(1)}, f32[64,128]{1,0:T(8,128)S(1)}, u32[]{:S(2)}, u32[]{:S(2)}) collective-permute-start(f32[64,128]{1,0:T(8,128)S(1)} %add_add_fusion.moment), channel_id=1, source_target_pairs={{0,8},{1,9},{2,10},{3,11},{4,12},{5,13},{6,14},{7,15},{8,0},{9,1},... | collective-permute-start | bytes 98312 | tf_op jit(solution)/shard_map/ppermute | solution.py:393
  84.6 2.9 %collective-permute-done.8.across = f32[64,128]{1,0:T(8,128)S(1)} collective-permute-done((f32[64,128]{1,0:T(8,128)S(1)}, f32[64,128]{1,0:T(8,128)S(1)}, u32[]{:S(2)}, u32[]{:S(2)}) %collective-permute-start.8) | collective-permute-done | bytes 32800 | tf_op jit(solution)/shard_map/ppermute | solution.py:393
  87.5 0.9 collective-permute-done.10
  89.0 2.4 %collective-permute-start.13 = (f32[320,128]{1,0:T(8,128)S(1)}, f32[320,128]{1,0:T(8,128)S(1)}, u32[]{:S(2)}, u32[]{:S(2)}) collective-permute-start(f32[320,128]{1,0:T(8,128)S(1)} %get-tuple-element.104), channel_id=1, source_target_pairs={{0,2},{1,3},{2,0},{3,1},{4,6},{5,7},{6,4},{7,5},{8,10},{9,11},{10,... | collective-permute-start | bytes 491528 | tf_op jit(solution)/shard_map/ppermute | solution.py:393
  91.4 1.9 %collective-permute-start.14 = (f32[320,128]{1,0:T(8,128)S(1)}, f32[320,128]{1,0:T(8,128)S(1)}, u32[]{:S(2)}, u32[]{:S(2)}) collective-permute-start(f32[320,128]{1,0:T(8,128)S(1)} %get-tuple-element.105), channel_id=1, source_target_pairs={{0,3},{1,2},{2,1},{3,0},{4,7},{5,6},{6,5},{7,4},{8,11},{9,10},{10,... | collective-permute-start | bytes 491528 | tf_op jit(solution)/shard_map/ppermute | solution.py:393
  93.3 0.9 shard_map.93
  94.2 2.3 %collective-permute-done.13.got_2 = f32[320,128]{1,0:T(8,128)S(1)} collective-permute-done((f32[320,128]{1,0:T(8,128)S(1)}, f32[320,128]{1,0:T(8,128)S(1)}, u32[]{:S(2)}, u32[]{:S(2)}) %collective-permute-start.13) | collective-permute-done | bytes 163872 | tf_op jit(solution)/shard_map/ppermute | solution.py:393
  96.5 1.7 %collective-permute-done.14.got_3 = f32[320,128]{1,0:T(8,128)S(1)} collective-permute-done((f32[320,128]{1,0:T(8,128)S(1)}, f32[320,128]{1,0:T(8,128)S(1)}, u32[]{:S(2)}, u32[]{:S(2)}) %collective-permute-start.14) | collective-permute-done | bytes 163872 | tf_op jit(solution)/shard_map/ppermute | solution.py:393
  98.4 0.7 shard_map.94
  (29 shorter events, 4.1 us)
Async XLA Ops:
  11.0 16.7 %all-to-all-start = ((f32[16,32,128]{2,1,0:T(8,128)}), f32[16,32,128]{2,1,0:T(8,128)S(1)}, u32[]{:S(2)}, u32[]{:S(2)}) async-start(f32[16,32,128]{2,1,0:T(8,128)} %get-tuple-element.58), calls=%async_computation | async-start | bytes 524288 | tf_op jit(solution)/shard_map/all_to_all | solution.py:408
  19.0 1.2 %copy-start = (bf16[4096,128]{1,0:T(8,128)(2,1)S(1)}, bf16[4096,128]{1,0:T(8,128)(2,1)}, u32[]{:S(2)}) copy-start(bf16[4096,128]{1,0:T(8,128)(2,1)} %src) | copy-start | bytes 3145732
  20.2 0.9 copy-start.1
  53.1 15.5 %copy-start.2 = (bf16[1024,128]{1,0:T(8,128)(2,1)S(1)}, bf16[1024,128]{1,0:T(8,128)(2,1)}, u32[]{:S(2)}) copy-start(bf16[1024,128]{1,0:T(8,128)(2,1)} %tgt.2) | copy-start | bytes 786436
  65.5 10.3 %collective-permute-start.4 = (f32[1024,128]{1,0:T(8,128)S(1)}, f32[1024,128]{1,0:T(8,128)S(1)}, u32[]{:S(2)}, u32[]{:S(2)}) collective-permute-start(f32[1024,128]{1,0:T(8,128)S(1)} %get-tuple-element.88), channel_id=1, source_target_pairs={{0,4},{1,5},{2,6},{3,7},{4,0},{5,1},{6,2},{7,3},{8,12},{9,13},{10,... | collective-permute-start | bytes 1572872 | tf_op jit(solution)/shard_map/ppermute | solution.py:393
  65.7 10.4 %collective-permute-start.5 = (f32[1024,128]{1,0:T(8,128)S(1)}, f32[1024,128]{1,0:T(8,128)S(1)}, u32[]{:S(2)}, u32[]{:S(2)}) collective-permute-start(f32[1024,128]{1,0:T(8,128)S(1)} %get-tuple-element.90), channel_id=1, source_target_pairs={{0,12},{1,13},{2,14},{3,15},{4,8},{5,9},{6,10},{7,11},{8,4},{9,5},... | collective-permute-start | bytes 1572872 | tf_op jit(solution)/shard_map/ppermute | solution.py:393
  67.0 1.5 %collective-permute-start = (f32[64,1024]{1,0:T(8,128)S(1)}, f32[64,1024]{1,0:T(8,128)S(1)}, u32[]{:S(2)}, u32[]{:S(2)}) collective-permute-start(f32[64,1024]{1,0:T(8,128)S(1)} %get-tuple-element.83), channel_id=1, source_target_pairs={{0,16},{16,0},{32,48},{48,32},{64,80},{80,64},{96,112},{112,96},{1... | collective-permute-start | bytes 786440 | tf_op jit(solution)/shard_map/ppermute | solution.py:385
  69.0 5.3 %collective-permute-start.3 = (f32[64,128]{1,0:T(8,128)S(1)}, f32[64,128]{1,0:T(8,128)S(1)}, u32[]{:S(2)}, u32[]{:S(2)}) collective-permute-start(f32[64,128]{1,0:T(8,128)S(1)} %shard_map.90), channel_id=1, source_target_pairs={{0,96},{1,97},{2,98},{3,99},{4,100},{5,101},{6,102},{7,103},{8,104... | collective-permute-start | bytes 98312 | tf_op jit(solution)/shard_map/ppermute | solution.py:393
  70.3 5.5 %collective-permute-start.2 = (f32[64,128]{1,0:T(8,128)S(1)}, f32[64,128]{1,0:T(8,128)S(1)}, u32[]{:S(2)}, u32[]{:S(2)}) collective-permute-start(f32[64,128]{1,0:T(8,128)S(1)} %shard_map.90), channel_id=1, source_target_pairs={{0,64},{1,65},{2,66},{3,67},{4,68},{5,69},{6,70},{7,71},{8,72},{9,... | collective-permute-start | bytes 98312 | tf_op jit(solution)/shard_map/ppermute | solution.py:393
  71.7 4.1 %collective-permute-start.1 = (f32[64,128]{1,0:T(8,128)S(1)}, f32[64,128]{1,0:T(8,128)S(1)}, u32[]{:S(2)}, u32[]{:S(2)}) collective-permute-start(f32[64,128]{1,0:T(8,128)S(1)} %shard_map.90), channel_id=1, source_target_pairs={{0,32},{1,33},{2,34},{3,35},{4,36},{5,37},{6,38},{7,39},{8,40},{9,... | collective-permute-start | bytes 98312 | tf_op jit(solution)/shard_map/ppermute | solution.py:393
  74.3 6.4 %collective-permute-start.9 = (f32[64,1024]{1,0:T(8,128)S(1)}, f32[64,1024]{1,0:T(8,128)S(1)}, u32[]{:S(2)}, u32[]{:S(2)}) collective-permute-start(f32[64,1024]{1,0:T(8,128)S(1)} %add.18.mine), channel_id=1, source_target_pairs={{0,32},{1,33},{2,34},{3,35},{4,36},{5,37},{6,38},{7,39},{8,40},{9,... | collective-permute-start | bytes 786440 | tf_op jit(solution)/shard_map/ppermute | solution.py:393
  76.2 11.3 %collective-permute-start.6 = (f32[576,128]{1,0:T(8,128)S(1)}, f32[576,128]{1,0:T(8,128)S(1)}, u32[]{:S(2)}, u32[]{:S(2)}) collective-permute-start(f32[576,128]{1,0:T(8,128)S(1)} %get-tuple-element.95), channel_id=1, source_target_pairs={{0,12},{1,13},{2,14},{3,15},{4,8},{5,9},{6,10},{7,11},{8,4},{9,5},... | collective-permute-start | bytes 884744 | tf_op jit(solution)/shard_map/ppermute | solution.py:393
  77.9 9.5 %collective-permute-start.7 = (f32[576,128]{1,0:T(8,128)S(1)}, f32[576,128]{1,0:T(8,128)S(1)}, u32[]{:S(2)}, u32[]{:S(2)}) collective-permute-start(f32[576,128]{1,0:T(8,128)S(1)} %get-tuple-element.97), channel_id=1, source_target_pairs={{0,4},{1,5},{2,6},{3,7},{4,0},{5,1},{6,2},{7,3},{8,12},{9,13},{10,... | collective-permute-start | bytes 884744 | tf_op jit(solution)/shard_map/ppermute | solution.py:393
  80.7 7.7 %collective-permute-start.10 = (f32[64,1024]{1,0:T(8,128)S(1)}, f32[64,1024]{1,0:T(8,128)S(1)}, u32[]{:S(2)}, u32[]{:S(2)}) collective-permute-start(f32[64,1024]{1,0:T(8,128)S(1)} %add.22), channel_id=1, source_target_pairs={{0,96},{1,97},{2,98},{3,99},{4,100},{5,101},{6,102},{7,103},{8,104... | collective-permute-start | bytes 786440 | tf_op jit(solution)/shard_map/ppermute | solution.py:393
  82.0 5.4 %collective-permute-start.8 = (f32[64,128]{1,0:T(8,128)S(1)}, f32[64,128]{1,0:T(8,128)S(1)}, u32[]{:S(2)}, u32[]{:S(2)}) collective-permute-start(f32[64,128]{1,0:T(8,128)S(1)} %add_add_fusion.moment), channel_id=1, source_target_pairs={{0,8},{1,9},{2,10},{3,11},{4,12},{5,13},{6,14},{7,15},{8,0},{9,1},... | collective-permute-start | bytes 98312 | tf_op jit(solution)/shard_map/ppermute | solution.py:393
  88.4 4.9 %collective-permute-start.11 = (f32[64,1024]{1,0:T(8,128)S(1)}, f32[64,1024]{1,0:T(8,128)S(1)}, u32[]{:S(2)}, u32[]{:S(2)}) collective-permute-start(f32[64,1024]{1,0:T(8,128)S(1)} %add.23.mine), channel_id=1, source_target_pairs={{0,16},{16,0},{32,48},{48,32},{64,80},{80,64},{96,112},{112,96},{1... | collective-permute-start | bytes 786440 | tf_op jit(solution)/shard_map/ppermute | solution.py:385
  88.5 5.6 %collective-permute-start.12 = (f32[320,128]{1,0:T(8,128)S(1)}, f32[320,128]{1,0:T(8,128)S(1)}, u32[]{:S(2)}, u32[]{:S(2)}) collective-permute-start(f32[320,128]{1,0:T(8,128)S(1)} %get-tuple-element.103), channel_id=1, source_target_pairs={{0,1},{1,0},{2,3},{3,2},{4,5},{5,4},{6,7},{7,6},{8,9},{9,8},{10,11... | collective-permute-start | bytes 491528 | tf_op jit(solution)/shard_map/ppermute | solution.py:393
  89.0 7.4 %collective-permute-start.13 = (f32[320,128]{1,0:T(8,128)S(1)}, f32[320,128]{1,0:T(8,128)S(1)}, u32[]{:S(2)}, u32[]{:S(2)}) collective-permute-start(f32[320,128]{1,0:T(8,128)S(1)} %get-tuple-element.104), channel_id=1, source_target_pairs={{0,2},{1,3},{2,0},{3,1},{4,6},{5,7},{6,4},{7,5},{8,10},{9,11},{10,... | collective-permute-start | bytes 491528 | tf_op jit(solution)/shard_map/ppermute | solution.py:393
  91.4 6.8 %collective-permute-start.14 = (f32[320,128]{1,0:T(8,128)S(1)}, f32[320,128]{1,0:T(8,128)S(1)}, u32[]{:S(2)}, u32[]{:S(2)}) collective-permute-start(f32[320,128]{1,0:T(8,128)S(1)} %get-tuple-element.105), channel_id=1, source_target_pairs={{0,3},{1,2},{2,1},{3,0},{4,7},{5,6},{6,5},{7,4},{8,11},{9,10},{10,... | collective-permute-start | bytes 491528 | tf_op jit(solution)/shard_map/ppermute | solution.py:393
  98.2 1.3 %collective-permute-start.15 = (f32[64,128]{1,0:T(8,128)S(1)}, f32[64,128]{1,0:T(8,128)S(1)}, u32[]{:S(2)}, u32[]{:S(2)}) collective-permute-start(f32[64,128]{1,0:T(8,128)S(1)} %shard_map.95.mine), channel_id=1, source_target_pairs={{0,16},{16,0},{32,48},{48,32},{64,80},{80,64},{96,112},{112,96},{1... | collective-permute-start | bytes 98312 | tf_op jit(solution)/shard_map/ppermute | solution.py:385

commit v8 on v7

--- a/solution.py
+++ b/solution.py
@@ -457,15 +457,13 @@
     )
     mine = keep + other
     moment, = call(moment_half, [f32(width // 2, width)], mine, gain, tgt_emb)
-    mine, moment = lax.optimization_barrier((mine, moment))
-    rest = along_y(mine, 1)
+    mine = mine + along_y(mine, 1)
     moment = (moment + along_y(moment, 1)) + (opposite_y(moment) + along_y(moment, 3))
     keep_a, moment, mine = lax.optimization_barrier((keep_a, moment, mine))
     both = [f32(576, 128), f32(512, 128)] * 2
     send_a, hold_a, send_b, hold_b = call(merge_first, both, keep_a, got_a, keep_b, got_b, moment)
     got_a, got_b, across = major(send_a, 3), major(send_b, 1), major(moment, 2)
     hold_a, mine = lax.optimization_barrier((hold_a, mine))
-    mine = mine + rest
     rest = along_y(mine, 3)
     sends = call(merge_second, [f32(320, 128)] * 4, hold_a, got_a, hold_b, got_b, moment, across)
     stay = sends[3]

time: 102 us -> 100 us (0.980)
  waiting for transfers between devices: 20 us -> 18.6 us
    ppermute x3, waiting for transfers between devices: 1.89 us -> 0.4 us  [swap(): return lax.ppermute(x, 'row', [(i, i ^ 1) for i in range(row_size)])]
  transfers between devices with their start and end apart: 17 -> 17, of which waited for: 11 -> 8; matrix products, arithmetic and copies ran while one was open for 0% -> 0% of each run, Pallas kernels for 3% -> 5%
where the time goes in v8:
time: 100 us; the launch traced here: 99 us
  blocking collectives  29.1 us (29%)
  starting transfers between devices  25.1 us (25%)
  Pallas kernels  23.1 us (23%)
  waiting for transfers between devices  18.6 us (19%)
  local copies, waits for them, and re-layouts  2.17 us (2%)
    all_to_all x3, blocking collectives, exchange(): return lax.all_to_all(x, axis, 0, 0)  29.1 us
    pallas_call x14, Pallas kernels, call(): pl.pallas_call(body, out_shape=outs, in_specs=[pl.BlockSpec(memory_space=...  23.1 us
    ppermute x13, starting transfers between devices, by_core(): return lax.ppermute(x, ('row', 'col'), pairs)  16.9 us
    ppermute x13, waiting for transfers between devices, by_core(): return lax.ppermute(x, ('row', 'col'), pairs)  12.2 us
    all_to_all x1, starting transfers between devices, exchange(): return lax.all_to_all(x, axis, 0, 0)  7.97 us
    all_to_all x1, waiting for transfers between devices, exchange(): return lax.all_to_all(x, axis, 0, 0)  6 us
    unnamed x6, local copies, waits for them, and re-layouts  2.17 us
  transfers between devices with their start and end apart: 17, of which 8 were waited for; matrix products, arithmetic and copies ran while one was open for 0% of the time, Pallas kernels for 5%

profile of v8, /device:TPU:0, one launch (start us, length us, event | category | flops | bytes accessed | tf_op | source)
XLA Modules:
  0.0 99.0 jit_solution(7128318951109118427)
XLA Ops:
  0.6 10.3 %shard_map.83 = (f32[16,32,128]{2,1,0:T(8,128)}, bf16[128,4096]{1,0:T(8,128)(2,1)S(1)}, bf16[1024,256]{1,0:T(8,128)(2,1)S(1)}, f32[8,128]{1,0:T(8,128)S(1)}) custom-call(bf16[4096,128]{1,0:T(8,128)(2,1)} %src, bf16[1024,128]{1,0:T(8,128)(2,1)} %tgt.2, bf16[128,128]{1,0:T(8,128)(2,1)} %factor_in.1, f32[8,128]{1,0:T(8,128)} %bitcast.3), custom_call_target="tpu_custom_call" | custom-call | flops 1 | bytes 1 | tf_op jit(solution)/shard_map/pallas_call | solution.py:348
  11.0 8.0 %all-to-all-start = ((f32[16,32,128]{2,1,0:T(8,128)}), f32[16,32,128]{2,1,0:T(8,128)S(1)}, u32[]{:S(2)}, u32[]{:S(2)}) async-start(f32[16,32,128]{2,1,0:T(8,128)} %get-tuple-element.56), calls=%async_computation | async-start | bytes 524288 | tf_op jit(solution)/shard_map/all_to_all | solution.py:408
  19.0 1.2 %copy-done = bf16[4096,128]{1,0:T(8,128)(2,1)S(1)} copy-done((bf16[4096,128]{1,0:T(8,128)(2,1)S(1)}, bf16[4096,128]{1,0:T(8,128)(2,1)}, u32[]{:S(2)}) %copy-start) | copy-done | bytes 1048600
  20.2 0.9 copy-done.1
  21.1 0.5 shard_map.84
  21.6 6.0 %all-to-all-done.parts = f32[16,32,128]{2,1,0:T(8,128)S(1)} async-done(((f32[16,32,128]{2,1,0:T(8,128)}), f32[16,32,128]{2,1,0:T(8,128)S(1)}, u32[]{:S(2)}, u32[]{:S(2)}) %all-to-all-start) | async-done | bytes 262176 | tf_op jit(solution)/shard_map/all_to_all | solution.py:408
  27.6 2.9 %shard_map.85 = (bf16[32,1024,128]{2,1,0:T(8,128)(2,1)S(1)}, f32[8,8,128]{2,1,0:T(8,128)S(1)}, f32[8,128]{1,0:T(8,128)S(1)}, f32[32,128]{1,0:T(8,128)S(1)}) custom-call(f32[16,32,128]{2,1,0:T(8,128)S(1)} %all-to-all-done.parts, bf16[128,4096]{1,0:T(8,128)(2,1)S(1)} %get-tuple-element.57.proj_t, bf16[1024,256]{1,0:T(8,128)(2,1)S(1)} %get-tuple-element.63.aug, ...), custom_call_target="tpu_custom_call" | custom-call | flops 1 | bytes 1 | tf_op jit(solution)/shard_map/pallas_call | solution.py:348
  30.5 9.7 %all_to_all.20.parts = f32[8,8,128]{2,1,0:T(8,128)S(1)} all-to-all(f32[8,8,128]{2,1,0:T(8,128)S(1)} %get-tuple-element.65), channel_id=1, replica_groups=mesh['row'=8,'col'=16] {'row'}, dimensions={0} | all-to-all | bytes 65536 | tf_op jit(solution)/shard_map/all_to_all | solution.py:408
  40.2 1.2 %shard_map.86 = (f32[16,32,128]{2,1,0:T(8,128)S(1)}, f32[8,128]{1,0:T(8,128)S(1)}, f32[8,128]{1,0:T(8,128)S(1)}) custom-call(f32[8,8,128]{2,1,0:T(8,128)S(1)} %all_to_all.20.parts, f32[8,128]{1,0:T(8,128)S(1)} %get-tuple-element.66.shift, bf16[32,1024,128]{2,1,0:T(8,128)(2,1)S(1)} %get-tuple-element.67.kernel_t), custom_call_target="tpu_custom_call" | custom-call | flops 1 | bytes 1 | tf_op jit(solution)/shard_map/pallas_call | solution.py:348
  41.5 11.6 %all_to_all.21.parts = f32[16,32,128]{2,1,0:T(8,128)S(1)} all-to-all(f32[16,32,128]{2,1,0:T(8,128)S(1)} %get-tuple-element.68), channel_id=1, replica_groups=mesh['row'=8,'col'=16] {'col'}, dimensions={0} | all-to-all | bytes 524288 | tf_op jit(solution)/shard_map/all_to_all | solution.py:408
  53.1 3.4 %shard_map.87 = (f32[8,8,128]{2,1,0:T(8,128)S(1)}, f32[64,1024]{1,0:T(8,128)S(1)}, f32[64,1024]{1,0:T(8,128)S(1)}, f32[32,128]{1,0:T(8,128)S(1)}, f32[32,128]{1,0:T(8,128)}) custom-call(f32[16,32,128]{2,1,0:T(8,128)S(1)} %all_to_all.21.parts, f32[32,128]{1,0:T(8,128)S(1)} %get-tuple-element.69.rho, bf16[32,1024,128]{2,1,0:T(8,128)(2,1)S(1)} %get-tuple-element.67.kernel_t, ...), custom_call_target="tpu_custom_call" | custom-call | flops 1 | bytes 1 | tf_op jit(solution)/shard_map/pallas_call | solution.py:348
  56.5 7.8 %all_to_all.22.parts = f32[8,8,128]{2,1,0:T(8,128)S(1)} all-to-all(f32[8,8,128]{2,1,0:T(8,128)S(1)} %get-tuple-element.72), channel_id=1, replica_groups=mesh['row'=8,'col'=16] {'row'}, dimensions={0} | all-to-all | bytes 65536 | tf_op jit(solution)/shard_map/all_to_all | solution.py:408
  64.3 1.2 %shard_map.88 = (f32[1024,128]{1,0:T(8,128)S(1)}, f32[1024,128]{1,0:T(8,128)S(1)}, bf16[128,1024]{1,0:T(8,128)(2,1)S(1)}, f32[8,128]{1,0:T(8,128)}, f32[8,128]{1,0:T(8,128)S(1)}) custom-call(f32[8,8,128]{2,1,0:T(8,128)S(1)} %all_to_all.22.parts, f32[8,128]{1,0:T(8,128)S(1)} %get-tuple-element.71.weight, f32[8,128]{1,0:T(8,128)S(1)} %get-tuple-element.75.before, ...), custom_call_target="tpu_custom_call" | custom-call | flops 2147483648 | bytes 1 | tf_op jit(solution)/shard_map/pallas_call | solution.py:348
  65.7 1.3 %collective-permute-start.6 = (f32[1024,128]{1,0:T(8,128)S(1)}, f32[1024,128]{1,0:T(8,128)S(1)}, u32[]{:S(2)}, u32[]{:S(2)}) collective-permute-start(f32[1024,128]{1,0:T(8,128)S(1)} %get-tuple-element.86), channel_id=1, source_target_pairs={{0,12},{1,13},{2,14},{3,15},{4,8},{5,9},{6,10},{7,11},{8,4},{9,5},... | collective-permute-start | bytes 1572872 | tf_op jit(solution)/shard_map/ppermute | solution.py:393
  67.5 1.2 %collective-permute-start.3 = (f32[64,128]{1,0:T(8,128)S(1)}, f32[64,128]{1,0:T(8,128)S(1)}, u32[]{:S(2)}, u32[]{:S(2)}) collective-permute-start(f32[64,128]{1,0:T(8,128)S(1)} %shard_map.90), channel_id=1, source_target_pairs={{0,96},{1,97},{2,98},{3,99},{4,100},{5,101},{6,102},{7,103},{8,104... | collective-permute-start | bytes 98312 | tf_op jit(solution)/shard_map/ppermute | solution.py:393
  68.7 3.5 %collective-permute-start.2 = (f32[64,128]{1,0:T(8,128)S(1)}, f32[64,128]{1,0:T(8,128)S(1)}, u32[]{:S(2)}, u32[]{:S(2)}) collective-permute-start(f32[64,128]{1,0:T(8,128)S(1)} %shard_map.90), channel_id=1, source_target_pairs={{0,64},{1,65},{2,66},{3,67},{4,68},{5,69},{6,70},{7,71},{8,72},{9,... | collective-permute-start | bytes 98312 | tf_op jit(solution)/shard_map/ppermute | solution.py:393
  72.3 1.1 %collective-permute-done.3 = f32[64,128]{1,0:T(8,128)S(1)} collective-permute-done((f32[64,128]{1,0:T(8,128)S(1)}, f32[64,128]{1,0:T(8,128)S(1)}, u32[]{:S(2)}, u32[]{:S(2)}) %collective-permute-start.3) | collective-permute-done | bytes 32800 | tf_op jit(solution)/shard_map/ppermute | solution.py:393
  73.4 0.7 shard_map.89
  74.1 2.9 %collective-permute-done.2 = f32[64,128]{1,0:T(8,128)S(1)} collective-permute-done((f32[64,128]{1,0:T(8,128)S(1)}, f32[64,128]{1,0:T(8,128)S(1)}, u32[]{:S(2)}, u32[]{:S(2)}) %collective-permute-start.2) | collective-permute-done | bytes 32800 | tf_op jit(solution)/shard_map/ppermute | solution.py:393
  77.5 1.7 %collective-permute-start.7 = (f32[576,128]{1,0:T(8,128)S(1)}, f32[576,128]{1,0:T(8,128)S(1)}, u32[]{:S(2)}, u32[]{:S(2)}) collective-permute-start(f32[576,128]{1,0:T(8,128)S(1)} %get-tuple-element.91), channel_id=1, source_target_pairs={{0,12},{1,13},{2,14},{3,15},{4,8},{5,9},{6,10},{7,11},{8,4},{9,5},... | collective-permute-start | bytes 884744 | tf_op jit(solution)/shard_map/ppermute | solution.py:393
  79.2 0.6 collective-permute-start.8
  79.8 1.5 %collective-permute-start.10 = (f32[64,1024]{1,0:T(8,128)S(1)}, f32[64,1024]{1,0:T(8,128)S(1)}, u32[]{:S(2)}, u32[]{:S(2)}) collective-permute-start(f32[64,1024]{1,0:T(8,128)S(1)} %add.22), channel_id=1, source_target_pairs={{0,96},{1,97},{2,98},{3,99},{4,100},{5,101},{6,102},{7,103},{8,104... | collective-permute-start | bytes 786440 | tf_op jit(solution)/shard_map/ppermute | solution.py:393
  81.3 2.0 %collective-permute-start.9 = (f32[64,128]{1,0:T(8,128)S(1)}, f32[64,128]{1,0:T(8,128)S(1)}, u32[]{:S(2)}, u32[]{:S(2)}) collective-permute-start(f32[64,128]{1,0:T(8,128)S(1)} %add_add_fusion.moment), channel_id=1, source_target_pairs={{0,8},{1,9},{2,10},{3,11},{4,12},{5,13},{6,14},{7,15},{8,0},{9,1},... | collective-permute-start | bytes 98312 | tf_op jit(solution)/shard_map/ppermute | solution.py:393
  83.3 4.0 %collective-permute-done.9.across = f32[64,128]{1,0:T(8,128)S(1)} collective-permute-done((f32[64,128]{1,0:T(8,128)S(1)}, f32[64,128]{1,0:T(8,128)S(1)}, u32[]{:S(2)}, u32[]{:S(2)}) %collective-permute-start.9) | collective-permute-done | bytes 32800 | tf_op jit(solution)/shard_map/ppermute | solution.py:393
  87.5 0.6 collective-permute-start.12
  88.2 2.1 %collective-permute-start.13 = (f32[320,128]{1,0:T(8,128)S(1)}, f32[320,128]{1,0:T(8,128)S(1)}, u32[]{:S(2)}, u32[]{:S(2)}) collective-permute-start(f32[320,128]{1,0:T(8,128)S(1)} %get-tuple-element.100), channel_id=1, source_target_pairs={{0,2},{1,3},{2,0},{3,1},{4,6},{5,7},{6,4},{7,5},{8,10},{9,11},{10,... | collective-permute-start | bytes 491528 | tf_op jit(solution)/shard_map/ppermute | solution.py:393
  90.2 2.1 %collective-permute-start.14 = (f32[320,128]{1,0:T(8,128)S(1)}, f32[320,128]{1,0:T(8,128)S(1)}, u32[]{:S(2)}, u32[]{:S(2)}) collective-permute-start(f32[320,128]{1,0:T(8,128)S(1)} %get-tuple-element.101), channel_id=1, source_target_pairs={{0,3},{1,2},{2,1},{3,0},{4,7},{5,6},{6,5},{7,4},{8,11},{9,10},{10,... | collective-permute-start | bytes 491528 | tf_op jit(solution)/shard_map/ppermute | solution.py:393
  92.3 0.9 shard_map.93
  93.2 2.1 %collective-permute-done.13.got_2 = f32[320,128]{1,0:T(8,128)S(1)} collective-permute-done((f32[320,128]{1,0:T(8,128)S(1)}, f32[320,128]{1,0:T(8,128)S(1)}, u32[]{:S(2)}, u32[]{:S(2)}) %collective-permute-start.13) | collective-permute-done | bytes 163872 | tf_op jit(solution)/shard_map/ppermute | solution.py:393
  95.3 1.7 %collective-permute-done.14.got_3 = f32[320,128]{1,0:T(8,128)S(1)} collective-permute-done((f32[320,128]{1,0:T(8,128)S(1)}, f32[320,128]{1,0:T(8,128)S(1)}, u32[]{:S(2)}, u32[]{:S(2)}) %collective-permute-start.14) | collective-permute-done | bytes 163872 | tf_op jit(solution)/shard_map/ppermute | solution.py:393
  97.2 0.7 shard_map.94
  98.3 0.6 shard_map.96
  (29 shorter events, 1.9 us)
Async XLA Ops:
  11.0 16.7 %all-to-all-start = ((f32[16,32,128]{2,1,0:T(8,128)}), f32[16,32,128]{2,1,0:T(8,128)S(1)}, u32[]{:S(2)}, u32[]{:S(2)}) async-start(f32[16,32,128]{2,1,0:T(8,128)} %get-tuple-element.56), calls=%async_computation | async-start | bytes 524288 | tf_op jit(solution)/shard_map/all_to_all | solution.py:408
  19.0 1.2 %copy-start = (bf16[4096,128]{1,0:T(8,128)(2,1)S(1)}, bf16[4096,128]{1,0:T(8,128)(2,1)}, u32[]{:S(2)}) copy-start(bf16[4096,128]{1,0:T(8,128)(2,1)} %src) | copy-start | bytes 3145732
  20.2 0.9 copy-start.1
  53.1 14.0 %copy-start.2 = (bf16[1024,128]{1,0:T(8,128)(2,1)S(1)}, bf16[1024,128]{1,0:T(8,128)(2,1)}, u32[]{:S(2)}) copy-start(bf16[1024,128]{1,0:T(8,128)(2,1)} %tgt.2) | copy-start | bytes 786436
  64.3 2.8 %collective-permute-start = (f32[64,1024]{1,0:T(8,128)S(1)}, f32[64,1024]{1,0:T(8,128)S(1)}, u32[]{:S(2)}, u32[]{:S(2)}) collective-permute-start(f32[64,1024]{1,0:T(8,128)S(1)} %get-tuple-element.81), channel_id=1, source_target_pairs={{0,16},{16,0},{32,48},{48,32},{64,80},{80,64},{96,112},{112,96},{1... | collective-permute-start | bytes 786440 | tf_op jit(solution)/shard_map/ppermute | solution.py:385
  65.5 11.9 %collective-permute-start.5 = (f32[1024,128]{1,0:T(8,128)S(1)}, f32[1024,128]{1,0:T(8,128)S(1)}, u32[]{:S(2)}, u32[]{:S(2)}) collective-permute-start(f32[1024,128]{1,0:T(8,128)S(1)} %get-tuple-element.84), channel_id=1, source_target_pairs={{0,4},{1,5},{2,6},{3,7},{4,0},{5,1},{6,2},{7,3},{8,12},{9,13},{10,... | collective-permute-start | bytes 1572872 | tf_op jit(solution)/shard_map/ppermute | solution.py:393
  65.7 11.7 %collective-permute-start.6 = (f32[1024,128]{1,0:T(8,128)S(1)}, f32[1024,128]{1,0:T(8,128)S(1)}, u32[]{:S(2)}, u32[]{:S(2)}) collective-permute-start(f32[1024,128]{1,0:T(8,128)S(1)} %get-tuple-element.86), channel_id=1, source_target_pairs={{0,12},{1,13},{2,14},{3,15},{4,8},{5,9},{6,10},{7,11},{8,4},{9,5},... | collective-permute-start | bytes 1572872 | tf_op jit(solution)/shard_map/ppermute | solution.py:393
  67.5 5.9 %collective-permute-start.3 = (f32[64,128]{1,0:T(8,128)S(1)}, f32[64,128]{1,0:T(8,128)S(1)}, u32[]{:S(2)}, u32[]{:S(2)}) collective-permute-start(f32[64,128]{1,0:T(8,128)S(1)} %shard_map.90), channel_id=1, source_target_pairs={{0,96},{1,97},{2,98},{3,99},{4,100},{5,101},{6,102},{7,103},{8,104... | collective-permute-start | bytes 98312 | tf_op jit(solution)/shard_map/ppermute | solution.py:393
  68.7 8.6 %collective-permute-start.4 = (f32[64,1024]{1,0:T(8,128)S(1)}, f32[64,1024]{1,0:T(8,128)S(1)}, u32[]{:S(2)}, u32[]{:S(2)}) collective-permute-start(f32[64,1024]{1,0:T(8,128)S(1)} %add.18.mine), channel_id=1, source_target_pairs={{0,32},{1,33},{2,34},{3,35},{4,36},{5,37},{6,38},{7,39},{8,40},{9,... | collective-permute-start | bytes 786440 | tf_op jit(solution)/shard_map/ppermute | solution.py:393
  68.7 8.2 %collective-permute-start.2 = (f32[64,128]{1,0:T(8,128)S(1)}, f32[64,128]{1,0:T(8,128)S(1)}, u32[]{:S(2)}, u32[]{:S(2)}) collective-permute-start(f32[64,128]{1,0:T(8,128)S(1)} %shard_map.90), channel_id=1, source_target_pairs={{0,64},{1,65},{2,66},{3,67},{4,68},{5,69},{6,70},{7,71},{8,72},{9,... | collective-permute-start | bytes 98312 | tf_op jit(solution)/shard_map/ppermute | solution.py:393
  73.4 3.9 %collective-permute-start.1 = (f32[64,128]{1,0:T(8,128)S(1)}, f32[64,128]{1,0:T(8,128)S(1)}, u32[]{:S(2)}, u32[]{:S(2)}) collective-permute-start(f32[64,128]{1,0:T(8,128)S(1)} %shard_map.90), channel_id=1, source_target_pairs={{0,32},{1,33},{2,34},{3,35},{4,36},{5,37},{6,38},{7,39},{8,40},{9,... | collective-permute-start | bytes 98312 | tf_op jit(solution)/shard_map/ppermute | solution.py:393
  77.5 9.8 %collective-permute-start.7 = (f32[576,128]{1,0:T(8,128)S(1)}, f32[576,128]{1,0:T(8,128)S(1)}, u32[]{:S(2)}, u32[]{:S(2)}) collective-permute-start(f32[576,128]{1,0:T(8,128)S(1)} %get-tuple-element.91), channel_id=1, source_target_pairs={{0,12},{1,13},{2,14},{3,15},{4,8},{5,9},{6,10},{7,11},{8,4},{9,5},... | collective-permute-start | bytes 884744 | tf_op jit(solution)/shard_map/ppermute | solution.py:393
  79.2 8.1 %collective-permute-start.8 = (f32[576,128]{1,0:T(8,128)S(1)}, f32[576,128]{1,0:T(8,128)S(1)}, u32[]{:S(2)}, u32[]{:S(2)}) collective-permute-start(f32[576,128]{1,0:T(8,128)S(1)} %get-tuple-element.93), channel_id=1, source_target_pairs={{0,4},{1,5},{2,6},{3,7},{4,0},{5,1},{6,2},{7,3},{8,12},{9,13},{10,... | collective-permute-start | bytes 884744 | tf_op jit(solution)/shard_map/ppermute | solution.py:393
  79.8 7.6 %collective-permute-start.10 = (f32[64,1024]{1,0:T(8,128)S(1)}, f32[64,1024]{1,0:T(8,128)S(1)}, u32[]{:S(2)}, u32[]{:S(2)}) collective-permute-start(f32[64,1024]{1,0:T(8,128)S(1)} %add.22), channel_id=1, source_target_pairs={{0,96},{1,97},{2,98},{3,99},{4,100},{5,101},{6,102},{7,103},{8,104... | collective-permute-start | bytes 786440 | tf_op jit(solution)/shard_map/ppermute | solution.py:393
  81.3 6.0 %collective-permute-start.9 = (f32[64,128]{1,0:T(8,128)S(1)}, f32[64,128]{1,0:T(8,128)S(1)}, u32[]{:S(2)}, u32[]{:S(2)}) collective-permute-start(f32[64,128]{1,0:T(8,128)S(1)} %add_add_fusion.moment), channel_id=1, source_target_pairs={{0,8},{1,9},{2,10},{3,11},{4,12},{5,13},{6,14},{7,15},{8,0},{9,1},... | collective-permute-start | bytes 98312 | tf_op jit(solution)/shard_map/ppermute | solution.py:393
  87.5 4.9 %collective-permute-start.11 = (f32[64,1024]{1,0:T(8,128)S(1)}, f32[64,1024]{1,0:T(8,128)S(1)}, u32[]{:S(2)}, u32[]{:S(2)}) collective-permute-start(f32[64,1024]{1,0:T(8,128)S(1)} %add.23.mine), channel_id=1, source_target_pairs={{0,16},{16,0},{32,48},{48,32},{64,80},{80,64},{96,112},{112,96},{1... | collective-permute-start | bytes 786440 | tf_op jit(solution)/shard_map/ppermute | solution.py:385
  87.5 5.6 %collective-permute-start.12 = (f32[320,128]{1,0:T(8,128)S(1)}, f32[320,128]{1,0:T(8,128)S(1)}, u32[]{:S(2)}, u32[]{:S(2)}) collective-permute-start(f32[320,128]{1,0:T(8,128)S(1)} %get-tuple-element.99), channel_id=1, source_target_pairs={{0,1},{1,0},{2,3},{3,2},{4,5},{5,4},{6,7},{7,6},{8,9},{9,8},{10,11... | collective-permute-start | bytes 491528 | tf_op jit(solution)/shard_map/ppermute | solution.py:393
  88.2 7.1 %collective-permute-start.13 = (f32[320,128]{1,0:T(8,128)S(1)}, f32[320,128]{1,0:T(8,128)S(1)}, u32[]{:S(2)}, u32[]{:S(2)}) collective-permute-start(f32[320,128]{1,0:T(8,128)S(1)} %get-tuple-element.100), channel_id=1, source_target_pairs={{0,2},{1,3},{2,0},{3,1},{4,6},{5,7},{6,4},{7,5},{8,10},{9,11},{10,... | collective-permute-start | bytes 491528 | tf_op jit(solution)/shard_map/ppermute | solution.py:393
  90.2 6.8 %collective-permute-start.14 = (f32[320,128]{1,0:T(8,128)S(1)}, f32[320,128]{1,0:T(8,128)S(1)}, u32[]{:S(2)}, u32[]{:S(2)}) collective-permute-start(f32[320,128]{1,0:T(8,128)S(1)} %get-tuple-element.101), channel_id=1, source_target_pairs={{0,3},{1,2},{2,1},{3,0},{4,7},{5,6},{6,5},{7,4},{8,11},{9,10},{10,... | collective-permute-start | bytes 491528 | tf_op jit(solution)/shard_map/ppermute | solution.py:393
  97.1 1.3 %collective-permute-start.15 = (f32[64,128]{1,0:T(8,128)S(1)}, f32[64,128]{1,0:T(8,128)S(1)}, u32[]{:S(2)}, u32[]{:S(2)}) collective-permute-start(f32[64,128]{1,0:T(8,128)S(1)} %shard_map.95.mine), channel_id=1, source_target_pairs={{0,16},{16,0},{32,48},{48,32},{64,80},{80,64},{96,112},{112,96},{1... | collective-permute-start | bytes 98312 | tf_op jit(solution)/shard_map/ppermute | solution.py:385

commit v9 on v8

--- a/solution.py
+++ b/solution.py
@@ -319,7 +319,7 @@
         send[512:, :] = moment[...]
 
 
-def merge_second(hold_a, got_a, hold_b, got_b, moment, across, send_1, send_2, send_3, stay):
+def merge_second(hold_a, got_a, hold_b, got_b, moment, across, send_2, send_1, send_3, stay):
     total = (moment[...] + got_b[512:, :]) + (across[...] + got_a[512:, :])
     for minor, out in enumerate((stay, send_1, send_2, send_3)):
         rows = slice(minor * 128, (minor + 1) * 128)
@@ -328,11 +328,11 @@
         out[256:, :] = total
 
 
-def merge_moment(stay, got_1, got_2, got_3, out):
+def merge_moment(stay, got_2, got_1, got_3, out):
     out[...] = (stay[256:, :] + got_1[256:, :]) + (got_2[256:, :] + got_3[256:, :])
 
 
-def merge_last(stay, got_1, got_2, got_3, bary):
+def merge_last(stay, got_2, got_1, got_3, bary):
     for half in range(2):
         rows = slice(half * 128, (half + 1) * 128)
         x = (stay[rows, :] + got_1[rows, :]) + (got_2[rows, :] + got_3[rows, :])
@@ -467,7 +467,7 @@
     rest = along_y(mine, 3)
     sends = call(merge_second, [f32(320, 128)] * 4, hold_a, got_a, hold_b, got_b, moment, across)
     stay = sends[3]
-    got = [minor(sends[0], 1), minor(sends[1], 2), minor(sends[2], 3)]
+    got = [minor(sends[0], 2), minor(sends[1], 1), minor(sends[2], 3)]
     stay, mine = lax.optimization_barrier((stay, mine))
     mine = mine + rest
     bary_tgt, = call(

time: 100 us -> 99.6 us (level)
  transfers between devices with their start and end apart: 17 -> 17, of which waited for: 8 -> 9; matrix products, arithmetic and copies ran while one was open for 0% -> 0% of each run, Pallas kernels for 5% -> 5%
where the time goes in v9:
time: 99.6 us; the launch traced here: 98.1 us
  blocking collectives  29.1 us (29%)
  starting transfers between devices  24.5 us (25%)
  Pallas kernels  23.1 us (23%)
  waiting for transfers between devices  18.4 us (18%)
  local copies, waits for them, and re-layouts  2.17 us (2%)
    all_to_all x3, blocking collectives, exchange(): return lax.all_to_all(x, axis, 0, 0)  29.1 us
    pallas_call x14, Pallas kernels, call(): pl.pallas_call(body, out_shape=outs, in_specs=[pl.BlockSpec(memory_space=...  23.1 us
    ppermute x13, starting transfers between devices, by_core(): return lax.ppermute(x, ('row', 'col'), pairs)  16.3 us
    ppermute x13, waiting for transfers between devices, by_core(): return lax.ppermute(x, ('row', 'col'), pairs)  11.9 us
    all_to_all x1, starting transfers between devices, exchange(): return lax.all_to_all(x, axis, 0, 0)  7.97 us
    all_to_all x1, waiting for transfers between devices, exchange(): return lax.all_to_all(x, axis, 0, 0)  6 us
    unnamed x6, local copies, waits for them, and re-layouts  2.17 us
  transfers between devices with their start and end apart: 17, of which 9 were waited for; matrix products, arithmetic and copies ran while one was open for 0% of the time, Pallas kernels for 5%

profile of v9, /device:TPU:0, one launch (start us, length us, event | category | flops | bytes accessed | tf_op | source)
XLA Modules:
  0.0 98.1 jit_solution(11093947393574214883)
XLA Ops:
  0.6 10.3 %shard_map.83 = (f32[16,32,128]{2,1,0:T(8,128)}, bf16[128,4096]{1,0:T(8,128)(2,1)S(1)}, bf16[1024,256]{1,0:T(8,128)(2,1)S(1)}, f32[8,128]{1,0:T(8,128)S(1)}) custom-call(bf16[4096,128]{1,0:T(8,128)(2,1)} %src, bf16[1024,128]{1,0:T(8,128)(2,1)} %tgt.2, bf16[128,128]{1,0:T(8,128)(2,1)} %factor_in.1, f32[8,128]{1,0:T(8,128)} %bitcast.3), custom_call_target="tpu_custom_call" | custom-call | flops 1 | bytes 1 | tf_op jit(solution)/shard_map/pallas_call | solution.py:348
  11.0 8.0 %all-to-all-start = ((f32[16,32,128]{2,1,0:T(8,128)}), f32[16,32,128]{2,1,0:T(8,128)S(1)}, u32[]{:S(2)}, u32[]{:S(2)}) async-start(f32[16,32,128]{2,1,0:T(8,128)} %get-tuple-element.56), calls=%async_computation | async-start | bytes 524288 | tf_op jit(solution)/shard_map/all_to_all | solution.py:408
  19.0 1.2 %copy-done = bf16[4096,128]{1,0:T(8,128)(2,1)S(1)} copy-done((bf16[4096,128]{1,0:T(8,128)(2,1)S(1)}, bf16[4096,128]{1,0:T(8,128)(2,1)}, u32[]{:S(2)}) %copy-start) | copy-done | bytes 1048600
  20.2 0.9 copy-done.1
  21.1 0.5 shard_map.84
  21.6 6.0 %all-to-all-done.parts = f32[16,32,128]{2,1,0:T(8,128)S(1)} async-done(((f32[16,32,128]{2,1,0:T(8,128)}), f32[16,32,128]{2,1,0:T(8,128)S(1)}, u32[]{:S(2)}, u32[]{:S(2)}) %all-to-all-start) | async-done | bytes 262176 | tf_op jit(solution)/shard_map/all_to_all | solution.py:408
  27.6 2.9 %shard_map.85 = (bf16[32,1024,128]{2,1,0:T(8,128)(2,1)S(1)}, f32[8,8,128]{2,1,0:T(8,128)S(1)}, f32[8,128]{1,0:T(8,128)S(1)}, f32[32,128]{1,0:T(8,128)S(1)}) custom-call(f32[16,32,128]{2,1,0:T(8,128)S(1)} %all-to-all-done.parts, bf16[128,4096]{1,0:T(8,128)(2,1)S(1)} %get-tuple-element.57.proj_t, bf16[1024,256]{1,0:T(8,128)(2,1)S(1)} %get-tuple-element.63.aug, ...), custom_call_target="tpu_custom_call" | custom-call | flops 1 | bytes 1 | tf_op jit(solution)/shard_map/pallas_call | solution.py:348
  30.5 9.7 %all_to_all.20.parts = f32[8,8,128]{2,1,0:T(8,128)S(1)} all-to-all(f32[8,8,128]{2,1,0:T(8,128)S(1)} %get-tuple-element.65), channel_id=1, replica_groups=mesh['row'=8,'col'=16] {'row'}, dimensions={0} | all-to-all | bytes 65536 | tf_op jit(solution)/shard_map/all_to_all | solution.py:408
  40.2 1.2 %shard_map.86 = (f32[16,32,128]{2,1,0:T(8,128)S(1)}, f32[8,128]{1,0:T(8,128)S(1)}, f32[8,128]{1,0:T(8,128)S(1)}) custom-call(f32[8,8,128]{2,1,0:T(8,128)S(1)} %all_to_all.20.parts, f32[8,128]{1,0:T(8,128)S(1)} %get-tuple-element.66.shift, bf16[32,1024,128]{2,1,0:T(8,128)(2,1)S(1)} %get-tuple-element.67.kernel_t), custom_call_target="tpu_custom_call" | custom-call | flops 1 | bytes 1 | tf_op jit(solution)/shard_map/pallas_call | solution.py:348
  41.5 11.6 %all_to_all.21.parts = f32[16,32,128]{2,1,0:T(8,128)S(1)} all-to-all(f32[16,32,128]{2,1,0:T(8,128)S(1)} %get-tuple-element.68), channel_id=1, replica_groups=mesh['row'=8,'col'=16] {'col'}, dimensions={0} | all-to-all | bytes 524288 | tf_op jit(solution)/shard_map/all_to_all | solution.py:408
  53.1 3.4 %shard_map.87 = (f32[8,8,128]{2,1,0:T(8,128)S(1)}, f32[64,1024]{1,0:T(8,128)S(1)}, f32[64,1024]{1,0:T(8,128)S(1)}, f32[32,128]{1,0:T(8,128)S(1)}, f32[32,128]{1,0:T(8,128)}) custom-call(f32[16,32,128]{2,1,0:T(8,128)S(1)} %all_to_all.21.parts, f32[32,128]{1,0:T(8,128)S(1)} %get-tuple-element.69.rho, bf16[32,1024,128]{2,1,0:T(8,128)(2,1)S(1)} %get-tuple-element.67.kernel_t, ...), custom_call_target="tpu_custom_call" | custom-call | flops 1 | bytes 1 | tf_op jit(solution)/shard_map/pallas_call | solution.py:348
  56.5 7.8 %all_to_all.22.parts = f32[8,8,128]{2,1,0:T(8,128)S(1)} all-to-all(f32[8,8,128]{2,1,0:T(8,128)S(1)} %get-tuple-element.72), channel_id=1, replica_groups=mesh['row'=8,'col'=16] {'row'}, dimensions={0} | all-to-all | bytes 65536 | tf_op jit(solution)/shard_map/all_to_all | solution.py:408
  64.3 1.2 %shard_map.88 = (f32[1024,128]{1,0:T(8,128)S(1)}, f32[1024,128]{1,0:T(8,128)S(1)}, bf16[128,1024]{1,0:T(8,128)(2,1)S(1)}, f32[8,128]{1,0:T(8,128)}, f32[8,128]{1,0:T(8,128)S(1)}) custom-call(f32[8,8,128]{2,1,0:T(8,128)S(1)} %all_to_all.22.parts, f32[8,128]{1,0:T(8,128)S(1)} %get-tuple-element.71.weight, f32[8,128]{1,0:T(8,128)S(1)} %get-tuple-element.75.before, ...), custom_call_target="tpu_custom_call" | custom-call | flops 2147483648 | bytes 1 | tf_op jit(solution)/shard_map/pallas_call | solution.py:348
  65.7 1.3 %collective-permute-start.6 = (f32[1024,128]{1,0:T(8,128)S(1)}, f32[1024,128]{1,0:T(8,128)S(1)}, u32[]{:S(2)}, u32[]{:S(2)}) collective-permute-start(f32[1024,128]{1,0:T(8,128)S(1)} %get-tuple-element.86), channel_id=1, source_target_pairs={{0,12},{1,13},{2,14},{3,15},{4,8},{5,9},{6,10},{7,11},{8,4},{9,5},... | collective-permute-start | bytes 1572872 | tf_op jit(solution)/shard_map/ppermute | solution.py:393
  67.5 1.2 %collective-permute-start.3 = (f32[64,128]{1,0:T(8,128)S(1)}, f32[64,128]{1,0:T(8,128)S(1)}, u32[]{:S(2)}, u32[]{:S(2)}) collective-permute-start(f32[64,128]{1,0:T(8,128)S(1)} %shard_map.90), channel_id=1, source_target_pairs={{0,96},{1,97},{2,98},{3,99},{4,100},{5,101},{6,102},{7,103},{8,104... | collective-permute-start | bytes 98312 | tf_op jit(solution)/shard_map/ppermute | solution.py:393
  68.7 3.5 %collective-permute-start.2 = (f32[64,128]{1,0:T(8,128)S(1)}, f32[64,128]{1,0:T(8,128)S(1)}, u32[]{:S(2)}, u32[]{:S(2)}) collective-permute-start(f32[64,128]{1,0:T(8,128)S(1)} %shard_map.90), channel_id=1, source_target_pairs={{0,64},{1,65},{2,66},{3,67},{4,68},{5,69},{6,70},{7,71},{8,72},{9,... | collective-permute-start | bytes 98312 | tf_op jit(solution)/shard_map/ppermute | solution.py:393
  72.3 1.1 %collective-permute-done.3 = f32[64,128]{1,0:T(8,128)S(1)} collective-permute-done((f32[64,128]{1,0:T(8,128)S(1)}, f32[64,128]{1,0:T(8,128)S(1)}, u32[]{:S(2)}, u32[]{:S(2)}) %collective-permute-start.3) | collective-permute-done | bytes 32800 | tf_op jit(solution)/shard_map/ppermute | solution.py:393
  73.4 0.7 shard_map.89
  74.1 2.9 %collective-permute-done.2 = f32[64,128]{1,0:T(8,128)S(1)} collective-permute-done((f32[64,128]{1,0:T(8,128)S(1)}, f32[64,128]{1,0:T(8,128)S(1)}, u32[]{:S(2)}, u32[]{:S(2)}) %collective-permute-start.2) | collective-permute-done | bytes 32800 | tf_op jit(solution)/shard_map/ppermute | solution.py:393
  77.5 1.7 %collective-permute-start.7 = (f32[576,128]{1,0:T(8,128)S(1)}, f32[576,128]{1,0:T(8,128)S(1)}, u32[]{:S(2)}, u32[]{:S(2)}) collective-permute-start(f32[576,128]{1,0:T(8,128)S(1)} %get-tuple-element.91), channel_id=1, source_target_pairs={{0,12},{1,13},{2,14},{3,15},{4,8},{5,9},{6,10},{7,11},{8,4},{9,5},... | collective-permute-start | bytes 884744 | tf_op jit(solution)/shard_map/ppermute | solution.py:393
  79.2 0.6 collective-permute-start.8
  79.8 1.5 %collective-permute-start.10 = (f32[64,1024]{1,0:T(8,128)S(1)}, f32[64,1024]{1,0:T(8,128)S(1)}, u32[]{:S(2)}, u32[]{:S(2)}) collective-permute-start(f32[64,1024]{1,0:T(8,128)S(1)} %add.22), channel_id=1, source_target_pairs={{0,96},{1,97},{2,98},{3,99},{4,100},{5,101},{6,102},{7,103},{8,104... | collective-permute-start | bytes 786440 | tf_op jit(solution)/shard_map/ppermute | solution.py:393
  81.3 2.0 %collective-permute-start.9 = (f32[64,128]{1,0:T(8,128)S(1)}, f32[64,128]{1,0:T(8,128)S(1)}, u32[]{:S(2)}, u32[]{:S(2)}) collective-permute-start(f32[64,128]{1,0:T(8,128)S(1)} %add_add_fusion.moment), channel_id=1, source_target_pairs={{0,8},{1,9},{2,10},{3,11},{4,12},{5,13},{6,14},{7,15},{8,0},{9,1},... | collective-permute-start | bytes 98312 | tf_op jit(solution)/shard_map/ppermute | solution.py:393
  83.3 4.0 %collective-permute-done.9.across = f32[64,128]{1,0:T(8,128)S(1)} collective-permute-done((f32[64,128]{1,0:T(8,128)S(1)}, f32[64,128]{1,0:T(8,128)S(1)}, u32[]{:S(2)}, u32[]{:S(2)}) %collective-permute-start.9) | collective-permute-done | bytes 32800 | tf_op jit(solution)/shard_map/ppermute | solution.py:393
  87.5 1.4 %collective-permute-start.12 = (f32[320,128]{1,0:T(8,128)S(1)}, f32[320,128]{1,0:T(8,128)S(1)}, u32[]{:S(2)}, u32[]{:S(2)}) collective-permute-start(f32[320,128]{1,0:T(8,128)S(1)} %get-tuple-element.99), channel_id=1, source_target_pairs={{0,2},{1,3},{2,0},{3,1},{4,6},{5,7},{6,4},{7,5},{8,10},{9,11},{10,... | collective-permute-start | bytes 491528 | tf_op jit(solution)/shard_map/ppermute | solution.py:393
  89.0 0.7 collective-permute-start.13
  89.6 2.1 %collective-permute-start.14 = (f32[320,128]{1,0:T(8,128)S(1)}, f32[320,128]{1,0:T(8,128)S(1)}, u32[]{:S(2)}, u32[]{:S(2)}) collective-permute-start(f32[320,128]{1,0:T(8,128)S(1)} %get-tuple-element.101), channel_id=1, source_target_pairs={{0,3},{1,2},{2,1},{3,0},{4,7},{5,6},{6,5},{7,4},{8,11},{9,10},{10,... | collective-permute-start | bytes 491528 | tf_op jit(solution)/shard_map/ppermute | solution.py:393
  91.7 0.9 shard_map.93
  92.6 1.9 %collective-permute-done.12.got_2 = f32[320,128]{1,0:T(8,128)S(1)} collective-permute-done((f32[320,128]{1,0:T(8,128)S(1)}, f32[320,128]{1,0:T(8,128)S(1)}, u32[]{:S(2)}, u32[]{:S(2)}) %collective-permute-start.12) | collective-permute-done | bytes 163872 | tf_op jit(solution)/shard_map/ppermute | solution.py:393
  94.7 1.5 %collective-permute-done.14.got_3 = f32[320,128]{1,0:T(8,128)S(1)} collective-permute-done((f32[320,128]{1,0:T(8,128)S(1)}, f32[320,128]{1,0:T(8,128)S(1)}, u32[]{:S(2)}, u32[]{:S(2)}) %collective-permute-start.14) | collective-permute-done | bytes 163872 | tf_op jit(solution)/shard_map/ppermute | solution.py:393
  96.3 0.7 shard_map.94
  97.5 0.6 shard_map.96
  (29 shorter events, 2.1 us)
Async XLA Ops:
  11.0 16.7 %all-to-all-start = ((f32[16,32,128]{2,1,0:T(8,128)}), f32[16,32,128]{2,1,0:T(8,128)S(1)}, u32[]{:S(2)}, u32[]{:S(2)}) async-start(f32[16,32,128]{2,1,0:T(8,128)} %get-tuple-element.56), calls=%async_computation | async-start | bytes 524288 | tf_op jit(solution)/shard_map/all_to_all | solution.py:408
  19.0 1.2 %copy-start = (bf16[4096,128]{1,0:T(8,128)(2,1)S(1)}, bf16[4096,128]{1,0:T(8,128)(2,1)}, u32[]{:S(2)}) copy-start(bf16[4096,128]{1,0:T(8,128)(2,1)} %src) | copy-start | bytes 3145732
  20.2 0.9 copy-start.1
  53.1 14.0 %copy-start.2 = (bf16[1024,128]{1,0:T(8,128)(2,1)S(1)}, bf16[1024,128]{1,0:T(8,128)(2,1)}, u32[]{:S(2)}) copy-start(bf16[1024,128]{1,0:T(8,128)(2,1)} %tgt.2) | copy-start | bytes 786436
  64.3 2.8 %collective-permute-start = (f32[64,1024]{1,0:T(8,128)S(1)}, f32[64,1024]{1,0:T(8,128)S(1)}, u32[]{:S(2)}, u32[]{:S(2)}) collective-permute-start(f32[64,1024]{1,0:T(8,128)S(1)} %get-tuple-element.81), channel_id=1, source_target_pairs={{0,16},{16,0},{32,48},{48,32},{64,80},{80,64},{96,112},{112,96},{1... | collective-permute-start | bytes 786440 | tf_op jit(solution)/shard_map/ppermute | solution.py:385
  65.5 11.9 %collective-permute-start.5 = (f32[1024,128]{1,0:T(8,128)S(1)}, f32[1024,128]{1,0:T(8,128)S(1)}, u32[]{:S(2)}, u32[]{:S(2)}) collective-permute-start(f32[1024,128]{1,0:T(8,128)S(1)} %get-tuple-element.84), channel_id=1, source_target_pairs={{0,4},{1,5},{2,6},{3,7},{4,0},{5,1},{6,2},{7,3},{8,12},{9,13},{10,... | collective-permute-start | bytes 1572872 | tf_op jit(solution)/shard_map/ppermute | solution.py:393
  65.7 11.7 %collective-permute-start.6 = (f32[1024,128]{1,0:T(8,128)S(1)}, f32[1024,128]{1,0:T(8,128)S(1)}, u32[]{:S(2)}, u32[]{:S(2)}) collective-permute-start(f32[1024,128]{1,0:T(8,128)S(1)} %get-tuple-element.86), channel_id=1, source_target_pairs={{0,12},{1,13},{2,14},{3,15},{4,8},{5,9},{6,10},{7,11},{8,4},{9,5},... | collective-permute-start | bytes 1572872 | tf_op jit(solution)/shard_map/ppermute | solution.py:393
  67.5 5.9 %collective-permute-start.3 = (f32[64,128]{1,0:T(8,128)S(1)}, f32[64,128]{1,0:T(8,128)S(1)}, u32[]{:S(2)}, u32[]{:S(2)}) collective-permute-start(f32[64,128]{1,0:T(8,128)S(1)} %shard_map.90), channel_id=1, source_target_pairs={{0,96},{1,97},{2,98},{3,99},{4,100},{5,101},{6,102},{7,103},{8,104... | collective-permute-start | bytes 98312 | tf_op jit(solution)/shard_map/ppermute | solution.py:393
  68.7 8.6 %collective-permute-start.4 = (f32[64,1024]{1,0:T(8,128)S(1)}, f32[64,1024]{1,0:T(8,128)S(1)}, u32[]{:S(2)}, u32[]{:S(2)}) collective-permute-start(f32[64,1024]{1,0:T(8,128)S(1)} %add.18.mine), channel_id=1, source_target_pairs={{0,32},{1,33},{2,34},{3,35},{4,36},{5,37},{6,38},{7,39},{8,40},{9,... | collective-permute-start | bytes 786440 | tf_op jit(solution)/shard_map/ppermute | solution.py:393
  68.7 8.2 %collective-permute-start.2 = (f32[64,128]{1,0:T(8,128)S(1)}, f32[64,128]{1,0:T(8,128)S(1)}, u32[]{:S(2)}, u32[]{:S(2)}) collective-permute-start(f32[64,128]{1,0:T(8,128)S(1)} %shard_map.90), channel_id=1, source_target_pairs={{0,64},{1,65},{2,66},{3,67},{4,68},{5,69},{6,70},{7,71},{8,72},{9,... | collective-permute-start | bytes 98312 | tf_op jit(solution)/shard_map/ppermute | solution.py:393
  73.4 3.9 %collective-permute-start.1 = (f32[64,128]{1,0:T(8,128)S(1)}, f32[64,128]{1,0:T(8,128)S(1)}, u32[]{:S(2)}, u32[]{:S(2)}) collective-permute-start(f32[64,128]{1,0:T(8,128)S(1)} %shard_map.90), channel_id=1, source_target_pairs={{0,32},{1,33},{2,34},{3,35},{4,36},{5,37},{6,38},{7,39},{8,40},{9,... | collective-permute-start | bytes 98312 | tf_op jit(solution)/shard_map/ppermute | solution.py:393
  77.5 9.8 %collective-permute-start.7 = (f32[576,128]{1,0:T(8,128)S(1)}, f32[576,128]{1,0:T(8,128)S(1)}, u32[]{:S(2)}, u32[]{:S(2)}) collective-permute-start(f32[576,128]{1,0:T(8,128)S(1)} %get-tuple-element.91), channel_id=1, source_target_pairs={{0,12},{1,13},{2,14},{3,15},{4,8},{5,9},{6,10},{7,11},{8,4},{9,5},... | collective-permute-start | bytes 884744 | tf_op jit(solution)/shard_map/ppermute | solution.py:393
  79.2 8.1 %collective-permute-start.8 = (f32[576,128]{1,0:T(8,128)S(1)}, f32[576,128]{1,0:T(8,128)S(1)}, u32[]{:S(2)}, u32[]{:S(2)}) collective-permute-start(f32[576,128]{1,0:T(8,128)S(1)} %get-tuple-element.93), channel_id=1, source_target_pairs={{0,4},{1,5},{2,6},{3,7},{4,0},{5,1},{6,2},{7,3},{8,12},{9,13},{10,... | collective-permute-start | bytes 884744 | tf_op jit(solution)/shard_map/ppermute | solution.py:393
  79.8 7.6 %collective-permute-start.10 = (f32[64,1024]{1,0:T(8,128)S(1)}, f32[64,1024]{1,0:T(8,128)S(1)}, u32[]{:S(2)}, u32[]{:S(2)}) collective-permute-start(f32[64,1024]{1,0:T(8,128)S(1)} %add.22), channel_id=1, source_target_pairs={{0,96},{1,97},{2,98},{3,99},{4,100},{5,101},{6,102},{7,103},{8,104... | collective-permute-start | bytes 786440 | tf_op jit(solution)/shard_map/ppermute | solution.py:393
  81.3 6.0 %collective-permute-start.9 = (f32[64,128]{1,0:T(8,128)S(1)}, f32[64,128]{1,0:T(8,128)S(1)}, u32[]{:S(2)}, u32[]{:S(2)}) collective-permute-start(f32[64,128]{1,0:T(8,128)S(1)} %add_add_fusion.moment), channel_id=1, source_target_pairs={{0,8},{1,9},{2,10},{3,11},{4,12},{5,13},{6,14},{7,15},{8,0},{9,1},... | collective-permute-start | bytes 98312 | tf_op jit(solution)/shard_map/ppermute | solution.py:393
  87.5 4.3 %collective-permute-start.11 = (f32[64,1024]{1,0:T(8,128)S(1)}, f32[64,1024]{1,0:T(8,128)S(1)}, u32[]{:S(2)}, u32[]{:S(2)}) collective-permute-start(f32[64,1024]{1,0:T(8,128)S(1)} %add.23.mine), channel_id=1, source_target_pairs={{0,16},{16,0},{32,48},{48,32},{64,80},{80,64},{96,112},{112,96},{1... | collective-permute-start | bytes 786440 | tf_op jit(solution)/shard_map/ppermute | solution.py:385
  87.5 6.9 %collective-permute-start.12 = (f32[320,128]{1,0:T(8,128)S(1)}, f32[320,128]{1,0:T(8,128)S(1)}, u32[]{:S(2)}, u32[]{:S(2)}) collective-permute-start(f32[320,128]{1,0:T(8,128)S(1)} %get-tuple-element.99), channel_id=1, source_target_pairs={{0,2},{1,3},{2,0},{3,1},{4,6},{5,7},{6,4},{7,5},{8,10},{9,11},{10,... | collective-permute-start | bytes 491528 | tf_op jit(solution)/shard_map/ppermute | solution.py:393
  89.0 5.7 %collective-permute-start.13 = (f32[320,128]{1,0:T(8,128)S(1)}, f32[320,128]{1,0:T(8,128)S(1)}, u32[]{:S(2)}, u32[]{:S(2)}) collective-permute-start(f32[320,128]{1,0:T(8,128)S(1)} %get-tuple-element.100), channel_id=1, source_target_pairs={{0,1},{1,0},{2,3},{3,2},{4,5},{5,4},{6,7},{7,6},{8,9},{9,8},{10,11... | collective-permute-start | bytes 491528 | tf_op jit(solution)/shard_map/ppermute | solution.py:393
  89.6 6.6 %collective-permute-start.14 = (f32[320,128]{1,0:T(8,128)S(1)}, f32[320,128]{1,0:T(8,128)S(1)}, u32[]{:S(2)}, u32[]{:S(2)}) collective-permute-start(f32[320,128]{1,0:T(8,128)S(1)} %get-tuple-element.101), channel_id=1, source_target_pairs={{0,3},{1,2},{2,1},{3,0},{4,7},{5,6},{6,5},{7,4},{8,11},{9,10},{10,... | collective-permute-start | bytes 491528 | tf_op jit(solution)/shard_map/ppermute | solution.py:393
  96.2 1.3 %collective-permute-start.15 = (f32[64,128]{1,0:T(8,128)S(1)}, f32[64,128]{1,0:T(8,128)S(1)}, u32[]{:S(2)}, u32[]{:S(2)}) collective-permute-start(f32[64,128]{1,0:T(8,128)S(1)} %shard_map.95.mine), channel_id=1, source_target_pairs={{0,16},{16,0},{32,48},{48,32},{64,80},{80,64},{96,112},{112,96},{1... | collective-permute-start | bytes 98312 | tf_op jit(solution)/shard_map/ppermute | solution.py:385

commit v10 on v9

--- a/solution.py
+++ b/solution.py
@@ -297,10 +297,13 @@
     mix(left[...], kernel_t, scale, (out_a, out_b), STAY, src_count)
 
 
-def moment_half(mine, gain, tgt, out):
-    out[...] = jnp.dot(
+def moment_half(mine, gain, tgt, out, both):
+    x = jnp.dot(
         mine[...] * flat(gain[...]), tgt[...].astype(F32), precision=lax.Precision.HIGHEST, preferred_element_type=F32
     )
+    out[...] = x
+    both[:, : mine.shape[1]] = mine[...]
+    both[:, mine.shape[1] :] = x
 
 
 def in_order(mine, other):
@@ -456,9 +459,12 @@
         functools.partial(target_keep, src_count=src_count), [message, message], left, near(kernel_t), scale
     )
     mine = keep + other
-    moment, = call(moment_half, [f32(width // 2, width)], mine, gain, tgt_emb)
-    mine = mine + along_y(mine, 1)
-    moment = (moment + along_y(moment, 1)) + (opposite_y(moment) + along_y(moment, 3))
+    moment, both = call(
+        moment_half, [f32(width // 2, width), f32(width // 2, cols + width)], mine, gain, tgt_emb
+    )
+    both = both + along_y(both, 1)
+    mine = both[:, :cols]
+    moment = both[:, cols:] + (opposite_y(moment) + along_y(moment, 3))
     keep_a, moment, mine = lax.optimization_barrier((keep_a, moment, mine))
     both = [f32(576, 128), f32(512, 128)] * 2
     send_a, hold_a, send_b, hold_b = call(merge_first, both, keep_a, got_a, keep_b, got_b, moment)

time: 99.6 us -> 98.3 us (0.987)
  waiting for transfers between devices: 18.4 us -> 17 us
    ppermute x13 -> x12, waiting for transfers between devices: 11.9 us -> 10.5 us  [by_core(): return lax.ppermute(x, ('row', 'col'), pairs)]
    ppermute x13 -> x12, starting transfers between devices: 16.3 us -> 16.4 us  [by_core(): return lax.ppermute(x, ('row', 'col'), pairs)]
  transfers between devices with their start and end apart: 17 -> 16, of which waited for: 9 -> 9; matrix products, arithmetic and copies ran while one was open for 0% -> 0% of each run, Pallas kernels for 5% -> 5%
where the time goes in v10:
time: 98.3 us; the launch traced here: 96.9 us
  blocking collectives  29.1 us (30%)
  starting transfers between devices  24.6 us (25%)
  Pallas kernels  23.1 us (23%)
  waiting for transfers between devices  17 us (17%)
  local copies, waits for them, and re-layouts  2.19 us (2%)
    all_to_all x3, blocking collectives, exchange(): return lax.all_to_all(x, axis, 0, 0)  29.1 us
    pallas_call x14, Pallas kernels, call(): pl.pallas_call(body, out_shape=outs, in_specs=[pl.BlockSpec(memory_space=...  23.1 us
    ppermute x12, starting transfers between devices, by_core(): return lax.ppermute(x, ('row', 'col'), pairs)  16.4 us
    ppermute x12, waiting for transfers between devices, by_core(): return lax.ppermute(x, ('row', 'col'), pairs)  10.5 us
    all_to_all x1, starting transfers between devices, exchange(): return lax.all_to_all(x, axis, 0, 0)  7.97 us
    all_to_all x1, waiting for transfers between devices, exchange(): return lax.all_to_all(x, axis, 0, 0)  6 us
    unnamed x6, local copies, waits for them, and re-layouts  2.17 us
  transfers between devices with their start and end apart: 16, of which 9 were waited for; matrix products, arithmetic and copies ran while one was open for 0% of the time, Pallas kernels for 5%

profile of v10, /device:TPU:0, one launch (start us, length us, event | category | flops | bytes accessed | tf_op | source)
XLA Modules:
  0.0 96.9 jit_solution(6216127331774262084)
XLA Ops:
  0.6 10.3 %shard_map.83 = (f32[16,32,128]{2,1,0:T(8,128)}, bf16[128,4096]{1,0:T(8,128)(2,1)S(1)}, bf16[1024,256]{1,0:T(8,128)(2,1)S(1)}, f32[8,128]{1,0:T(8,128)S(1)}) custom-call(bf16[4096,128]{1,0:T(8,128)(2,1)} %src, bf16[1024,128]{1,0:T(8,128)(2,1)} %tgt.2, bf16[128,128]{1,0:T(8,128)(2,1)} %factor_in.1, f32[8,128]{1,0:T(8,128)} %bitcast.3), custom_call_target="tpu_custom_call" | custom-call | flops 1 | bytes 1 | tf_op jit(solution)/shard_map/pallas_call | solution.py:351
  11.0 8.0 %all-to-all-start = ((f32[16,32,128]{2,1,0:T(8,128)}), f32[16,32,128]{2,1,0:T(8,128)S(1)}, u32[]{:S(2)}, u32[]{:S(2)}) async-start(f32[16,32,128]{2,1,0:T(8,128)} %get-tuple-element.58), calls=%async_computation | async-start | bytes 524288 | tf_op jit(solution)/shard_map/all_to_all | solution.py:411
  19.0 1.2 %copy-done = bf16[4096,128]{1,0:T(8,128)(2,1)S(1)} copy-done((bf16[4096,128]{1,0:T(8,128)(2,1)S(1)}, bf16[4096,128]{1,0:T(8,128)(2,1)}, u32[]{:S(2)}) %copy-start) | copy-done | bytes 1048600
  20.2 0.9 copy-done.1
  21.1 0.5 shard_map.84
  21.6 6.0 %all-to-all-done.parts = f32[16,32,128]{2,1,0:T(8,128)S(1)} async-done(((f32[16,32,128]{2,1,0:T(8,128)}), f32[16,32,128]{2,1,0:T(8,128)S(1)}, u32[]{:S(2)}, u32[]{:S(2)}) %all-to-all-start) | async-done | bytes 262176 | tf_op jit(solution)/shard_map/all_to_all | solution.py:411
  27.6 2.9 %shard_map.85 = (bf16[32,1024,128]{2,1,0:T(8,128)(2,1)S(1)}, f32[8,8,128]{2,1,0:T(8,128)S(1)}, f32[8,128]{1,0:T(8,128)S(1)}, f32[32,128]{1,0:T(8,128)S(1)}) custom-call(f32[16,32,128]{2,1,0:T(8,128)S(1)} %all-to-all-done.parts, bf16[128,4096]{1,0:T(8,128)(2,1)S(1)} %get-tuple-element.59.proj_t, bf16[1024,256]{1,0:T(8,128)(2,1)S(1)} %get-tuple-element.65.aug, ...), custom_call_target="tpu_custom_call" | custom-call | flops 1 | bytes 1 | tf_op jit(solution)/shard_map/pallas_call | solution.py:351
  30.5 9.7 %all_to_all.20.parts = f32[8,8,128]{2,1,0:T(8,128)S(1)} all-to-all(f32[8,8,128]{2,1,0:T(8,128)S(1)} %get-tuple-element.67), channel_id=1, replica_groups=mesh['row'=8,'col'=16] {'row'}, dimensions={0} | all-to-all | bytes 65536 | tf_op jit(solution)/shard_map/all_to_all | solution.py:411
  40.2 1.2 %shard_map.86 = (f32[16,32,128]{2,1,0:T(8,128)S(1)}, f32[8,128]{1,0:T(8,128)S(1)}, f32[8,128]{1,0:T(8,128)S(1)}) custom-call(f32[8,8,128]{2,1,0:T(8,128)S(1)} %all_to_all.20.parts, f32[8,128]{1,0:T(8,128)S(1)} %get-tuple-element.68.shift, bf16[32,1024,128]{2,1,0:T(8,128)(2,1)S(1)} %get-tuple-element.69.kernel_t), custom_call_target="tpu_custom_call" | custom-call | flops 1 | bytes 1 | tf_op jit(solution)/shard_map/pallas_call | solution.py:351
  41.5 11.6 %all_to_all.21.parts = f32[16,32,128]{2,1,0:T(8,128)S(1)} all-to-all(f32[16,32,128]{2,1,0:T(8,128)S(1)} %get-tuple-element.70), channel_id=1, replica_groups=mesh['row'=8,'col'=16] {'col'}, dimensions={0} | all-to-all | bytes 524288 | tf_op jit(solution)/shard_map/all_to_all | solution.py:411
  53.1 3.4 %shard_map.87 = (f32[8,8,128]{2,1,0:T(8,128)S(1)}, f32[64,1024]{1,0:T(8,128)S(1)}, f32[64,1024]{1,0:T(8,128)S(1)}, f32[32,128]{1,0:T(8,128)S(1)}, f32[32,128]{1,0:T(8,128)}) custom-call(f32[16,32,128]{2,1,0:T(8,128)S(1)} %all_to_all.21.parts, f32[32,128]{1,0:T(8,128)S(1)} %get-tuple-element.71.rho, bf16[32,1024,128]{2,1,0:T(8,128)(2,1)S(1)} %get-tuple-element.69.kernel_t, ...), custom_call_target="tpu_custom_call" | custom-call | flops 1 | bytes 1 | tf_op jit(solution)/shard_map/pallas_call | solution.py:351
  56.5 7.8 %all_to_all.22.parts = f32[8,8,128]{2,1,0:T(8,128)S(1)} all-to-all(f32[8,8,128]{2,1,0:T(8,128)S(1)} %get-tuple-element.74), channel_id=1, replica_groups=mesh['row'=8,'col'=16] {'row'}, dimensions={0} | all-to-all | bytes 65536 | tf_op jit(solution)/shard_map/all_to_all | solution.py:411
  64.3 1.2 %shard_map.88 = (f32[1024,128]{1,0:T(8,128)S(1)}, f32[1024,128]{1,0:T(8,128)S(1)}, bf16[128,1024]{1,0:T(8,128)(2,1)S(1)}, f32[8,128]{1,0:T(8,128)}, f32[8,128]{1,0:T(8,128)S(1)}) custom-call(f32[8,8,128]{2,1,0:T(8,128)S(1)} %all_to_all.22.parts, f32[8,128]{1,0:T(8,128)S(1)} %get-tuple-element.73.weight, f32[8,128]{1,0:T(8,128)S(1)} %get-tuple-element.77.before, ...), custom_call_target="tpu_custom_call" | custom-call | flops 2147483648 | bytes 1 | tf_op jit(solution)/shard_map/pallas_call | solution.py:351
  65.7 1.3 %collective-permute-start.5 = (f32[1024,128]{1,0:T(8,128)S(1)}, f32[1024,128]{1,0:T(8,128)S(1)}, u32[]{:S(2)}, u32[]{:S(2)}) collective-permute-start(f32[1024,128]{1,0:T(8,128)S(1)} %get-tuple-element.90), channel_id=1, source_target_pairs={{0,12},{1,13},{2,14},{3,15},{4,8},{5,9},{6,10},{7,11},{8,4},{9,5},... | collective-permute-start | bytes 1572872 | tf_op jit(solution)/shard_map/ppermute | solution.py:396
  67.5 0.7 collective-permute-start.1
  68.2 1.1 %collective-permute-start.3 = (f32[64,128]{1,0:T(8,128)S(1)}, f32[64,128]{1,0:T(8,128)S(1)}, u32[]{:S(2)}, u32[]{:S(2)}) collective-permute-start(f32[64,128]{1,0:T(8,128)S(1)} %get-tuple-element.86), channel_id=1, source_target_pairs={{0,96},{1,97},{2,98},{3,99},{4,100},{5,101},{6,102},{7,103},{8,104... | collective-permute-start | bytes 98312 | tf_op jit(solution)/shard_map/ppermute | solution.py:396
  69.2 2.5 %collective-permute-start.2 = (f32[64,128]{1,0:T(8,128)S(1)}, f32[64,128]{1,0:T(8,128)S(1)}, u32[]{:S(2)}, u32[]{:S(2)}) collective-permute-start(f32[64,128]{1,0:T(8,128)S(1)} %get-tuple-element.86), channel_id=1, source_target_pairs={{0,64},{1,65},{2,66},{3,67},{4,68},{5,69},{6,70},{7,71},{8,72},{9,... | collective-permute-start | bytes 98312 | tf_op jit(solution)/shard_map/ppermute | solution.py:396
  71.7 0.7 shard_map.89
  72.4 2.4 %collective-permute-done.1 = f32[64,1152]{1,0:T(8,128)S(1)} collective-permute-done((f32[64,1152]{1,0:T(8,128)S(1)}, f32[64,1152]{1,0:T(8,128)S(1)}, u32[]{:S(2)}, u32[]{:S(2)}) %collective-permute-start.1) | collective-permute-done | bytes 294944 | tf_op jit(solution)/shard_map/ppermute | solution.py:396
  74.9 1.1 %collective-permute-done.2 = f32[64,128]{1,0:T(8,128)S(1)} collective-permute-done((f32[64,128]{1,0:T(8,128)S(1)}, f32[64,128]{1,0:T(8,128)S(1)}, u32[]{:S(2)}, u32[]{:S(2)}) %collective-permute-start.2) | collective-permute-done | bytes 32800 | tf_op jit(solution)/shard_map/ppermute | solution.py:396
  76.2 1.9 %collective-permute-start.6 = (f32[576,128]{1,0:T(8,128)S(1)}, f32[576,128]{1,0:T(8,128)S(1)}, u32[]{:S(2)}, u32[]{:S(2)}) collective-permute-start(f32[576,128]{1,0:T(8,128)S(1)} %get-tuple-element.95), channel_id=1, source_target_pairs={{0,12},{1,13},{2,14},{3,15},{4,8},{5,9},{6,10},{7,11},{8,4},{9,5},... | collective-permute-start | bytes 884744 | tf_op jit(solution)/shard_map/ppermute | solution.py:396
  78.2 1.8 %collective-permute-start.9 = (f32[64,1024]{1,0:T(8,128)S(1)}, f32[64,1024]{1,0:T(8,128)S(1)}, u32[]{:S(2)}, u32[]{:S(2)}) collective-permute-start(f32[64,1024]{1,0:T(8,128)S(1)} %slice.9), channel_id=1, source_target_pairs={{0,96},{1,97},{2,98},{3,99},{4,100},{5,101},{6,102},{7,103},{8,104... | collective-permute-start | bytes 786440 | tf_op jit(solution)/shard_map/ppermute | solution.py:396
  80.1 2.7 %collective-permute-start.8 = (f32[64,128]{1,0:T(8,128)S(1)}, f32[64,128]{1,0:T(8,128)S(1)}, u32[]{:S(2)}, u32[]{:S(2)}) collective-permute-start(f32[64,128]{1,0:T(8,128)S(1)} %slice_add_fusion.moment), channel_id=1, source_target_pairs={{0,8},{1,9},{2,10},{3,11},{4,12},{5,13},{6,14},{7,15},{8,0},{9,1},... | collective-permute-start | bytes 98312 | tf_op jit(solution)/shard_map/ppermute | solution.py:396
  82.8 3.3 %collective-permute-done.8.across = f32[64,128]{1,0:T(8,128)S(1)} collective-permute-done((f32[64,128]{1,0:T(8,128)S(1)}, f32[64,128]{1,0:T(8,128)S(1)}, u32[]{:S(2)}, u32[]{:S(2)}) %collective-permute-start.8) | collective-permute-done | bytes 32800 | tf_op jit(solution)/shard_map/ppermute | solution.py:396
  86.3 1.4 %collective-permute-start.11 = (f32[320,128]{1,0:T(8,128)S(1)}, f32[320,128]{1,0:T(8,128)S(1)}, u32[]{:S(2)}, u32[]{:S(2)}) collective-permute-start(f32[320,128]{1,0:T(8,128)S(1)} %get-tuple-element.103), channel_id=1, source_target_pairs={{0,2},{1,3},{2,0},{3,1},{4,6},{5,7},{6,4},{7,5},{8,10},{9,11},{10,... | collective-permute-start | bytes 491528 | tf_op jit(solution)/shard_map/ppermute | solution.py:396
  87.6 0.7 collective-permute-start.12
  88.3 2.1 %collective-permute-start.13 = (f32[320,128]{1,0:T(8,128)S(1)}, f32[320,128]{1,0:T(8,128)S(1)}, u32[]{:S(2)}, u32[]{:S(2)}) collective-permute-start(f32[320,128]{1,0:T(8,128)S(1)} %get-tuple-element.105), channel_id=1, source_target_pairs={{0,3},{1,2},{2,1},{3,0},{4,7},{5,6},{6,5},{7,4},{8,11},{9,10},{10,... | collective-permute-start | bytes 491528 | tf_op jit(solution)/shard_map/ppermute | solution.py:396
  90.4 0.9 shard_map.93
  91.3 1.9 %collective-permute-done.11.got_2 = f32[320,128]{1,0:T(8,128)S(1)} collective-permute-done((f32[320,128]{1,0:T(8,128)S(1)}, f32[320,128]{1,0:T(8,128)S(1)}, u32[]{:S(2)}, u32[]{:S(2)}) %collective-permute-start.11) | collective-permute-done | bytes 163872 | tf_op jit(solution)/shard_map/ppermute | solution.py:396
  93.4 1.6 %collective-permute-done.13.got_3 = f32[320,128]{1,0:T(8,128)S(1)} collective-permute-done((f32[320,128]{1,0:T(8,128)S(1)}, f32[320,128]{1,0:T(8,128)S(1)}, u32[]{:S(2)}, u32[]{:S(2)}) %collective-permute-start.13) | collective-permute-done | bytes 163872 | tf_op jit(solution)/shard_map/ppermute | solution.py:396
  95.0 0.7 shard_map.94
  96.2 0.6 shard_map.96
  (28 shorter events, 2.0 us)
Async XLA Ops:
  11.0 16.7 %all-to-all-start = ((f32[16,32,128]{2,1,0:T(8,128)}), f32[16,32,128]{2,1,0:T(8,128)S(1)}, u32[]{:S(2)}, u32[]{:S(2)}) async-start(f32[16,32,128]{2,1,0:T(8,128)} %get-tuple-element.58), calls=%async_computation | async-start | bytes 524288 | tf_op jit(solution)/shard_map/all_to_all | solution.py:411
  19.0 1.2 %copy-start = (bf16[4096,128]{1,0:T(8,128)(2,1)S(1)}, bf16[4096,128]{1,0:T(8,128)(2,1)}, u32[]{:S(2)}) copy-start(bf16[4096,128]{1,0:T(8,128)(2,1)} %src) | copy-start | bytes 3145732
  20.2 0.9 copy-start.1
  53.1 14.0 %copy-start.2 = (bf16[1024,128]{1,0:T(8,128)(2,1)S(1)}, bf16[1024,128]{1,0:T(8,128)(2,1)}, u32[]{:S(2)}) copy-start(bf16[1024,128]{1,0:T(8,128)(2,1)} %tgt.2) | copy-start | bytes 786436
  64.3 2.8 %collective-permute-start = (f32[64,1024]{1,0:T(8,128)S(1)}, f32[64,1024]{1,0:T(8,128)S(1)}, u32[]{:S(2)}, u32[]{:S(2)}) collective-permute-start(f32[64,1024]{1,0:T(8,128)S(1)} %get-tuple-element.83), channel_id=1, source_target_pairs={{0,16},{16,0},{32,48},{48,32},{64,80},{80,64},{96,112},{112,96},{1... | collective-permute-start | bytes 786440 | tf_op jit(solution)/shard_map/ppermute | solution.py:388
  65.5 10.5 %collective-permute-start.4 = (f32[1024,128]{1,0:T(8,128)S(1)}, f32[1024,128]{1,0:T(8,128)S(1)}, u32[]{:S(2)}, u32[]{:S(2)}) collective-permute-start(f32[1024,128]{1,0:T(8,128)S(1)} %get-tuple-element.88), channel_id=1, source_target_pairs={{0,4},{1,5},{2,6},{3,7},{4,0},{5,1},{6,2},{7,3},{8,12},{9,13},{10,... | collective-permute-start | bytes 1572872 | tf_op jit(solution)/shard_map/ppermute | solution.py:396
  65.7 10.4 %collective-permute-start.5 = (f32[1024,128]{1,0:T(8,128)S(1)}, f32[1024,128]{1,0:T(8,128)S(1)}, u32[]{:S(2)}, u32[]{:S(2)}) collective-permute-start(f32[1024,128]{1,0:T(8,128)S(1)} %get-tuple-element.90), channel_id=1, source_target_pairs={{0,12},{1,13},{2,14},{3,15},{4,8},{5,9},{6,10},{7,11},{8,4},{9,5},... | collective-permute-start | bytes 1572872 | tf_op jit(solution)/shard_map/ppermute | solution.py:396
  67.5 7.3 %collective-permute-start.1 = (f32[64,1152]{1,0:T(8,128)S(1)}, f32[64,1152]{1,0:T(8,128)S(1)}, u32[]{:S(2)}, u32[]{:S(2)}) collective-permute-start(f32[64,1152]{1,0:T(8,128)S(1)} %get-tuple-element.85), channel_id=1, source_target_pairs={{0,32},{1,33},{2,34},{3,35},{4,36},{5,37},{6,38},{7,39},{8,40},{9,... | collective-permute-start | bytes 884744 | tf_op jit(solution)/shard_map/ppermute | solution.py:396
  68.2 6.7 %collective-permute-start.3 = (f32[64,128]{1,0:T(8,128)S(1)}, f32[64,128]{1,0:T(8,128)S(1)}, u32[]{:S(2)}, u32[]{:S(2)}) collective-permute-start(f32[64,128]{1,0:T(8,128)S(1)} %get-tuple-element.86), channel_id=1, source_target_pairs={{0,96},{1,97},{2,98},{3,99},{4,100},{5,101},{6,102},{7,103},{8,104... | collective-permute-start | bytes 98312 | tf_op jit(solution)/shard_map/ppermute | solution.py:396
  69.2 6.7 %collective-permute-start.2 = (f32[64,128]{1,0:T(8,128)S(1)}, f32[64,128]{1,0:T(8,128)S(1)}, u32[]{:S(2)}, u32[]{:S(2)}) collective-permute-start(f32[64,128]{1,0:T(8,128)S(1)} %get-tuple-element.86), channel_id=1, source_target_pairs={{0,64},{1,65},{2,66},{3,67},{4,68},{5,69},{6,70},{7,71},{8,72},{9,... | collective-permute-start | bytes 98312 | tf_op jit(solution)/shard_map/ppermute | solution.py:396
  76.2 9.8 %collective-permute-start.6 = (f32[576,128]{1,0:T(8,128)S(1)}, f32[576,128]{1,0:T(8,128)S(1)}, u32[]{:S(2)}, u32[]{:S(2)}) collective-permute-start(f32[576,128]{1,0:T(8,128)S(1)} %get-tuple-element.95), channel_id=1, source_target_pairs={{0,12},{1,13},{2,14},{3,15},{4,8},{5,9},{6,10},{7,11},{8,4},{9,5},... | collective-permute-start | bytes 884744 | tf_op jit(solution)/shard_map/ppermute | solution.py:396
  78.1 8.0 %collective-permute-start.7 = (f32[576,128]{1,0:T(8,128)S(1)}, f32[576,128]{1,0:T(8,128)S(1)}, u32[]{:S(2)}, u32[]{:S(2)}) collective-permute-start(f32[576,128]{1,0:T(8,128)S(1)} %get-tuple-element.97), channel_id=1, source_target_pairs={{0,4},{1,5},{2,6},{3,7},{4,0},{5,1},{6,2},{7,3},{8,12},{9,13},{10,... | collective-permute-start | bytes 884744 | tf_op jit(solution)/shard_map/ppermute | solution.py:396
  78.2 7.9 %collective-permute-start.9 = (f32[64,1024]{1,0:T(8,128)S(1)}, f32[64,1024]{1,0:T(8,128)S(1)}, u32[]{:S(2)}, u32[]{:S(2)}) collective-permute-start(f32[64,1024]{1,0:T(8,128)S(1)} %slice.9), channel_id=1, source_target_pairs={{0,96},{1,97},{2,98},{3,99},{4,100},{5,101},{6,102},{7,103},{8,104... | collective-permute-start | bytes 786440 | tf_op jit(solution)/shard_map/ppermute | solution.py:396
  80.1 6.0 %collective-permute-start.8 = (f32[64,128]{1,0:T(8,128)S(1)}, f32[64,128]{1,0:T(8,128)S(1)}, u32[]{:S(2)}, u32[]{:S(2)}) collective-permute-start(f32[64,128]{1,0:T(8,128)S(1)} %slice_add_fusion.moment), channel_id=1, source_target_pairs={{0,8},{1,9},{2,10},{3,11},{4,12},{5,13},{6,14},{7,15},{8,0},{9,1},... | collective-permute-start | bytes 98312 | tf_op jit(solution)/shard_map/ppermute | solution.py:396
  86.2 4.3 %collective-permute-start.10 = (f32[64,1024]{1,0:T(8,128)S(1)}, f32[64,1024]{1,0:T(8,128)S(1)}, u32[]{:S(2)}, u32[]{:S(2)}) collective-permute-start(f32[64,1024]{1,0:T(8,128)S(1)} %add.19.mine), channel_id=1, source_target_pairs={{0,16},{16,0},{32,48},{48,32},{64,80},{80,64},{96,112},{112,96},{1... | collective-permute-start | bytes 786440 | tf_op jit(solution)/shard_map/ppermute | solution.py:388
  86.3 6.9 %collective-permute-start.11 = (f32[320,128]{1,0:T(8,128)S(1)}, f32[320,128]{1,0:T(8,128)S(1)}, u32[]{:S(2)}, u32[]{:S(2)}) collective-permute-start(f32[320,128]{1,0:T(8,128)S(1)} %get-tuple-element.103), channel_id=1, source_target_pairs={{0,2},{1,3},{2,0},{3,1},{4,6},{5,7},{6,4},{7,5},{8,10},{9,11},{10,... | collective-permute-start | bytes 491528 | tf_op jit(solution)/shard_map/ppermute | solution.py:396
  87.6 5.7 %collective-permute-start.12 = (f32[320,128]{1,0:T(8,128)S(1)}, f32[320,128]{1,0:T(8,128)S(1)}, u32[]{:S(2)}, u32[]{:S(2)}) collective-permute-start(f32[320,128]{1,0:T(8,128)S(1)} %get-tuple-element.104), channel_id=1, source_target_pairs={{0,1},{1,0},{2,3},{3,2},{4,5},{5,4},{6,7},{7,6},{8,9},{9,8},{10,11... | collective-permute-start | bytes 491528 | tf_op jit(solution)/shard_map/ppermute | solution.py:396
  88.3 6.6 %collective-permute-start.13 = (f32[320,128]{1,0:T(8,128)S(1)}, f32[320,128]{1,0:T(8,128)S(1)}, u32[]{:S(2)}, u32[]{:S(2)}) collective-permute-start(f32[320,128]{1,0:T(8,128)S(1)} %get-tuple-element.105), channel_id=1, source_target_pairs={{0,3},{1,2},{2,1},{3,0},{4,7},{5,6},{6,5},{7,4},{8,11},{9,10},{10,... | collective-permute-start | bytes 491528 | tf_op jit(solution)/shard_map/ppermute | solution.py:396
  94.9 1.3 %collective-permute-start.14 = (f32[64,128]{1,0:T(8,128)S(1)}, f32[64,128]{1,0:T(8,128)S(1)}, u32[]{:S(2)}, u32[]{:S(2)}) collective-permute-start(f32[64,128]{1,0:T(8,128)S(1)} %shard_map.95.mine), channel_id=1, source_target_pairs={{0,16},{16,0},{32,48},{48,32},{64,80},{80,64},{96,112},{112,96},{1... | collective-permute-start | bytes 98312 | tf_op jit(solution)/shard_map/ppermute | solution.py:388

commit v11 on v10

--- a/solution.py
+++ b/solution.py
@@ -465,12 +465,11 @@
     both = both + along_y(both, 1)
     mine = both[:, :cols]
     moment = both[:, cols:] + (opposite_y(moment) + along_y(moment, 3))
+    rest = along_y(mine, 3)
     keep_a, moment, mine = lax.optimization_barrier((keep_a, moment, mine))
     both = [f32(576, 128), f32(512, 128)] * 2
     send_a, hold_a, send_b, hold_b = call(merge_first, both, keep_a, got_a, keep_b, got_b, moment)
     got_a, got_b, across = major(send_a, 3), major(send_b, 1), major(moment, 2)
-    hold_a, mine = lax.optimization_barrier((hold_a, mine))
-    rest = along_y(mine, 3)
     sends = call(merge_second, [f32(320, 128)] * 4, hold_a, got_a, hold_b, got_b, moment, across)
     stay = sends[3]
     got = [minor(sends[0], 2), minor(sends[1], 1), minor(sends[2], 3)]

time: 98.3 us -> 98.3 us (level)
  no operation moved by 1% of the time
where the time goes in v11:
time: 98.3 us; the launch traced here: 96.9 us
  blocking collectives  29.1 us (30%)
  starting transfers between devices  24.6 us (25%)
  Pallas kernels  23.1 us (23%)
  waiting for transfers between devices  17 us (17%)
  local copies, waits for them, and re-layouts  2.19 us (2%)
    all_to_all x3, blocking collectives, exchange(): return lax.all_to_all(x, axis, 0, 0)  29.1 us
    pallas_call x14, Pallas kernels, call(): pl.pallas_call(body, out_shape=outs, in_specs=[pl.BlockSpec(memory_space=...  23.1 us
    ppermute x12, starting transfers between devices, by_core(): return lax.ppermute(x, ('row', 'col'), pairs)  16.4 us
    ppermute x12, waiting for transfers between devices, by_core(): return lax.ppermute(x, ('row', 'col'), pairs)  10.5 us
    all_to_all x1, starting transfers between devices, exchange(): return lax.all_to_all(x, axis, 0, 0)  7.97 us
    all_to_all x1, waiting for transfers between devices, exchange(): return lax.all_to_all(x, axis, 0, 0)  6 us
    unnamed x6, local copies, waits for them, and re-layouts  2.17 us
  transfers between devices with their start and end apart: 16, of which 9 were waited for; matrix products, arithmetic and copies ran while one was open for 0% of the time, Pallas kernels for 5%

profile of v11, /device:TPU:0, one launch (start us, length us, event | category | flops | bytes accessed | tf_op | source)
XLA Modules:
  0.0 96.9 jit_solution(12672990265228210629)
XLA Ops:
  0.6 10.3 %shard_map.83 = (f32[16,32,128]{2,1,0:T(8,128)}, bf16[128,4096]{1,0:T(8,128)(2,1)S(1)}, bf16[1024,256]{1,0:T(8,128)(2,1)S(1)}, f32[8,128]{1,0:T(8,128)S(1)}) custom-call(bf16[4096,128]{1,0:T(8,128)(2,1)} %src, bf16[1024,128]{1,0:T(8,128)(2,1)} %tgt.2, bf16[128,128]{1,0:T(8,128)(2,1)} %factor_in.1, f32[8,128]{1,0:T(8,128)} %bitcast.3), custom_call_target="tpu_custom_call" | custom-call | flops 1 | bytes 1 | tf_op jit(solution)/shard_map/pallas_call | solution.py:351
  11.0 8.0 %all-to-all-start = ((f32[16,32,128]{2,1,0:T(8,128)}), f32[16,32,128]{2,1,0:T(8,128)S(1)}, u32[]{:S(2)}, u32[]{:S(2)}) async-start(f32[16,32,128]{2,1,0:T(8,128)} %get-tuple-element.56), calls=%async_computation | async-start | bytes 524288 | tf_op jit(solution)/shard_map/all_to_all | solution.py:411
  19.0 1.2 %copy-done = bf16[4096,128]{1,0:T(8,128)(2,1)S(1)} copy-done((bf16[4096,128]{1,0:T(8,128)(2,1)S(1)}, bf16[4096,128]{1,0:T(8,128)(2,1)}, u32[]{:S(2)}) %copy-start) | copy-done | bytes 1048600
  20.2 0.9 copy-done.1
  21.1 0.5 shard_map.84
  21.6 6.0 %all-to-all-done.parts = f32[16,32,128]{2,1,0:T(8,128)S(1)} async-done(((f32[16,32,128]{2,1,0:T(8,128)}), f32[16,32,128]{2,1,0:T(8,128)S(1)}, u32[]{:S(2)}, u32[]{:S(2)}) %all-to-all-start) | async-done | bytes 262176 | tf_op jit(solution)/shard_map/all_to_all | solution.py:411
  27.6 2.9 %shard_map.85 = (bf16[32,1024,128]{2,1,0:T(8,128)(2,1)S(1)}, f32[8,8,128]{2,1,0:T(8,128)S(1)}, f32[8,128]{1,0:T(8,128)S(1)}, f32[32,128]{1,0:T(8,128)S(1)}) custom-call(f32[16,32,128]{2,1,0:T(8,128)S(1)} %all-to-all-done.parts, bf16[128,4096]{1,0:T(8,128)(2,1)S(1)} %get-tuple-element.57.proj_t, bf16[1024,256]{1,0:T(8,128)(2,1)S(1)} %get-tuple-element.63.aug, ...), custom_call_target="tpu_custom_call" | custom-call | flops 1 | bytes 1 | tf_op jit(solution)/shard_map/pallas_call | solution.py:351
  30.5 9.7 %all_to_all.20.parts = f32[8,8,128]{2,1,0:T(8,128)S(1)} all-to-all(f32[8,8,128]{2,1,0:T(8,128)S(1)} %get-tuple-element.65), channel_id=1, replica_groups=mesh['row'=8,'col'=16] {'row'}, dimensions={0} | all-to-all | bytes 65536 | tf_op jit(solution)/shard_map/all_to_all | solution.py:411
  40.2 1.2 %shard_map.86 = (f32[16,32,128]{2,1,0:T(8,128)S(1)}, f32[8,128]{1,0:T(8,128)S(1)}, f32[8,128]{1,0:T(8,128)S(1)}) custom-call(f32[8,8,128]{2,1,0:T(8,128)S(1)} %all_to_all.20.parts, f32[8,128]{1,0:T(8,128)S(1)} %get-tuple-element.66.shift, bf16[32,1024,128]{2,1,0:T(8,128)(2,1)S(1)} %get-tuple-element.67.kernel_t), custom_call_target="tpu_custom_call" | custom-call | flops 1 | bytes 1 | tf_op jit(solution)/shard_map/pallas_call | solution.py:351
  41.5 11.6 %all_to_all.21.parts = f32[16,32,128]{2,1,0:T(8,128)S(1)} all-to-all(f32[16,32,128]{2,1,0:T(8,128)S(1)} %get-tuple-element.68), channel_id=1, replica_groups=mesh['row'=8,'col'=16] {'col'}, dimensions={0} | all-to-all | bytes 524288 | tf_op jit(solution)/shard_map/all_to_all | solution.py:411
  53.1 3.4 %shard_map.87 = (f32[8,8,128]{2,1,0:T(8,128)S(1)}, f32[64,1024]{1,0:T(8,128)S(1)}, f32[64,1024]{1,0:T(8,128)S(1)}, f32[32,128]{1,0:T(8,128)S(1)}, f32[32,128]{1,0:T(8,128)}) custom-call(f32[16,32,128]{2,1,0:T(8,128)S(1)} %all_to_all.21.parts, f32[32,128]{1,0:T(8,128)S(1)} %get-tuple-element.69.rho, bf16[32,1024,128]{2,1,0:T(8,128)(2,1)S(1)} %get-tuple-element.67.kernel_t, ...), custom_call_target="tpu_custom_call" | custom-call | flops 1 | bytes 1 | tf_op jit(solution)/shard_map/pallas_call | solution.py:351
  56.5 7.8 %all_to_all.22.parts = f32[8,8,128]{2,1,0:T(8,128)S(1)} all-to-all(f32[8,8,128]{2,1,0:T(8,128)S(1)} %get-tuple-element.72), channel_id=1, replica_groups=mesh['row'=8,'col'=16] {'row'}, dimensions={0} | all-to-all | bytes 65536 | tf_op jit(solution)/shard_map/all_to_all | solution.py:411
  64.3 1.2 %shard_map.88 = (f32[1024,128]{1,0:T(8,128)S(1)}, f32[1024,128]{1,0:T(8,128)S(1)}, bf16[128,1024]{1,0:T(8,128)(2,1)S(1)}, f32[8,128]{1,0:T(8,128)}, f32[8,128]{1,0:T(8,128)S(1)}) custom-call(f32[8,8,128]{2,1,0:T(8,128)S(1)} %all_to_all.22.parts, f32[8,128]{1,0:T(8,128)S(1)} %get-tuple-element.71.weight, f32[8,128]{1,0:T(8,128)S(1)} %get-tuple-element.75.before, ...), custom_call_target="tpu_custom_call" | custom-call | flops 2147483648 | bytes 1 | tf_op jit(solution)/shard_map/pallas_call | solution.py:351
  65.7 1.3 %collective-permute-start.5 = (f32[1024,128]{1,0:T(8,128)S(1)}, f32[1024,128]{1,0:T(8,128)S(1)}, u32[]{:S(2)}, u32[]{:S(2)}) collective-permute-start(f32[1024,128]{1,0:T(8,128)S(1)} %get-tuple-element.88), channel_id=1, source_target_pairs={{0,12},{1,13},{2,14},{3,15},{4,8},{5,9},{6,10},{7,11},{8,4},{9,5},... | collective-permute-start | bytes 1572872 | tf_op jit(solution)/shard_map/ppermute | solution.py:396
  67.5 0.7 collective-permute-start.1
  68.2 1.1 %collective-permute-start.3 = (f32[64,128]{1,0:T(8,128)S(1)}, f32[64,128]{1,0:T(8,128)S(1)}, u32[]{:S(2)}, u32[]{:S(2)}) collective-permute-start(f32[64,128]{1,0:T(8,128)S(1)} %get-tuple-element.84), channel_id=1, source_target_pairs={{0,96},{1,97},{2,98},{3,99},{4,100},{5,101},{6,102},{7,103},{8,104... | collective-permute-start | bytes 98312 | tf_op jit(solution)/shard_map/ppermute | solution.py:396
  69.2 2.5 %collective-permute-start.2 = (f32[64,128]{1,0:T(8,128)S(1)}, f32[64,128]{1,0:T(8,128)S(1)}, u32[]{:S(2)}, u32[]{:S(2)}) collective-permute-start(f32[64,128]{1,0:T(8,128)S(1)} %get-tuple-element.84), channel_id=1, source_target_pairs={{0,64},{1,65},{2,66},{3,67},{4,68},{5,69},{6,70},{7,71},{8,72},{9,... | collective-permute-start | bytes 98312 | tf_op jit(solution)/shard_map/ppermute | solution.py:396
  71.7 0.7 shard_map.89
  72.4 2.4 %collective-permute-done.1 = f32[64,1152]{1,0:T(8,128)S(1)} collective-permute-done((f32[64,1152]{1,0:T(8,128)S(1)}, f32[64,1152]{1,0:T(8,128)S(1)}, u32[]{:S(2)}, u32[]{:S(2)}) %collective-permute-start.1) | collective-permute-done | bytes 294944 | tf_op jit(solution)/shard_map/ppermute | solution.py:396
  74.9 1.1 %collective-permute-done.2 = f32[64,128]{1,0:T(8,128)S(1)} collective-permute-done((f32[64,128]{1,0:T(8,128)S(1)}, f32[64,128]{1,0:T(8,128)S(1)}, u32[]{:S(2)}, u32[]{:S(2)}) %collective-permute-start.2) | collective-permute-done | bytes 32800 | tf_op jit(solution)/shard_map/ppermute | solution.py:396
  76.2 1.9 %collective-permute-start.6 = (f32[576,128]{1,0:T(8,128)S(1)}, f32[576,128]{1,0:T(8,128)S(1)}, u32[]{:S(2)}, u32[]{:S(2)}) collective-permute-start(f32[576,128]{1,0:T(8,128)S(1)} %get-tuple-element.91), channel_id=1, source_target_pairs={{0,12},{1,13},{2,14},{3,15},{4,8},{5,9},{6,10},{7,11},{8,4},{9,5},... | collective-permute-start | bytes 884744 | tf_op jit(solution)/shard_map/ppermute | solution.py:396
  78.2 1.8 %collective-permute-start.9 = (f32[64,1024]{1,0:T(8,128)S(1)}, f32[64,1024]{1,0:T(8,128)S(1)}, u32[]{:S(2)}, u32[]{:S(2)}) collective-permute-start(f32[64,1024]{1,0:T(8,128)S(1)} %slice.9), channel_id=1, source_target_pairs={{0,96},{1,97},{2,98},{3,99},{4,100},{5,101},{6,102},{7,103},{8,104... | collective-permute-start | bytes 786440 | tf_op jit(solution)/shard_map/ppermute | solution.py:396
  80.1 2.7 %collective-permute-start.8 = (f32[64,128]{1,0:T(8,128)S(1)}, f32[64,128]{1,0:T(8,128)S(1)}, u32[]{:S(2)}, u32[]{:S(2)}) collective-permute-start(f32[64,128]{1,0:T(8,128)S(1)} %slice_add_fusion.moment), channel_id=1, source_target_pairs={{0,8},{1,9},{2,10},{3,11},{4,12},{5,13},{6,14},{7,15},{8,0},{9,1},... | collective-permute-start | bytes 98312 | tf_op jit(solution)/shard_map/ppermute | solution.py:396
  82.8 3.3 %collective-permute-done.8.across = f32[64,128]{1,0:T(8,128)S(1)} collective-permute-done((f32[64,128]{1,0:T(8,128)S(1)}, f32[64,128]{1,0:T(8,128)S(1)}, u32[]{:S(2)}, u32[]{:S(2)}) %collective-permute-start.8) | collective-permute-done | bytes 32800 | tf_op jit(solution)/shard_map/ppermute | solution.py:396
  86.3 1.4 %collective-permute-start.11 = (f32[320,128]{1,0:T(8,128)S(1)}, f32[320,128]{1,0:T(8,128)S(1)}, u32[]{:S(2)}, u32[]{:S(2)}) collective-permute-start(f32[320,128]{1,0:T(8,128)S(1)} %get-tuple-element.99), channel_id=1, source_target_pairs={{0,2},{1,3},{2,0},{3,1},{4,6},{5,7},{6,4},{7,5},{8,10},{9,11},{10,... | collective-permute-start | bytes 491528 | tf_op jit(solution)/shard_map/ppermute | solution.py:396
  87.6 0.7 collective-permute-start.12
  88.3 2.1 %collective-permute-start.13 = (f32[320,128]{1,0:T(8,128)S(1)}, f32[320,128]{1,0:T(8,128)S(1)}, u32[]{:S(2)}, u32[]{:S(2)}) collective-permute-start(f32[320,128]{1,0:T(8,128)S(1)} %get-tuple-element.101), channel_id=1, source_target_pairs={{0,3},{1,2},{2,1},{3,0},{4,7},{5,6},{6,5},{7,4},{8,11},{9,10},{10,... | collective-permute-start | bytes 491528 | tf_op jit(solution)/shard_map/ppermute | solution.py:396
  90.4 0.9 shard_map.93
  91.3 1.9 %collective-permute-done.11.got_2 = f32[320,128]{1,0:T(8,128)S(1)} collective-permute-done((f32[320,128]{1,0:T(8,128)S(1)}, f32[320,128]{1,0:T(8,128)S(1)}, u32[]{:S(2)}, u32[]{:S(2)}) %collective-permute-start.11) | collective-permute-done | bytes 163872 | tf_op jit(solution)/shard_map/ppermute | solution.py:396
  93.4 1.6 %collective-permute-done.13.got_3 = f32[320,128]{1,0:T(8,128)S(1)} collective-permute-done((f32[320,128]{1,0:T(8,128)S(1)}, f32[320,128]{1,0:T(8,128)S(1)}, u32[]{:S(2)}, u32[]{:S(2)}) %collective-permute-start.13) | collective-permute-done | bytes 163872 | tf_op jit(solution)/shard_map/ppermute | solution.py:396
  95.0 0.7 shard_map.94
  96.2 0.6 shard_map.96
  (28 shorter events, 2.0 us)
Async XLA Ops:
  11.0 16.7 %all-to-all-start = ((f32[16,32,128]{2,1,0:T(8,128)}), f32[16,32,128]{2,1,0:T(8,128)S(1)}, u32[]{:S(2)}, u32[]{:S(2)}) async-start(f32[16,32,128]{2,1,0:T(8,128)} %get-tuple-element.56), calls=%async_computation | async-start | bytes 524288 | tf_op jit(solution)/shard_map/all_to_all | solution.py:411
  19.0 1.2 %copy-start = (bf16[4096,128]{1,0:T(8,128)(2,1)S(1)}, bf16[4096,128]{1,0:T(8,128)(2,1)}, u32[]{:S(2)}) copy-start(bf16[4096,128]{1,0:T(8,128)(2,1)} %src) | copy-start | bytes 3145732
  20.2 0.9 copy-start.1
  53.1 14.0 %copy-start.2 = (bf16[1024,128]{1,0:T(8,128)(2,1)S(1)}, bf16[1024,128]{1,0:T(8,128)(2,1)}, u32[]{:S(2)}) copy-start(bf16[1024,128]{1,0:T(8,128)(2,1)} %tgt.2) | copy-start | bytes 786436
  64.3 2.8 %collective-permute-start = (f32[64,1024]{1,0:T(8,128)S(1)}, f32[64,1024]{1,0:T(8,128)S(1)}, u32[]{:S(2)}, u32[]{:S(2)}) collective-permute-start(f32[64,1024]{1,0:T(8,128)S(1)} %get-tuple-element.81), channel_id=1, source_target_pairs={{0,16},{16,0},{32,48},{48,32},{64,80},{80,64},{96,112},{112,96},{1... | collective-permute-start | bytes 786440 | tf_op jit(solution)/shard_map/ppermute | solution.py:388
  65.5 10.5 %collective-permute-start.4 = (f32[1024,128]{1,0:T(8,128)S(1)}, f32[1024,128]{1,0:T(8,128)S(1)}, u32[]{:S(2)}, u32[]{:S(2)}) collective-permute-start(f32[1024,128]{1,0:T(8,128)S(1)} %get-tuple-element.86), channel_id=1, source_target_pairs={{0,4},{1,5},{2,6},{3,7},{4,0},{5,1},{6,2},{7,3},{8,12},{9,13},{10,... | collective-permute-start | bytes 1572872 | tf_op jit(solution)/shard_map/ppermute | solution.py:396
  65.7 10.4 %collective-permute-start.5 = (f32[1024,128]{1,0:T(8,128)S(1)}, f32[1024,128]{1,0:T(8,128)S(1)}, u32[]{:S(2)}, u32[]{:S(2)}) collective-permute-start(f32[1024,128]{1,0:T(8,128)S(1)} %get-tuple-element.88), channel_id=1, source_target_pairs={{0,12},{1,13},{2,14},{3,15},{4,8},{5,9},{6,10},{7,11},{8,4},{9,5},... | collective-permute-start | bytes 1572872 | tf_op jit(solution)/shard_map/ppermute | solution.py:396
  67.5 7.3 %collective-permute-start.1 = (f32[64,1152]{1,0:T(8,128)S(1)}, f32[64,1152]{1,0:T(8,128)S(1)}, u32[]{:S(2)}, u32[]{:S(2)}) collective-permute-start(f32[64,1152]{1,0:T(8,128)S(1)} %get-tuple-element.83), channel_id=1, source_target_pairs={{0,32},{1,33},{2,34},{3,35},{4,36},{5,37},{6,38},{7,39},{8,40},{9,... | collective-permute-start | bytes 884744 | tf_op jit(solution)/shard_map/ppermute | solution.py:396
  68.2 6.7 %collective-permute-start.3 = (f32[64,128]{1,0:T(8,128)S(1)}, f32[64,128]{1,0:T(8,128)S(1)}, u32[]{:S(2)}, u32[]{:S(2)}) collective-permute-start(f32[64,128]{1,0:T(8,128)S(1)} %get-tuple-element.84), channel_id=1, source_target_pairs={{0,96},{1,97},{2,98},{3,99},{4,100},{5,101},{6,102},{7,103},{8,104... | collective-permute-start | bytes 98312 | tf_op jit(solution)/shard_map/ppermute | solution.py:396
  69.2 6.7 %collective-permute-start.2 = (f32[64,128]{1,0:T(8,128)S(1)}, f32[64,128]{1,0:T(8,128)S(1)}, u32[]{:S(2)}, u32[]{:S(2)}) collective-permute-start(f32[64,128]{1,0:T(8,128)S(1)} %get-tuple-element.84), channel_id=1, source_target_pairs={{0,64},{1,65},{2,66},{3,67},{4,68},{5,69},{6,70},{7,71},{8,72},{9,... | collective-permute-start | bytes 98312 | tf_op jit(solution)/shard_map/ppermute | solution.py:396
  76.2 9.8 %collective-permute-start.6 = (f32[576,128]{1,0:T(8,128)S(1)}, f32[576,128]{1,0:T(8,128)S(1)}, u32[]{:S(2)}, u32[]{:S(2)}) collective-permute-start(f32[576,128]{1,0:T(8,128)S(1)} %get-tuple-element.91), channel_id=1, source_target_pairs={{0,12},{1,13},{2,14},{3,15},{4,8},{5,9},{6,10},{7,11},{8,4},{9,5},... | collective-permute-start | bytes 884744 | tf_op jit(solution)/shard_map/ppermute | solution.py:396
  78.1 8.0 %collective-permute-start.7 = (f32[576,128]{1,0:T(8,128)S(1)}, f32[576,128]{1,0:T(8,128)S(1)}, u32[]{:S(2)}, u32[]{:S(2)}) collective-permute-start(f32[576,128]{1,0:T(8,128)S(1)} %get-tuple-element.93), channel_id=1, source_target_pairs={{0,4},{1,5},{2,6},{3,7},{4,0},{5,1},{6,2},{7,3},{8,12},{9,13},{10,... | collective-permute-start | bytes 884744 | tf_op jit(solution)/shard_map/ppermute | solution.py:396
  78.2 7.9 %collective-permute-start.9 = (f32[64,1024]{1,0:T(8,128)S(1)}, f32[64,1024]{1,0:T(8,128)S(1)}, u32[]{:S(2)}, u32[]{:S(2)}) collective-permute-start(f32[64,1024]{1,0:T(8,128)S(1)} %slice.9), channel_id=1, source_target_pairs={{0,96},{1,97},{2,98},{3,99},{4,100},{5,101},{6,102},{7,103},{8,104... | collective-permute-start | bytes 786440 | tf_op jit(solution)/shard_map/ppermute | solution.py:396
  80.1 6.0 %collective-permute-start.8 = (f32[64,128]{1,0:T(8,128)S(1)}, f32[64,128]{1,0:T(8,128)S(1)}, u32[]{:S(2)}, u32[]{:S(2)}) collective-permute-start(f32[64,128]{1,0:T(8,128)S(1)} %slice_add_fusion.moment), channel_id=1, source_target_pairs={{0,8},{1,9},{2,10},{3,11},{4,12},{5,13},{6,14},{7,15},{8,0},{9,1},... | collective-permute-start | bytes 98312 | tf_op jit(solution)/shard_map/ppermute | solution.py:396
  86.2 4.3 %collective-permute-start.10 = (f32[64,1024]{1,0:T(8,128)S(1)}, f32[64,1024]{1,0:T(8,128)S(1)}, u32[]{:S(2)}, u32[]{:S(2)}) collective-permute-start(f32[64,1024]{1,0:T(8,128)S(1)} %add.19.mine), channel_id=1, source_target_pairs={{0,16},{16,0},{32,48},{48,32},{64,80},{80,64},{96,112},{112,96},{1... | collective-permute-start | bytes 786440 | tf_op jit(solution)/shard_map/ppermute | solution.py:388
  86.3 6.9 %collective-permute-start.11 = (f32[320,128]{1,0:T(8,128)S(1)}, f32[320,128]{1,0:T(8,128)S(1)}, u32[]{:S(2)}, u32[]{:S(2)}) collective-permute-start(f32[320,128]{1,0:T(8,128)S(1)} %get-tuple-element.99), channel_id=1, source_target_pairs={{0,2},{1,3},{2,0},{3,1},{4,6},{5,7},{6,4},{7,5},{8,10},{9,11},{10,... | collective-permute-start | bytes 491528 | tf_op jit(solution)/shard_map/ppermute | solution.py:396
  87.6 5.7 %collective-permute-start.12 = (f32[320,128]{1,0:T(8,128)S(1)}, f32[320,128]{1,0:T(8,128)S(1)}, u32[]{:S(2)}, u32[]{:S(2)}) collective-permute-start(f32[320,128]{1,0:T(8,128)S(1)} %get-tuple-element.100), channel_id=1, source_target_pairs={{0,1},{1,0},{2,3},{3,2},{4,5},{5,4},{6,7},{7,6},{8,9},{9,8},{10,11... | collective-permute-start | bytes 491528 | tf_op jit(solution)/shard_map/ppermute | solution.py:396
  88.3 6.6 %collective-permute-start.13 = (f32[320,128]{1,0:T(8,128)S(1)}, f32[320,128]{1,0:T(8,128)S(1)}, u32[]{:S(2)}, u32[]{:S(2)}) collective-permute-start(f32[320,128]{1,0:T(8,128)S(1)} %get-tuple-element.101), channel_id=1, source_target_pairs={{0,3},{1,2},{2,1},{3,0},{4,7},{5,6},{6,5},{7,4},{8,11},{9,10},{10,... | collective-permute-start | bytes 491528 | tf_op jit(solution)/shard_map/ppermute | solution.py:396
  94.9 1.3 %collective-permute-start.14 = (f32[64,128]{1,0:T(8,128)S(1)}, f32[64,128]{1,0:T(8,128)S(1)}, u32[]{:S(2)}, u32[]{:S(2)}) collective-permute-start(f32[64,128]{1,0:T(8,128)S(1)} %shard_map.95.mine), channel_id=1, source_target_pairs={{0,16},{16,0},{32,48},{48,32},{64,80},{80,64},{96,112},{112,96},{1... | collective-permute-start | bytes 98312 | tf_op jit(solution)/shard_map/ppermute | solution.py:388
